TPU v7x, 32 devices: a whole 2x2x4 slice. The times are simulated.
32 devices in a mesh: grp: 4 (over z), shard: 2 (over x), tp: 4 (over y, core).
Axes of the slice: x: 2, y: 2, z: 4, core: 2. Of those that a mesh axis runs over, the one named last changes fastest.
Arguments:
- inner_weights: float32 [4, 2, 4096, 7168], P('grp', None, 'shard', 'tp'), may hold values from -6 to 6
- start_weights: float32 [2, 4096, 7168], P(None, 'shard', 'tp'), may hold values from -6 to 6
- momentum: float32 [2, 2, 4, 32, 64, 1792], P(None, None, None, ('grp', 'shard', 'tp')), may hold values from -6 to 6
Outputs:
- new_weights: float32 [2, 4096, 7168], P(None, 'shard', 'tp')
- new_momentum: float32 [2, 2, 4, 32, 64, 1792], P(None, None, None, ('grp', 'shard', 'tp'))
All inputs are finite; a program needn't handle non-finite values.
Results may differ from a plain program's by a relative error of at most 0.00002.
Values sent between devices are 32-bit elements; how exact they have to be, the bound alone decides.
No kernel may reach another device: no remote copies, remote signals or barrier semaphores. Data moves between devices by JAX's collectives and lax.ppermute only.
A program may use at most 192 MiB of HBM per device.

v0:
```python
import jax
import jax.numpy as jnp
from jax import lax
from jax.sharding import PartitionSpec as P

OUTER_RATE = 0.7
MOMENTUM_COEF = 0.5


def body(inner_weights, start_weights, momentum):
    groups = lax.axis_size("grp")
    shards = lax.axis_size("shard")
    tp_size = lax.axis_size("tp")
    devices = groups * shards * tp_size
    row_count = start_weights.shape[1]
    col_count = start_weights.shape[2]
    q_rows = row_count // devices
    differ = start_weights - inner_weights[0]
    pieces = differ.reshape(2, devices, q_rows, col_count)
    landed = lax.all_to_all(pieces, ("grp", "shard", "tp"), split_axis=1, concat_axis=1, tiled=True)
    summed = jnp.sum(landed.reshape(2, groups, shards * tp_size, q_rows, col_count), axis=1)
    flat_diff = summed.reshape(2, shards, tp_size, 1, q_rows, col_count) / groups
    new_momentum = MOMENTUM_COEF * momentum + flat_diff
    flat_step = OUTER_RATE * (flat_diff + MOMENTUM_COEF * new_momentum)
    outgoing = flat_step.reshape(2, shards * tp_size, q_rows, col_count)
    own_part = lax.all_to_all(outgoing, ("shard", "tp"), split_axis=1, concat_axis=1, tiled=True)
    gathered = lax.all_gather(own_part, "grp", axis=1, tiled=True)
    new_weights = start_weights - gathered.reshape(2, row_count, col_count)
    return (new_weights, new_momentum)


def solution(mesh):
    in_specs = (
        P("grp", None, "shard", "tp"),
        P(None, "shard", "tp"),
        P(None, None, None, ("grp", "shard", "tp"), None, None),
    )
    out_specs = (P(None, "shard", "tp"), P(None, None, None, ("grp", "shard", "tp"), None, None))
    return jax.shard_map(body, mesh=mesh, in_specs=in_specs, out_specs=out_specs, check_vma=False)
```

profile of v0, /device:TPU:0, one launch (start us, length us, event | category | flops | bytes accessed | tf_op | source)
XLA Modules:
  0.0 1332.2 jit_solution(9270215449554085753)
XLA Ops:
  7.2 0.0 all-gather.2.cloned.1.call-start
  7.2 29.8 %bitcast_subtract_fusion.1 = f32[2,2048,1792]{2,1,0:T(8,128)} fusion(f32[2,2048,1792]{2,1,0:T(8,128)} %param.4, f32[1,2,2048,1792]{3,2,1,0:T(8,128)} %param.3), kind=kLoop, calls=%fused_computation.1 | loop fusion | flops 7340032 | bytes 88080384 | tf_op jit(solution)/shard_map/sub | solution.py:18
  37.0 11.4 copy.9
  48.4 640.2 %all_to_all.10 = f32[2,32,64,1792]{3,2,0,1:T(8,128)} all-to-all(f32[2,32,64,1792]{3,2,0,1:T(8,128)S(1)} %copy.9), channel_id=1, replica_groups=mesh['grp'=4,'shard'=2,'tp'=4] {'grp','shard','tp'}, dimensions={1} | all-to-all | bytes 58720256 | tf_op jit(solution)/shard_map/all_to_all | solution.py:20
  688.6 14.5 %reduce_sum.9 = f32[2,8,64,1792]{3,2,0,1:T(8,128)} reduce(f32[2,4,8,64,1792]{4,3,0,2,1:T(8,128)} %bitcast.8, f32[]{:T(128)} %constant.1.clone.1), dimensions={1}, to_apply=%region_0.0 | reduce | flops 5505024 | bytes 36700164 | tf_op jit(solution)/shard_map/reduce_sum | solution.py:21
  703.1 3.7 broadcast_multiply_fusion
  706.8 5.9 add_multiply_fusion
  712.7 0.7 copy.12
  713.4 86.5 %all_to_all.11 = f32[2,8,64,1792]{3,2,0,1:T(8,128)S(1)} all-to-all(f32[2,8,64,1792]{3,2,0,1:T(8,128)S(1)} %bitcast.11), channel_id=1, replica_groups=mesh['grp'=4,'shard'=2,'tp'=4] {'shard','tp'}, dimensions={1} | all-to-all | bytes 14680064 | tf_op jit(solution)/shard_map/all_to_all | solution.py:26
  800.0 3.8 copy.13
  803.7 0.0 all-gather.2.cloned.1.call-update
  803.8 491.8 %all-gather.2.cloned.1.call-done = f32[2,32,64,1792]{3,2,1,0:T(8,128)} async-done(((f32[2,8,64,1792]{3,2,1,0:T(8,128)}), f32[2,32,64,1792]{3,2,1,0:T(8,128)}) %all-gather.2.cloned.1.call-update) | async-done | bytes 29360144 | tf_op jit(solution)/shard_map/all_gather | solution.py:27
  1295.6 29.8 %bitcast_subtract_fusion = f32[2,2048,1792]{2,1,0:T(8,128)} fusion(f32[2,2048,1792]{2,1,0:T(8,128)} %param.4, f32[2,32,64,1792]{3,2,1,0:T(8,128)} %all-gather.2.cloned.1.call-done), kind=kLoop, calls=%fused_computation | loop fusion | flops 7340032 | bytes 88080384 | tf_op jit(solution)/shard_map/sub | solution.py:28
Async XLA Ops:
  7.2 1288.4 %all-gather.2.cloned.1.call-start = ((), (), s32[]{:S(2)}) async-start(), calls=%async_computation.2 | async-start | bytes 36700160 | tf_op jit(solution)/shard_map/all_gather | solution.py:27
Sparse Core Ops, SparseCore 0:
  803.9 491.6 all-gather.1
where the time goes:
time: 1330 us
  blocking collectives  727 us (55%)
  waiting for transfers between devices  492 us (37%)
  other arithmetic  83.7 us (6%)
  local copies, waits for them, and re-layouts  15.9 us (1%)
  between operations  14.1 us (1%)
    all_to_all x1, blocking collectives, body(): lax.all_to_all(pieces, ('grp', 'shard', 'tp'), split_axis=1, concat_axis=...  640 us
    all_gather x1, waiting for transfers between devices, body(): gathered = lax.all_gather(own_part, 'grp', axis=1, tiled=True)  492 us
    all_to_all x1, blocking collectives, body(): lax.all_to_all(outgoing, ('shard', 'tp'), split_axis=1, concat_axis=1, ti...  86.5 us
    sub x1, other arithmetic, body(): differ = start_weights - inner_weights[0]  29.8 us
    sub x1, other arithmetic, body(): new_weights = start_weights - gathered.reshape(2, row_count, col_count)  29.8 us
  transfers between devices with their start and end apart: 1, of which 1 were waited for; matrix products, arithmetic and copies ran while one was open for 0% of the time, Pallas kernels for 0%

commit v1 on v0

v1 whole, which is shorter than its diff:
```python
import jax
import jax.numpy as jnp
from jax import lax
from jax.experimental import pallas as pl
from jax.sharding import PartitionSpec as P

OUTER_RATE = 0.7
MOMENTUM_COEF = 0.5
STEPS = 8


def blank(shape):
    return pl.pallas_call(
        lambda out: None,
        out_shape=jax.ShapeDtypeStruct(shape, jnp.float32),
        out_specs=pl.BlockSpec(memory_space=pl.ANY),
    )()


def body(inner_weights, start_weights, momentum):
    groups = lax.axis_size("grp")
    shards = lax.axis_size("shard")
    tp_size = lax.axis_size("tp")
    plane = shards * tp_size
    group = lax.axis_index("grp")
    place = lax.axis_index(("shard", "tp"))
    row_count, col_count = start_weights.shape[1:]
    q_rows = row_count // (groups * plane)
    steps = min(STEPS, plane)
    merge = plane // steps
    block = (q_rows, col_count)

    inner = inner_weights.reshape((2, groups, plane) + block)
    start = start_weights.reshape((2, groups, plane) + block)
    held = momentum.reshape((2, plane) + block)
    rightward = [(i, i + 1) for i in range(groups - 1)]
    leftward = [(i + 1, i) for i in range(groups - 1)]

    def lane(shift):
        return lax.rem(place + shift, plane)

    def cut(array, *at):
        return lax.dynamic_slice(array, at + (0, 0), (1,) * len(at) + block).reshape(block)

    def join(parts):
        return parts[0] if merge == 1 else jnp.concatenate(parts, axis=0)

    def parts_of(chunk):
        return [chunk[m * q_rows : (m + 1) * q_rows] for m in range(merge)]

    def rows_of(array, matrix, owner, step):
        return join([cut(array, matrix, owner, lane(step * merge + m)) for m in range(merge)])

    def own(matrix, owner, step):
        return rows_of(start, matrix, owner, step) - rows_of(inner, matrix, owner, step)

    def momentum_of(matrix, step):
        parts = []
        for m in range(merge):
            shift = step * merge + m
            part = cut(held, matrix, lane(plane - shift))
            if shift:
                part = lax.ppermute(part, ("shard", "tp"), [(i, (i - shift) % plane) for i in range(plane)])
            parts.append(part)
        return join(parts)

    new_weights = blank(start.shape)
    new_held = blank(held.shape)

    def write_weights(array, matrix, owner, step, update):
        for m, part in enumerate(parts_of(update)):
            at = (matrix, owner, lane(step * merge + m))
            array = lax.dynamic_update_slice(array, (cut(start, *at) - part)[None, None, None], at + (0, 0))
        return array

    def write_momentum(array, matrix, step, value):
        for m, part in enumerate(parts_of(value)):
            shift = step * merge + m
            if shift:
                part = lax.ppermute(part, ("shard", "tp"), [(i, (i + shift) % plane) for i in range(plane)])
            array = lax.dynamic_update_slice(array, part[None, None], (matrix, lane(plane - shift), 0, 0))
        return array

    moved = [[momentum_of(matrix, step) for step in range(steps)] for matrix in range(2)]
    zero = jnp.zeros((merge * q_rows, col_count), jnp.float32)
    from_left, from_right = [zero, zero], [zero, zero]
    arrived_left, arrived_right = [[], []], [[], []]

    for turn in range(steps + 1):
        for phase in range(1, groups + 1):
            for matrix in range(2):
                if turn == steps and phase == groups:
                    continue
                if phase < groups:
                    to_right, to_left = from_left[matrix], from_right[matrix]
                    if turn < steps:
                        right_owner = jnp.minimum(groups - phase + group, groups - 1)
                        left_owner = jnp.maximum(group - (groups - phase), 0)
                        to_right = jnp.where(group < phase, to_right + own(matrix, right_owner, turn), to_right)
                        to_left = jnp.where(
                            groups - 1 - group < phase, to_left + own(matrix, left_owner, turn), to_left
                        )
                else:
                    total = own(matrix, group, turn) + from_left[matrix] + from_right[matrix]
                    mean_diff = total / groups
                    new_momentum = MOMENTUM_COEF * moved[matrix][turn] + mean_diff
                    update = OUTER_RATE * (mean_diff + MOMENTUM_COEF * new_momentum)
                    new_held = write_momentum(new_held, matrix, turn, new_momentum)
                    new_weights = write_weights(new_weights, matrix, group, turn, update)
                    to_right = to_left = update
                if turn == steps and phase == groups - 1:
                    continue
                other = 1 - matrix
                to_right, to_left, from_left[other], from_right[other] = lax.optimization_barrier(
                    (to_right, to_left, from_left[other], from_right[other])
                )
                from_left[matrix] = lax.ppermute(to_right, "grp", rightward)
                from_right[matrix] = lax.ppermute(to_left, "grp", leftward)
                if phase == groups:
                    arrived_left[matrix], arrived_right[matrix] = [], []
                if phase == groups or turn > 0:
                    arrived_left[matrix].append(from_left[matrix])
                    arrived_right[matrix].append(from_right[matrix])
                    if len(arrived_left[matrix]) == groups - 1:
                        step = turn - 1
                        for hop in range(groups - 1):
                            update = jnp.where(
                                group > hop,
                                arrived_left[matrix][hop],
                                arrived_right[matrix][groups - 2 - hop],
                            )
                            owner = lax.rem(group + groups - 1 - hop, groups)
                            new_weights = write_weights(new_weights, matrix, owner, step, update)
    return (new_weights.reshape(start_weights.shape), new_held.reshape(momentum.shape))


def solution(mesh):
    in_specs = (
        P("grp", None, "shard", "tp"),
        P(None, "shard", "tp"),
        P(None, None, None, ("grp", "shard", "tp"), None, None),
    )
    out_specs = (P(None, "shard", "tp"), P(None, None, None, ("grp", "shard", "tp"), None, None))
    return jax.shard_map(body, mesh=mesh, in_specs=in_specs, out_specs=out_specs, check_vma=False)
```

time: 1330 us -> 1090 us (0.82)
  blocking collectives: 727 us -> 0 us
  starting transfers between devices: 0.04 us -> 393 us
  other arithmetic: 83.7 us -> 151 us
  waiting for transfers between devices: 492 us -> 523 us
    all_to_all x2 -> x0, blocking collectives: 727 us -> none  [the longest x1 640 us: body(): lax.all_to_all(pieces, ('grp', 'shard', 'tp'), split_axis=1, concat_axis=...]
    ppermute x0 -> x164, waiting for transfers between devices: none -> 523 us  [the longest x68 286 us: body(): from_right[matrix] = lax.ppermute(to_left, 'grp', leftward)]
    all_gather x1 -> x0, waiting for transfers between devices: 492 us -> none  [body(): gathered = lax.all_gather(own_part, 'grp', axis=1, tiled=True)]
    ppermute x0 -> x164, starting transfers between devices: none -> 393 us  [the longest x68 264 us: body(): from_left[matrix] = lax.ppermute(to_right, 'grp', rightward)]
    select_n x0 -> x48, other arithmetic: none -> 67.7 us  [body(): jnp.where(groups - 1 - group < phase, to_left + own(matrix, left_owner, t...]
    dynamic_update_slice x0 -> x66, other arithmetic: none -> 67.2 us  [the longest x64 59.6 us: write_weights(): lax.dynamic_update_slice(array, (cut(start, *at) - part)[None, None, None...]
    sub x2 -> x0, other arithmetic: 59.6 us -> none  [the longest x1 29.8 us: body(): differ = start_weights - inner_weights[0]]
    add x0 -> x14, other arithmetic: none -> 16.4 us  [body(): new_momentum = MOMENTUM_COEF * moved[matrix][turn] + mean_diff]
  transfers between devices with their start and end apart: 1 -> 164, of which waited for: 1 -> 130; matrix products, arithmetic and copies ran while one was open for 0% -> 15% of each run, Pallas kernels for 0% -> 0%
where the time goes in v1:
time: 1090 us; the launch traced here: 1080 us
  waiting for transfers between devices  523 us (48%)
  starting transfers between devices  393 us (36%)
  other arithmetic  151 us (14%)
  local copies, waits for them, and re-layouts  11.3 us (1%)
    ppermute x68, waiting for transfers between devices, body(): from_right[matrix] = lax.ppermute(to_left, 'grp', leftward)  286 us
    ppermute x68, starting transfers between devices, body(): from_left[matrix] = lax.ppermute(to_right, 'grp', rightward)  264 us
    ppermute x68, waiting for transfers between devices, body(): from_left[matrix] = lax.ppermute(to_right, 'grp', rightward)  214 us
    ppermute x68, starting transfers between devices, body(): from_right[matrix] = lax.ppermute(to_left, 'grp', leftward)  87.9 us
    select_n x48, other arithmetic, body(): jnp.where(groups - 1 - group < phase, to_left + own(matrix, left_owner, t...  67.7 us
    dynamic_update_slice x64, other arithmetic, write_weights(): lax.dynamic_update_slice(array, (cut(start, *at) - part)[None, None, None...  59.6 us
    ppermute x14, starting transfers between devices, momentum_of(): lax.ppermute(part, ('shard', 'tp'), [(i, (i - shift) % plane) for i in ra...  23.4 us
    ppermute x14, waiting for transfers between devices, write_momentum(): lax.ppermute(part, ('shard', 'tp'), [(i, (i + shift) % plane) for i in ra...  22.9 us
  transfers between devices with their start and end apart: 164, of which 130 were waited for; matrix products, arithmetic and copies ran while one was open for 15% of the time, Pallas kernels for 0%

profile of v1, /device:TPU:0, one launch (start us, length us, event | category | flops | bytes accessed | tf_op | source)
XLA Modules:
  0.0 1081.1 jit_solution(17093674460810461036)
XLA Ops:
  10.2 6.7 collective-permute-done
  27.4 5.7 collective-permute-done.2
  112.3 6.6 collective-permute-done.14
  128.2 5.7 collective-permute-done.16
  221.9 7.7 collective-permute-done.31
  237.1 7.1 collective-permute-done.32
  244.2 6.0 collective-permute-done.33
  254.5 7.4 collective-permute-done.34
  270.9 6.5 collective-permute-done.36
  342.1 11.6 %collective-permute-done.152 = f32[64,1792]{1,0:T(8,128)S(1)} collective-permute-done((f32[64,1792]{1,0:T(8,128)S(1)}, f32[64,1792]{1,0:T(8,128)S(1)}, u32[]{:S(2)}, u32[]{:S(2)}) %collective-permute-start.152) | collective-permute-done | bytes 458784 | tf_op jit(solution)/shard_map/ppermute | solution.py:80
  355.8 13.6 %collective-permute-done.49 = f32[64,1792]{1,0:T(8,128)S(1)} collective-permute-done((f32[64,1792]{1,0:T(8,128)S(1)}, f32[64,1792]{1,0:T(8,128)S(1)}, u32[]{:S(2)}, u32[]{:S(2)}) %collective-permute-start.49) | collective-permute-done | bytes 458784 | tf_op jit(solution)/shard_map/ppermute | solution.py:118
  376.4 5.9 collective-permute-done.50
  392.7 5.8 collective-permute-done.52
  501.6 5.8 collective-permute-done.69
  594.0 9.3 collective-permute-start.116
  603.3 6.3 collective-permute-start.156
  620.2 8.2 collective-permute-done.85
  637.9 5.8 collective-permute-done.87
  665.0 7.2 collective-permute-done.91
  679.4 7.0 collective-permute-done.92
  689.5 14.2 %collective-permute-start.95 = (f32[64,1792]{1,0:T(8,128)S(1)}, f32[64,1792]{1,0:T(8,128)S(1)}, u32[]{:S(2)}, u32[]{:S(2)}) collective-permute-start(f32[64,1792]{1,0:T(8,128)S(1)} %get-tuple-element.445), channel_id=1, source_target_pairs={{0,8},{8,16},{16,24},{1,9},{9,17},{17,25},{2,10},{10,18},{18,26},{... | collective-permute-start | bytes 1376264 | tf_op jit(solution)/shard_map/ppermute | solution.py:117
  717.4 9.8 collective-permute-start.119
  758.3 8.0 collective-permute-done.103
  766.2 5.8 collective-permute-start.104
  775.5 7.0 collective-permute-done.104
  792.8 6.2 collective-permute-done.106
  895.2 5.5 collective-permute-done.122
  984.9 5.6 collective-permute-done.136
  999.0 6.0 collective-permute-done.138
  1005.0 6.0 collective-permute-done.139
  1046.0 6.4 collective-permute-done.145
  1059.1 6.7 collective-permute-done.146
  (460 shorter events, 845.5 us)
Async XLA Ops:
  99.4 97.5 %collective-permute-start.26 = (f32[64,1792]{1,0:T(8,128)}, f32[64,1792]{1,0:T(8,128)S(1)}, u32[]{:S(2)}, u32[]{:S(2)}) collective-permute-start(f32[64,1792]{1,0:T(8,128)} %get-tuple-element.717), channel_id=1, source_target_pairs={{0,7},{1,0},{2,1},{3,2},{4,3},{5,4},{6,5},{7,6},{8,15},{9,8},{10,9... | collective-permute-start | bytes 1376264 | tf_op jit(solution)/shard_map/ppermute | solution.py:63
  99.4 107.9 %collective-permute-start.29 = (f32[64,1792]{1,0:T(8,128)}, f32[64,1792]{1,0:T(8,128)S(1)}, u32[]{:S(2)}, u32[]{:S(2)}) collective-permute-start(f32[64,1792]{1,0:T(8,128)} %get-tuple-element.716), channel_id=1, source_target_pairs={{0,7},{1,0},{2,1},{3,2},{4,3},{5,4},{6,5},{7,6},{8,15},{9,8},{10,9... | collective-permute-start | bytes 1376264 | tf_op jit(solution)/shard_map/ppermute | solution.py:63
  101.9 224.7 %collective-permute-start.44 = (f32[64,1792]{1,0:T(8,128)S(1)}, f32[64,1792]{1,0:T(8,128)S(1)}, u32[]{:S(2)}, u32[]{:S(2)}) collective-permute-start(f32[64,1792]{1,0:T(8,128)S(1)} %get-tuple-element.715), channel_id=1, source_target_pairs={{0,6},{1,7},{2,0},{3,1},{4,2},{5,3},{6,4},{7,5},{8,14},{9,15},{10,... | collective-permute-start | bytes 1376264 | tf_op jit(solution)/shard_map/ppermute | solution.py:63
  188.2 149.1 %collective-permute-start.47 = (f32[64,1792]{1,0:T(8,128)S(1)}, f32[64,1792]{1,0:T(8,128)S(1)}, u32[]{:S(2)}, u32[]{:S(2)}) collective-permute-start(f32[64,1792]{1,0:T(8,128)S(1)} %get-tuple-element.714), channel_id=1, source_target_pairs={{0,6},{1,7},{2,0},{3,1},{4,2},{5,3},{6,4},{7,5},{8,14},{9,15},{10,... | collective-permute-start | bytes 1376264 | tf_op jit(solution)/shard_map/ppermute | solution.py:63
  202.9 259.3 %collective-permute-start.62 = (f32[64,1792]{1,0:T(8,128)S(1)}, f32[64,1792]{1,0:T(8,128)S(1)}, u32[]{:S(2)}, u32[]{:S(2)}) collective-permute-start(f32[64,1792]{1,0:T(8,128)S(1)} %get-tuple-element.713), channel_id=1, source_target_pairs={{0,5},{1,6},{2,7},{3,0},{4,1},{5,2},{6,3},{7,4},{8,13},{9,14},{10,... | collective-permute-start | bytes 1376264 | tf_op jit(solution)/shard_map/ppermute | solution.py:63
  234.9 15.2 %collective-permute-start.33 = (f32[64,1792]{1,0:T(8,128)S(1)}, f32[64,1792]{1,0:T(8,128)S(1)}, u32[]{:S(2)}, u32[]{:S(2)}) collective-permute-start(f32[64,1792]{1,0:T(8,128)S(1)} %get-tuple-element.335), channel_id=1, source_target_pairs={{8,0},{16,8},{24,16},{9,1},{17,9},{25,17},{10,2},{18,10},{26,18},{... | collective-permute-start | bytes 1376264 | tf_op jit(solution)/shard_map/ppermute | solution.py:118
  318.6 153.9 %collective-permute-start.65 = (f32[64,1792]{1,0:T(8,128)S(1)}, f32[64,1792]{1,0:T(8,128)S(1)}, u32[]{:S(2)}, u32[]{:S(2)}) collective-permute-start(f32[64,1792]{1,0:T(8,128)S(1)} %get-tuple-element.712), channel_id=1, source_target_pairs={{0,5},{1,6},{2,7},{3,0},{4,1},{5,2},{6,3},{7,4},{8,13},{9,14},{10,... | collective-permute-start | bytes 1376264 | tf_op jit(solution)/shard_map/ppermute | solution.py:63
  332.6 255.5 %collective-permute-start.80 = (f32[64,1792]{1,0:T(8,128)S(1)}, f32[64,1792]{1,0:T(8,128)S(1)}, u32[]{:S(2)}, u32[]{:S(2)}) collective-permute-start(f32[64,1792]{1,0:T(8,128)S(1)} %get-tuple-element.711), channel_id=1, source_target_pairs={{0,4},{1,5},{2,6},{3,7},{4,0},{5,1},{6,2},{7,3},{8,12},{9,13},{10,... | collective-permute-start | bytes 1376264 | tf_op jit(solution)/shard_map/ppermute | solution.py:63
  337.3 16.4 %collective-permute-start.152 = (f32[64,1792]{1,0:T(8,128)S(1)}, f32[64,1792]{1,0:T(8,128)S(1)}, u32[]{:S(2)}, u32[]{:S(2)}) collective-permute-start(f32[64,1792]{1,0:T(8,128)S(1)} %get-tuple-element.566), channel_id=1, source_target_pairs={{0,2},{1,3},{2,4},{3,5},{4,6},{5,7},{6,0},{7,1},{8,10},{9,11},{10,... | collective-permute-start | bytes 1376264 | tf_op jit(solution)/shard_map/ppermute | solution.py:80
  337.3 18.4 %collective-permute-start.48 = (f32[64,1792]{1,0:T(8,128)S(1)}, f32[64,1792]{1,0:T(8,128)S(1)}, u32[]{:S(2)}, u32[]{:S(2)}) collective-permute-start(f32[64,1792]{1,0:T(8,128)S(1)} %get-tuple-element.363), channel_id=1, source_target_pairs={{0,8},{8,16},{16,24},{1,9},{9,17},{17,25},{2,10},{10,18},{18,26},{... | collective-permute-start | bytes 1376264 | tf_op jit(solution)/shard_map/ppermute | solution.py:117
  353.7 15.7 %collective-permute-start.49 = (f32[64,1792]{1,0:T(8,128)S(1)}, f32[64,1792]{1,0:T(8,128)S(1)}, u32[]{:S(2)}, u32[]{:S(2)}) collective-permute-start(f32[64,1792]{1,0:T(8,128)S(1)} %get-tuple-element.363), channel_id=1, source_target_pairs={{8,0},{16,8},{24,16},{9,1},{17,9},{25,17},{10,2},{18,10},{26,18},{... | collective-permute-start | bytes 1376264 | tf_op jit(solution)/shard_map/ppermute | solution.py:118
  355.8 18.6 %collective-permute-start.153 = (f32[64,1792]{1,0:T(8,128)S(1)}, f32[64,1792]{1,0:T(8,128)S(1)}, u32[]{:S(2)}, u32[]{:S(2)}) collective-permute-start(f32[64,1792]{1,0:T(8,128)S(1)} %get-tuple-element.564), channel_id=1, source_target_pairs={{0,2},{1,3},{2,4},{3,5},{4,6},{5,7},{6,0},{7,1},{8,10},{9,11},{10,... | collective-permute-start | bytes 1376264 | tf_op jit(solution)/shard_map/ppermute | solution.py:80
  452.1 157.5 %collective-permute-start.83 = (f32[64,1792]{1,0:T(8,128)S(1)}, f32[64,1792]{1,0:T(8,128)S(1)}, u32[]{:S(2)}, u32[]{:S(2)}) collective-permute-start(f32[64,1792]{1,0:T(8,128)S(1)} %get-tuple-element.710), channel_id=1, source_target_pairs={{0,4},{1,5},{2,6},{3,7},{4,0},{5,1},{6,2},{7,3},{8,12},{9,13},{10,... | collective-permute-start | bytes 1376264 | tf_op jit(solution)/shard_map/ppermute | solution.py:63
  468.1 263.6 %collective-permute-start.98 = (f32[64,1792]{1,0:T(8,128)S(1)}, f32[64,1792]{1,0:T(8,128)S(1)}, u32[]{:S(2)}, u32[]{:S(2)}) collective-permute-start(f32[64,1792]{1,0:T(8,128)S(1)} %get-tuple-element.709), channel_id=1, source_target_pairs={{0,3},{1,4},{2,5},{3,6},{4,7},{5,0},{6,1},{7,2},{8,11},{9,12},{10,... | collective-permute-start | bytes 1376264 | tf_op jit(solution)/shard_map/ppermute | solution.py:63
  568.9 14.9 %collective-permute-start.79 = (f32[64,1792]{1,0:T(8,128)S(1)}, f32[64,1792]{1,0:T(8,128)S(1)}, u32[]{:S(2)}, u32[]{:S(2)}) collective-permute-start(f32[64,1792]{1,0:T(8,128)S(1)} %get-tuple-element.419), channel_id=1, source_target_pairs={{8,0},{16,8},{24,16},{9,1},{17,9},{25,17},{10,2},{18,10},{26,18},{... | collective-permute-start | bytes 1376264 | tf_op jit(solution)/shard_map/ppermute | solution.py:118
  578.8 164.4 %collective-permute-start.101 = (f32[64,1792]{1,0:T(8,128)S(1)}, f32[64,1792]{1,0:T(8,128)S(1)}, u32[]{:S(2)}, u32[]{:S(2)}) collective-permute-start(f32[64,1792]{1,0:T(8,128)S(1)} %get-tuple-element.708), channel_id=1, source_target_pairs={{0,3},{1,4},{2,5},{3,6},{4,7},{5,0},{6,1},{7,2},{8,11},{9,12},{10,... | collective-permute-start | bytes 1376264 | tf_op jit(solution)/shard_map/ppermute | solution.py:63
  588.1 15.2 %collective-permute-start.82 = (f32[64,1792]{1,0:T(8,128)S(1)}, f32[64,1792]{1,0:T(8,128)S(1)}, u32[]{:S(2)}, u32[]{:S(2)}) collective-permute-start(f32[64,1792]{1,0:T(8,128)S(1)} %get-tuple-element.423), channel_id=1, source_target_pairs={{8,0},{16,8},{24,16},{9,1},{17,9},{25,17},{10,2},{18,10},{26,18},{... | collective-permute-start | bytes 1376264 | tf_op jit(solution)/shard_map/ppermute | solution.py:118
  594.0 268.0 %collective-permute-start.116 = (f32[64,1792]{1,0:T(8,128)S(1)}, f32[64,1792]{1,0:T(8,128)S(1)}, u32[]{:S(2)}, u32[]{:S(2)}) collective-permute-start(f32[64,1792]{1,0:T(8,128)S(1)} %get-tuple-element.707), channel_id=1, source_target_pairs={{0,2},{1,3},{2,4},{3,5},{4,6},{5,7},{6,0},{7,1},{8,10},{9,11},{10,... | collective-permute-start | bytes 1376264 | tf_op jit(solution)/shard_map/ppermute | solution.py:63
  688.2 19.4 %collective-permute-start.94 = (f32[64,1792]{1,0:T(8,128)S(1)}, f32[64,1792]{1,0:T(8,128)S(1)}, u32[]{:S(2)}, u32[]{:S(2)}) collective-permute-start(f32[64,1792]{1,0:T(8,128)S(1)} %get-tuple-element.444), channel_id=1, source_target_pairs={{8,0},{16,8},{24,16},{9,1},{17,9},{25,17},{10,2},{18,10},{26,18},{... | collective-permute-start | bytes 1376264 | tf_op jit(solution)/shard_map/ppermute | solution.py:118
  689.5 18.1 %collective-permute-start.95 = (f32[64,1792]{1,0:T(8,128)S(1)}, f32[64,1792]{1,0:T(8,128)S(1)}, u32[]{:S(2)}, u32[]{:S(2)}) collective-permute-start(f32[64,1792]{1,0:T(8,128)S(1)} %get-tuple-element.445), channel_id=1, source_target_pairs={{0,8},{8,16},{16,24},{1,9},{9,17},{17,25},{2,10},{10,18},{18,26},{... | collective-permute-start | bytes 1376264 | tf_op jit(solution)/shard_map/ppermute | solution.py:117
  711.5 15.8 %collective-permute-start.97 = (f32[64,1792]{1,0:T(8,128)S(1)}, f32[64,1792]{1,0:T(8,128)S(1)}, u32[]{:S(2)}, u32[]{:S(2)}) collective-permute-start(f32[64,1792]{1,0:T(8,128)S(1)} %get-tuple-element.451), channel_id=1, source_target_pairs={{8,0},{16,8},{24,16},{9,1},{17,9},{25,17},{10,2},{18,10},{26,18},{... | collective-permute-start | bytes 1376264 | tf_op jit(solution)/shard_map/ppermute | solution.py:118
  717.4 159.4 %collective-permute-start.119 = (f32[64,1792]{1,0:T(8,128)S(1)}, f32[64,1792]{1,0:T(8,128)S(1)}, u32[]{:S(2)}, u32[]{:S(2)}) collective-permute-start(f32[64,1792]{1,0:T(8,128)S(1)} %get-tuple-element.706), channel_id=1, source_target_pairs={{0,2},{1,3},{2,4},{3,5},{4,6},{5,7},{6,0},{7,1},{8,10},{9,11},{10,... | collective-permute-start | bytes 1376264 | tf_op jit(solution)/shard_map/ppermute | solution.py:63
  737.6 240.9 %collective-permute-start.134 = (f32[64,1792]{1,0:T(8,128)S(1)}, f32[64,1792]{1,0:T(8,128)S(1)}, u32[]{:S(2)}, u32[]{:S(2)}) collective-permute-start(f32[64,1792]{1,0:T(8,128)S(1)} %get-tuple-element.705), channel_id=1, source_target_pairs={{0,1},{1,2},{2,3},{3,4},{4,5},{5,6},{6,7},{7,0},{8,9},{9,10},{10,1... | collective-permute-start | bytes 1376264 | tf_op jit(solution)/shard_map/ppermute | solution.py:63
  751.4 14.9 %collective-permute-start.103 = (f32[64,1792]{1,0:T(8,128)S(1)}, f32[64,1792]{1,0:T(8,128)S(1)}, u32[]{:S(2)}, u32[]{:S(2)}) collective-permute-start(f32[64,1792]{1,0:T(8,128)S(1)} %get-tuple-element.459), channel_id=1, source_target_pairs={{8,0},{16,8},{24,16},{9,1},{17,9},{25,17},{10,2},{18,10},{26,18},{... | collective-permute-start | bytes 1376264 | tf_op jit(solution)/shard_map/ppermute | solution.py:118
  757.7 15.6 %collective-permute-start.159 = (f32[64,1792]{1,0:T(8,128)S(1)}, f32[64,1792]{1,0:T(8,128)S(1)}, u32[]{:S(2)}, u32[]{:S(2)}) collective-permute-start(f32[64,1792]{1,0:T(8,128)S(1)} %get-tuple-element.552), channel_id=1, source_target_pairs={{0,5},{1,6},{2,7},{3,0},{4,1},{5,2},{6,3},{7,4},{8,13},{9,14},{10,... | collective-permute-start | bytes 1376264 | tf_op jit(solution)/shard_map/ppermute | solution.py:80
  766.2 16.2 %collective-permute-start.104 = (f32[64,1792]{1,0:T(8,128)S(1)}, f32[64,1792]{1,0:T(8,128)S(1)}, u32[]{:S(2)}, u32[]{:S(2)}) collective-permute-start(f32[64,1792]{1,0:T(8,128)S(1)} %get-tuple-element.463), channel_id=1, source_target_pairs={{0,8},{8,16},{16,24},{1,9},{9,17},{17,25},{2,10},{10,18},{18,26},{... | collective-permute-start | bytes 1376264 | tf_op jit(solution)/shard_map/ppermute | solution.py:117
  853.5 143.5 %collective-permute-start.137 = (f32[64,1792]{1,0:T(8,128)S(1)}, f32[64,1792]{1,0:T(8,128)S(1)}, u32[]{:S(2)}, u32[]{:S(2)}) collective-permute-start(f32[64,1792]{1,0:T(8,128)S(1)} %get-tuple-element.704), channel_id=1, source_target_pairs={{0,1},{1,2},{2,3},{3,4},{4,5},{5,6},{6,7},{7,0},{8,9},{9,10},{10,1... | collective-permute-start | bytes 1376264 | tf_op jit(solution)/shard_map/ppermute | solution.py:63
  870.4 146.3 %collective-permute-start.160 = (f32[64,1792]{1,0:T(8,128)S(1)}, f32[64,1792]{1,0:T(8,128)S(1)}, u32[]{:S(2)}, u32[]{:S(2)}) collective-permute-start(f32[64,1792]{1,0:T(8,128)S(1)} %get-tuple-element.550), channel_id=1, source_target_pairs={{0,6},{1,7},{2,0},{3,1},{4,2},{5,3},{6,4},{7,5},{8,14},{9,15},{10,... | collective-permute-start | bytes 1376264 | tf_op jit(solution)/shard_map/ppermute | solution.py:80
  969.1 59.9 %collective-permute-start.161 = (f32[64,1792]{1,0:T(8,128)S(1)}, f32[64,1792]{1,0:T(8,128)S(1)}, u32[]{:S(2)}, u32[]{:S(2)}) collective-permute-start(f32[64,1792]{1,0:T(8,128)S(1)} %get-tuple-element.548), channel_id=1, source_target_pairs={{0,6},{1,7},{2,0},{3,1},{4,2},{5,3},{6,4},{7,5},{8,14},{9,15},{10,... | collective-permute-start | bytes 1376264 | tf_op jit(solution)/shard_map/ppermute | solution.py:80
  995.7 15.3 %collective-permute-start.139 = (f32[64,1792]{1,0:T(8,128)S(1)}, f32[64,1792]{1,0:T(8,128)S(1)}, u32[]{:S(2)}, u32[]{:S(2)}) collective-permute-start(f32[64,1792]{1,0:T(8,128)S(1)} %get-tuple-element.523), channel_id=1, source_target_pairs={{8,0},{16,8},{24,16},{9,1},{17,9},{25,17},{10,2},{18,10},{26,18},{... | collective-permute-start | bytes 1376264 | tf_op jit(solution)/shard_map/ppermute | solution.py:118
  1017.6 23.8 %collective-permute-start.162 = (f32[64,1792]{1,0:T(8,128)S(1)}, f32[64,1792]{1,0:T(8,128)S(1)}, u32[]{:S(2)}, u32[]{:S(2)}) collective-permute-start(f32[64,1792]{1,0:T(8,128)S(1)} %get-tuple-element.546), channel_id=1, source_target_pairs={{0,7},{1,0},{2,1},{3,2},{4,3},{5,4},{6,5},{7,6},{8,15},{9,8},{10,9... | collective-permute-start | bytes 1376264 | tf_op jit(solution)/shard_map/ppermute | solution.py:80
  1029.9 28.4 %collective-permute-start.163 = (f32[64,1792]{1,0:T(8,128)S(1)}, f32[64,1792]{1,0:T(8,128)S(1)}, u32[]{:S(2)}, u32[]{:S(2)}) collective-permute-start(f32[64,1792]{1,0:T(8,128)S(1)} %get-tuple-element.544), channel_id=1, source_target_pairs={{0,7},{1,0},{2,1},{3,2},{4,3},{5,4},{6,5},{7,6},{8,15},{9,8},{10,9... | collective-permute-start | bytes 1376264 | tf_op jit(solution)/shard_map/ppermute | solution.py:80
  (141 other events, 2076.5 us)

commit v2 on v1

v2 whole, which is shorter than its diff:
```python
import jax
import jax.numpy as jnp
from jax import lax
from jax.experimental import pallas as pl
from jax.sharding import PartitionSpec as P

OUTER_RATE = 0.7
MOMENTUM_COEF = 0.5
STEPS = 8


def blank(shape):
    return pl.pallas_call(
        lambda out: None,
        out_shape=jax.ShapeDtypeStruct(shape, jnp.float32),
        out_specs=pl.BlockSpec(memory_space=pl.ANY),
    )()


def body(inner_weights, start_weights, momentum):
    groups = lax.axis_size("grp")
    shards = lax.axis_size("shard")
    tp_size = lax.axis_size("tp")
    plane = shards * tp_size
    group = lax.axis_index("grp")
    place = lax.axis_index(("shard", "tp"))
    row_count, col_count = start_weights.shape[1:]
    q_rows = row_count // (groups * plane)
    steps = min(STEPS, plane)
    merge = plane // steps
    block = (q_rows, col_count)

    inner = inner_weights.reshape((2, groups, plane) + block)
    start = start_weights.reshape((2, groups, plane) + block)
    held = momentum.reshape((2, plane) + block)
    rightward = [(i, i + 1) for i in range(groups - 1)]
    leftward = [(i + 1, i) for i in range(groups - 1)]

    def lane(shift):
        return lax.rem(place + shift, plane)

    def cut(array, *at):
        return lax.dynamic_slice(array, at + (0, 0), (1,) * len(at) + block).reshape(block)

    def join(parts):
        return parts[0] if merge == 1 else jnp.concatenate(parts, axis=0)

    def parts_of(chunk):
        return [chunk[m * q_rows : (m + 1) * q_rows] for m in range(merge)]

    def rows_of(array, matrix, owner, step):
        return join([cut(array, matrix, owner, lane(step * merge + m)) for m in range(merge)])

    def own(matrix, owner, step):
        return rows_of(start, matrix, owner, step) - rows_of(inner, matrix, owner, step)

    def rotate(part, shift):
        if shift % plane == 0:
            return part
        return lax.ppermute(part, ("shard", "tp"), [(i, (i + shift) % plane) for i in range(plane)])

    new_weights = blank(start.shape)
    new_held = blank(held.shape)

    def write_weights(array, matrix, owner, step, update):
        for m, part in enumerate(parts_of(update)):
            at = (matrix, owner, lane(step * merge + m))
            array = lax.dynamic_update_slice(array, (cut(start, *at) - part)[None, None, None], at + (0, 0))
        return array

    def after(first, *arrays):
        return lax.optimization_barrier((first, *arrays))[1:]

    order = [(turn + 1) % steps for turn in range(steps)]
    zero = jnp.zeros((merge * q_rows, col_count), jnp.float32)
    from_left, from_right = [zero, zero], [zero, zero]
    arrived_left, arrived_right = [[], []], [[], []]
    moved, outgoing, transit = {}, {}, []
    payload = zero

    def fetch(matrix, step):
        shifts = [step * merge + m for m in range(merge)]
        parts = after(payload, *[cut(held, matrix, lane(plane - shift)) for shift in shifts])
        return ("fetch", matrix, step, [rotate(part, -shift) for part, shift in zip(parts, shifts)])

    def deliver(matrix, step):
        shifts = [step * merge + m for m in range(merge)]
        parts = after(payload, *parts_of(outgoing[matrix, step]))
        return ("deliver", matrix, step, [rotate(part, shift) for part, shift in zip(parts, shifts)])

    def land(array, matrix, step, parts):
        for m, part in enumerate(parts):
            shift = step * merge + m
            array = lax.dynamic_update_slice(array, part[None, None], (matrix, lane(plane - shift), 0, 0))
        return array

    last_phase = groups - 2
    for turn in range(steps + 1):
        for phase in range(1, groups + 1):
            if turn == steps and phase > last_phase:
                break
            for matrix in range(2):
                tick = ((turn * groups) + phase - 1) * 2 + matrix
                landed = [entry for entry in transit if entry[0] <= tick]
                transit = [entry for entry in transit if entry[0] > tick]
                values = after(payload, from_left[matrix], from_right[matrix], *[p for e in landed for p in e[4]])
                here_left, here_right, values = values[0], values[1], list(values[2:])
                for _, kind, at, step, parts in landed:
                    parts, values = values[: len(parts)], values[len(parts) :]
                    if kind == "fetch":
                        moved[at, step] = join(parts)
                    else:
                        new_held = land(new_held, at, step, parts)
                if phase < groups:
                    to_right, to_left = here_left, here_right
                    if turn < steps:
                        right_owner = jnp.minimum(groups - phase + group, groups - 1)
                        left_owner = jnp.maximum(group - (groups - phase), 0)
                        to_right = jnp.where(group < phase, to_right + own(matrix, right_owner, order[turn]), to_right)
                        to_left = jnp.where(
                            groups - 1 - group < phase, to_left + own(matrix, left_owner, order[turn]), to_left
                        )
                else:
                    step = order[turn]
                    if (matrix, step) not in moved:
                        moved[matrix, step] = join(fetch(matrix, step)[3])
                    total = own(matrix, group, step) + here_left + here_right
                    mean_diff = total / groups
                    new_momentum = MOMENTUM_COEF * moved[matrix, step] + mean_diff
                    update = OUTER_RATE * (mean_diff + MOMENTUM_COEF * new_momentum)
                    outgoing[matrix, step] = new_momentum
                    if turn == steps - 1:
                        new_held = land(new_held, *deliver(matrix, step)[1:])
                    new_weights = write_weights(new_weights, matrix, group, step, update)
                    to_right = to_left = update
                payload = to_right
                from_left[matrix] = lax.ppermute(to_right, "grp", rightward)
                from_right[matrix] = lax.ppermute(to_left, "grp", leftward)
                place_in_turn = tick - turn * groups * 2
                if place_in_turn in (0, 2) and turn < steps - 1:
                    transit.append((tick + 2,) + fetch(place_in_turn // 2, order[turn]))
                if place_in_turn in (4, 6) and 0 < turn < steps:
                    transit.append((tick + 2,) + deliver(place_in_turn // 2 - 2, order[turn - 1]))
                if phase == groups:
                    arrived_left[matrix], arrived_right[matrix] = [], []
                arrived_left[matrix].append(from_left[matrix])
                arrived_right[matrix].append(from_right[matrix])
                if len(arrived_left[matrix]) == groups - 1 and turn > 0:
                    for hop in range(groups - 1):
                        update = jnp.where(
                            group > hop,
                            arrived_left[matrix][hop],
                            arrived_right[matrix][groups - 2 - hop],
                        )
                        owner = lax.rem(group + groups - 1 - hop, groups)
                        new_weights = write_weights(new_weights, matrix, owner, order[turn - 1], update)
    for _, _, at, step, parts in transit:
        new_held = land(new_held, at, step, parts)
    return (new_weights.reshape(start_weights.shape), new_held.reshape(momentum.shape))


def solution(mesh):
    in_specs = (
        P("grp", None, "shard", "tp"),
        P(None, "shard", "tp"),
        P(None, None, None, ("grp", "shard", "tp"), None, None),
    )
    out_specs = (P(None, "shard", "tp"), P(None, None, None, ("grp", "shard", "tp"), None, None))
    return jax.shard_map(body, mesh=mesh, in_specs=in_specs, out_specs=out_specs, check_vma=False)
```

time: 1090 us -> 915 us (0.84)
  waiting for transfers between devices: 523 us -> 253 us
  starting transfers between devices: 393 us -> 443 us
  other arithmetic: 151 us -> 194 us
    ppermute x68, waiting for transfers between devices: 214 us -> 21.8 us  [body(): from_left[matrix] = lax.ppermute(to_right, 'grp', rightward)]
    ppermute x68, waiting for transfers between devices: 286 us -> 224 us  [body(): from_right[matrix] = lax.ppermute(to_left, 'grp', leftward)]
    ppermute x68, starting transfers between devices: 264 us -> 306 us  [body(): from_left[matrix] = lax.ppermute(to_right, 'grp', rightward)]
    dynamic_update_slice x64, other arithmetic: 59.6 us -> 86.4 us  [write_weights(): lax.dynamic_update_slice(array, (cut(start, *at) - part)[None, None, None...]
    ppermute x28, waiting for transfers between devices: 22.9 us -> 7.98 us  [rotate(): lax.ppermute(part, ('shard', 'tp'), [(i, (i + shift) % plane) for i in ra...]
    select_n x48, other arithmetic: 67.7 us -> 81.5 us  [the longest x26 47.6 us: body(): jnp.where(groups - 1 - group < phase, to_left + own(matrix, left_owner, o...]
    add x14 -> x16, other arithmetic: 16.4 us -> 26.2 us  [body(): new_momentum = MOMENTUM_COEF * moved[matrix, step] + mean_diff]
  transfers between devices with their start and end apart: 164 -> 164, of which waited for: 130 -> 71; matrix products, arithmetic and copies ran while one was open for 15% -> 22% of each run, Pallas kernels for 0% -> 0%
where the time goes in v2:
time: 915 us; the launch traced here: 902 us
  starting transfers between devices  443 us (48%)
  waiting for transfers between devices  253 us (28%)
  other arithmetic  194 us (21%)
    ppermute x68, starting transfers between devices, body(): from_left[matrix] = lax.ppermute(to_right, 'grp', rightward)  306 us
    ppermute x68, waiting for transfers between devices, body(): from_right[matrix] = lax.ppermute(to_left, 'grp', leftward)  224 us
    ppermute x68, starting transfers between devices, body(): from_right[matrix] = lax.ppermute(to_left, 'grp', leftward)  97.8 us
    dynamic_update_slice x64, other arithmetic, write_weights(): lax.dynamic_update_slice(array, (cut(start, *at) - part)[None, None, None...  86.4 us
    select_n x26, other arithmetic, body(): jnp.where(groups - 1 - group < phase, to_left + own(matrix, left_owner, o...  47.6 us
    ppermute x28, starting transfers between devices, rotate(): lax.ppermute(part, ('shard', 'tp'), [(i, (i + shift) % plane) for i in ra...  39.4 us
    select_n x22, other arithmetic, body(): jnp.where(group < phase, to_right + own(matrix, right_owner, order[turn])...  33.9 us
    add x16, other arithmetic, body(): new_momentum = MOMENTUM_COEF * moved[matrix, step] + mean_diff  26.2 us
  transfers between devices with their start and end apart: 164, of which 71 were waited for; matrix products, arithmetic and copies ran while one was open for 22% of the time, Pallas kernels for 0%

profile of v2, /device:TPU:0, one launch (start us, length us, event | category | flops | bytes accessed | tf_op | source)
XLA Modules:
  0.0 901.9 jit_solution(4585114339779845184)
XLA Ops:
  2.7 4.9 collective-permute-start
  10.6 6.1 dynamic-slice_bitcast_fusion
  28.3 5.7 collective-permute-start.5
  36.4 6.4 collective-permute-done.4
  46.5 5.3 collective-permute-start.8
  51.8 8.0 collective-permute-done.6
  62.8 5.3 collective-permute-start.10
  68.1 7.0 collective-permute-done.9
  84.6 8.1 collective-permute-done.11
  137.3 5.8 collective-permute-start.22
  155.4 5.1 collective-permute-done.21
  233.5 7.6 collective-permute-done.39
  248.8 8.2 collective-permute-done.44
  264.5 7.5 collective-permute-done.41
  290.8 5.1 collective-permute-start.51
  350.0 5.6 collective-permute-start.62
  474.6 8.3 collective-permute-done.81
  511.8 5.6 collective-permute-done.89
  554.5 5.4 collective-permute-done.99
  562.7 5.3 collective-permute-start.102
  574.2 10.7 %collective-permute-start.101 = (f32[64,1792]{1,0:T(8,128)S(1)}, f32[64,1792]{1,0:T(8,128)S(1)}, u32[]{:S(2)}, u32[]{:S(2)}) collective-permute-start(f32[64,1792]{1,0:T(8,128)S(1)} %get-tuple-element.488), channel_id=1, source_target_pairs={{8,0},{16,8},{24,16},{9,1},{17,9},{25,17},{10,2},{18,10},{26,18},{... | collective-permute-start | bytes 1376264 | tf_op jit(solution)/shard_map/ppermute | solution.py:138
  612.7 5.7 collective-permute-done.109
  655.9 7.8 collective-permute-done.119
  671.1 6.8 collective-permute-done.124
  685.2 6.0 collective-permute-done.121
  717.7 5.7 collective-permute-done.129
  733.2 5.6 collective-permute-start.135
  770.6 5.9 collective-permute-start.141
  776.5 7.6 collective-permute-done.143
  791.6 8.4 collective-permute-done.140
  802.7 4.9 collective-permute-start.146
  822.8 10.2 %collective-permute-done.147 = f32[64,1792]{1,0:T(8,128)S(1)} collective-permute-done((f32[64,1792]{1,0:T(8,128)S(1)}, f32[64,1792]{1,0:T(8,128)S(1)}, u32[]{:S(2)}, u32[]{:S(2)}) %collective-permute-start.147) | collective-permute-done | bytes 458784 | tf_op jit(solution)/shard_map/ppermute | solution.py:138
  (524 shorter events, 687.0 us)
Async XLA Ops:
  28.3 23.5 %collective-permute-start.5 = (f32[64,1792]{1,0:T(8,128)S(1)}, f32[64,1792]{1,0:T(8,128)}, u32[]{:S(2)}, u32[]{:S(2)}) collective-permute-start(f32[64,1792]{1,0:T(8,128)S(1)} %get-tuple-element.545), channel_id=1, source_target_pairs={{0,8},{8,16},{16,24},{1,9},{9,17},{17,25},{2,10},{10,18},{18,26},{... | collective-permute-start | bytes 1376264 | tf_op jit(solution)/shard_map/ppermute | solution.py:137
  46.5 21.7 %collective-permute-start.8 = (f32[64,1792]{1,0:T(8,128)S(1)}, f32[64,1792]{1,0:T(8,128)}, u32[]{:S(2)}, u32[]{:S(2)}) collective-permute-start(f32[64,1792]{1,0:T(8,128)S(1)} %get-tuple-element.543), channel_id=1, source_target_pairs={{0,8},{8,16},{16,24},{1,9},{9,17},{17,25},{2,10},{10,18},{18,26},{... | collective-permute-start | bytes 1376264 | tf_op jit(solution)/shard_map/ppermute | solution.py:137
  62.8 21.8 %collective-permute-start.10 = (f32[64,1792]{1,0:T(8,128)S(1)}, f32[64,1792]{1,0:T(8,128)}, u32[]{:S(2)}, u32[]{:S(2)}) collective-permute-start(f32[64,1792]{1,0:T(8,128)S(1)} %get-tuple-element.541), channel_id=1, source_target_pairs={{0,8},{8,16},{16,24},{1,9},{9,17},{17,25},{2,10},{10,18},{18,26},{... | collective-permute-start | bytes 1376264 | tf_op jit(solution)/shard_map/ppermute | solution.py:137
  78.7 22.8 %collective-permute-start.12 = (f32[64,1792]{1,0:T(8,128)S(1)}, f32[64,1792]{1,0:T(8,128)S(1)}, u32[]{:S(2)}, u32[]{:S(2)}) collective-permute-start(f32[64,1792]{1,0:T(8,128)S(1)} %get-tuple-element.539), channel_id=1, source_target_pairs={{0,8},{8,16},{16,24},{1,9},{9,17},{17,25},{2,10},{10,18},{18,26},{... | collective-permute-start | bytes 1376264 | tf_op jit(solution)/shard_map/ppermute | solution.py:137
  150.7 23.5 %collective-permute-start.26 = (f32[64,1792]{1,0:T(8,128)}, f32[64,1792]{1,0:T(8,128)S(1)}, u32[]{:S(2)}, u32[]{:S(2)}) collective-permute-start(f32[64,1792]{1,0:T(8,128)} %get-tuple-element.531), channel_id=1, source_target_pairs={{0,8},{8,16},{16,24},{1,9},{9,17},{17,25},{2,10},{10,18},{18,26},{... | collective-permute-start | bytes 1376264 | tf_op jit(solution)/shard_map/ppermute | solution.py:137
  163.5 25.6 %collective-permute-start.28 = (f32[64,1792]{1,0:T(8,128)S(1)}, f32[64,1792]{1,0:T(8,128)S(1)}, u32[]{:S(2)}, u32[]{:S(2)}) collective-permute-start(f32[64,1792]{1,0:T(8,128)S(1)} %get-tuple-element.529), channel_id=1, source_target_pairs={{0,8},{8,16},{16,24},{1,9},{9,17},{17,25},{2,10},{10,18},{18,26},{... | collective-permute-start | bytes 1376264 | tf_op jit(solution)/shard_map/ppermute | solution.py:137
  168.4 20.7 %collective-permute-start.30 = (f32[64,1792]{1,0:T(8,128)}, f32[64,1792]{1,0:T(8,128)S(1)}, u32[]{:S(2)}, u32[]{:S(2)}) collective-permute-start(f32[64,1792]{1,0:T(8,128)} %get-tuple-element.231), channel_id=1, source_target_pairs={{0,1},{1,2},{2,3},{3,4},{4,5},{5,6},{6,7},{7,0},{8,9},{9,10},{10,1... | collective-permute-start | bytes 1376264 | tf_op jit(solution)/shard_map/ppermute | solution.py:60
  177.6 21.2 %collective-permute-start.31 = (f32[64,1792]{1,0:T(8,128)S(1)}, f32[64,1792]{1,0:T(8,128)S(1)}, u32[]{:S(2)}, u32[]{:S(2)}) collective-permute-start(f32[64,1792]{1,0:T(8,128)S(1)} %get-tuple-element.528), channel_id=1, source_target_pairs={{0,8},{8,16},{16,24},{1,9},{9,17},{17,25},{2,10},{10,18},{18,26},{... | collective-permute-start | bytes 1376264 | tf_op jit(solution)/shard_map/ppermute | solution.py:137
  212.7 20.8 %collective-permute-start.38 = (f32[64,1792]{1,0:T(8,128)S(1)}, f32[64,1792]{1,0:T(8,128)S(1)}, u32[]{:S(2)}, u32[]{:S(2)}) collective-permute-start(f32[64,1792]{1,0:T(8,128)S(1)} %add_select_fusion.71), channel_id=1, source_target_pairs={{0,8},{8,16},{16,24},{1,9},{9,17},{17,25},{2,10},{10,18},{18,26},{... | collective-permute-start | bytes 1376264 | tf_op jit(solution)/shard_map/ppermute | solution.py:137
  244.1 20.4 %collective-permute-start.42 = (f32[64,1792]{1,0:T(8,128)S(1)}, f32[64,1792]{1,0:T(8,128)S(1)}, u32[]{:S(2)}, u32[]{:S(2)}) collective-permute-start(f32[64,1792]{1,0:T(8,128)S(1)} %get-tuple-element.523), channel_id=1, source_target_pairs={{0,8},{8,16},{16,24},{1,9},{9,17},{17,25},{2,10},{10,18},{18,26},{... | collective-permute-start | bytes 1376264 | tf_op jit(solution)/shard_map/ppermute | solution.py:137
  259.9 25.7 %collective-permute-start.46 = (f32[64,1792]{1,0:T(8,128)S(1)}, f32[64,1792]{1,0:T(8,128)S(1)}, u32[]{:S(2)}, u32[]{:S(2)}) collective-permute-start(f32[64,1792]{1,0:T(8,128)S(1)} %get-tuple-element.520), channel_id=1, source_target_pairs={{0,8},{8,16},{16,24},{1,9},{9,17},{17,25},{2,10},{10,18},{18,26},{... | collective-permute-start | bytes 1376264 | tf_op jit(solution)/shard_map/ppermute | solution.py:137
  275.0 28.1 %collective-permute-start.48 = (f32[64,1792]{1,0:T(8,128)S(1)}, f32[64,1792]{1,0:T(8,128)S(1)}, u32[]{:S(2)}, u32[]{:S(2)}) collective-permute-start(f32[64,1792]{1,0:T(8,128)S(1)} %get-tuple-element.518), channel_id=1, source_target_pairs={{0,8},{8,16},{16,24},{1,9},{9,17},{17,25},{2,10},{10,18},{18,26},{... | collective-permute-start | bytes 1376264 | tf_op jit(solution)/shard_map/ppermute | solution.py:137
  279.9 23.2 %collective-permute-start.50 = (f32[64,1792]{1,0:T(8,128)S(1)}, f32[64,1792]{1,0:T(8,128)S(1)}, u32[]{:S(2)}, u32[]{:S(2)}) collective-permute-start(f32[64,1792]{1,0:T(8,128)S(1)} %get-tuple-element.253), channel_id=1, source_target_pairs={{0,2},{1,3},{2,4},{3,5},{4,6},{5,7},{6,0},{7,1},{8,10},{9,11},{10,... | collective-permute-start | bytes 1376264 | tf_op jit(solution)/shard_map/ppermute | solution.py:60
  290.8 23.9 %collective-permute-start.51 = (f32[64,1792]{1,0:T(8,128)S(1)}, f32[64,1792]{1,0:T(8,128)S(1)}, u32[]{:S(2)}, u32[]{:S(2)}) collective-permute-start(f32[64,1792]{1,0:T(8,128)S(1)} %get-tuple-element.517), channel_id=1, source_target_pairs={{0,8},{8,16},{16,24},{1,9},{9,17},{17,25},{2,10},{10,18},{18,26},{... | collective-permute-start | bytes 1376264 | tf_op jit(solution)/shard_map/ppermute | solution.py:137
  363.4 23.3 %collective-permute-start.66 = (f32[64,1792]{1,0:T(8,128)}, f32[64,1792]{1,0:T(8,128)S(1)}, u32[]{:S(2)}, u32[]{:S(2)}) collective-permute-start(f32[64,1792]{1,0:T(8,128)} %get-tuple-element.509), channel_id=1, source_target_pairs={{0,8},{8,16},{16,24},{1,9},{9,17},{17,25},{2,10},{10,18},{18,26},{... | collective-permute-start | bytes 1376264 | tf_op jit(solution)/shard_map/ppermute | solution.py:137
  375.8 26.6 %collective-permute-start.68 = (f32[64,1792]{1,0:T(8,128)S(1)}, f32[64,1792]{1,0:T(8,128)S(1)}, u32[]{:S(2)}, u32[]{:S(2)}) collective-permute-start(f32[64,1792]{1,0:T(8,128)S(1)} %get-tuple-element.507), channel_id=1, source_target_pairs={{0,8},{8,16},{16,24},{1,9},{9,17},{17,25},{2,10},{10,18},{18,26},{... | collective-permute-start | bytes 1376264 | tf_op jit(solution)/shard_map/ppermute | solution.py:137
  380.5 21.9 %collective-permute-start.70 = (f32[64,1792]{1,0:T(8,128)}, f32[64,1792]{1,0:T(8,128)S(1)}, u32[]{:S(2)}, u32[]{:S(2)}) collective-permute-start(f32[64,1792]{1,0:T(8,128)} %get-tuple-element.275), channel_id=1, source_target_pairs={{0,3},{1,4},{2,5},{3,6},{4,7},{5,0},{6,1},{7,2},{8,11},{9,12},{10,... | collective-permute-start | bytes 1376264 | tf_op jit(solution)/shard_map/ppermute | solution.py:60
  390.1 22.5 %collective-permute-start.71 = (f32[64,1792]{1,0:T(8,128)S(1)}, f32[64,1792]{1,0:T(8,128)S(1)}, u32[]{:S(2)}, u32[]{:S(2)}) collective-permute-start(f32[64,1792]{1,0:T(8,128)S(1)} %get-tuple-element.506), channel_id=1, source_target_pairs={{0,8},{8,16},{16,24},{1,9},{9,17},{17,25},{2,10},{10,18},{18,26},{... | collective-permute-start | bytes 1376264 | tf_op jit(solution)/shard_map/ppermute | solution.py:137
  469.8 29.2 %collective-permute-start.86 = (f32[64,1792]{1,0:T(8,128)S(1)}, f32[64,1792]{1,0:T(8,128)S(1)}, u32[]{:S(2)}, u32[]{:S(2)}) collective-permute-start(f32[64,1792]{1,0:T(8,128)S(1)} %get-tuple-element.498), channel_id=1, source_target_pairs={{0,8},{8,16},{16,24},{1,9},{9,17},{17,25},{2,10},{10,18},{18,26},{... | collective-permute-start | bytes 1376264 | tf_op jit(solution)/shard_map/ppermute | solution.py:137
  485.9 25.9 %collective-permute-start.88 = (f32[64,1792]{1,0:T(8,128)S(1)}, f32[64,1792]{1,0:T(8,128)S(1)}, u32[]{:S(2)}, u32[]{:S(2)}) collective-permute-start(f32[64,1792]{1,0:T(8,128)S(1)} %get-tuple-element.496), channel_id=1, source_target_pairs={{0,8},{8,16},{16,24},{1,9},{9,17},{17,25},{2,10},{10,18},{18,26},{... | collective-permute-start | bytes 1376264 | tf_op jit(solution)/shard_map/ppermute | solution.py:137
  490.5 21.3 %collective-permute-start.90 = (f32[64,1792]{1,0:T(8,128)S(1)}, f32[64,1792]{1,0:T(8,128)S(1)}, u32[]{:S(2)}, u32[]{:S(2)}) collective-permute-start(f32[64,1792]{1,0:T(8,128)S(1)} %get-tuple-element.297), channel_id=1, source_target_pairs={{0,4},{1,5},{2,6},{3,7},{4,0},{5,1},{6,2},{7,3},{8,12},{9,13},{10,... | collective-permute-start | bytes 1376264 | tf_op jit(solution)/shard_map/ppermute | solution.py:60
  503.4 21.9 %collective-permute-start.91 = (f32[64,1792]{1,0:T(8,128)}, f32[64,1792]{1,0:T(8,128)S(1)}, u32[]{:S(2)}, u32[]{:S(2)}) collective-permute-start(f32[64,1792]{1,0:T(8,128)} %get-tuple-element.495), channel_id=1, source_target_pairs={{0,8},{8,16},{16,24},{1,9},{9,17},{17,25},{2,10},{10,18},{18,26},{... | collective-permute-start | bytes 1376264 | tf_op jit(solution)/shard_map/ppermute | solution.py:137
  562.7 26.9 %collective-permute-start.102 = (f32[64,1792]{1,0:T(8,128)S(1)}, f32[64,1792]{1,0:T(8,128)S(1)}, u32[]{:S(2)}, u32[]{:S(2)}) collective-permute-start(f32[64,1792]{1,0:T(8,128)S(1)} %get-tuple-element.490), channel_id=1, source_target_pairs={{0,8},{8,16},{16,24},{1,9},{9,17},{17,25},{2,10},{10,18},{18,26},{... | collective-permute-start | bytes 1376264 | tf_op jit(solution)/shard_map/ppermute | solution.py:137
  568.0 21.6 %collective-permute-start.107 = (f32[64,1792]{1,0:T(8,128)S(1)}, f32[64,1792]{1,0:T(8,128)S(1)}, u32[]{:S(2)}, u32[]{:S(2)}) collective-permute-start(f32[64,1792]{1,0:T(8,128)S(1)} %copy-done.22), channel_id=1, source_target_pairs={{0,2},{1,3},{2,4},{3,5},{4,6},{5,7},{6,0},{7,1},{8,10},{9,11},{10,... | collective-permute-start | bytes 1376264 | tf_op jit(solution)/shard_map/ppermute | solution.py:60
  604.3 21.3 %collective-permute-start.111 = (f32[64,1792]{1,0:T(8,128)S(1)}, f32[64,1792]{1,0:T(8,128)S(1)}, u32[]{:S(2)}, u32[]{:S(2)}) collective-permute-start(f32[64,1792]{1,0:T(8,128)S(1)} %get-tuple-element.484), channel_id=1, source_target_pairs={{0,8},{8,16},{16,24},{1,9},{9,17},{17,25},{2,10},{10,18},{18,26},{... | collective-permute-start | bytes 1376264 | tf_op jit(solution)/shard_map/ppermute | solution.py:137
  680.6 24.9 %collective-permute-start.126 = (f32[64,1792]{1,0:T(8,128)S(1)}, f32[64,1792]{1,0:T(8,128)S(1)}, u32[]{:S(2)}, u32[]{:S(2)}) collective-permute-start(f32[64,1792]{1,0:T(8,128)S(1)} %get-tuple-element.476), channel_id=1, source_target_pairs={{0,8},{8,16},{16,24},{1,9},{9,17},{17,25},{2,10},{10,18},{18,26},{... | collective-permute-start | bytes 1376264 | tf_op jit(solution)/shard_map/ppermute | solution.py:137
  693.9 23.9 %collective-permute-start.128 = (f32[64,1792]{1,0:T(8,128)S(1)}, f32[64,1792]{1,0:T(8,128)S(1)}, u32[]{:S(2)}, u32[]{:S(2)}) collective-permute-start(f32[64,1792]{1,0:T(8,128)S(1)} %get-tuple-element.474), channel_id=1, source_target_pairs={{0,8},{8,16},{16,24},{1,9},{9,17},{17,25},{2,10},{10,18},{18,26},{... | collective-permute-start | bytes 1376264 | tf_op jit(solution)/shard_map/ppermute | solution.py:137
  709.3 21.0 %collective-permute-start.131 = (f32[64,1792]{1,0:T(8,128)}, f32[64,1792]{1,0:T(8,128)S(1)}, u32[]{:S(2)}, u32[]{:S(2)}) collective-permute-start(f32[64,1792]{1,0:T(8,128)} %get-tuple-element.473), channel_id=1, source_target_pairs={{0,8},{8,16},{16,24},{1,9},{9,17},{17,25},{2,10},{10,18},{18,26},{... | collective-permute-start | bytes 1376264 | tf_op jit(solution)/shard_map/ppermute | solution.py:137
  770.6 21.0 %collective-permute-start.141 = (f32[64,1792]{1,0:T(8,128)S(1)}, f32[64,1792]{1,0:T(8,128)S(1)}, u32[]{:S(2)}, u32[]{:S(2)}) collective-permute-start(f32[64,1792]{1,0:T(8,128)S(1)} %get-tuple-element.468), channel_id=1, source_target_pairs={{0,8},{8,16},{16,24},{1,9},{9,17},{17,25},{2,10},{10,18},{18,26},{... | collective-permute-start | bytes 1376264 | tf_op jit(solution)/shard_map/ppermute | solution.py:137
  786.7 23.5 %collective-permute-start.145 = (f32[64,1792]{1,0:T(8,128)S(1)}, f32[64,1792]{1,0:T(8,128)S(1)}, u32[]{:S(2)}, u32[]{:S(2)}) collective-permute-start(f32[64,1792]{1,0:T(8,128)S(1)} %get-tuple-element.465), channel_id=1, source_target_pairs={{0,8},{8,16},{16,24},{1,9},{9,17},{17,25},{2,10},{10,18},{18,26},{... | collective-permute-start | bytes 1376264 | tf_op jit(solution)/shard_map/ppermute | solution.py:137
  813.7 25.0 %collective-permute-start.149 = (f32[64,1792]{1,0:T(8,128)S(1)}, f32[64,1792]{1,0:T(8,128)S(1)}, u32[]{:S(2)}, u32[]{:S(2)}) collective-permute-start(f32[64,1792]{1,0:T(8,128)S(1)} %get-tuple-element.462), channel_id=1, source_target_pairs={{0,8},{8,16},{16,24},{1,9},{9,17},{17,25},{2,10},{10,18},{18,26},{... | collective-permute-start | bytes 1376264 | tf_op jit(solution)/shard_map/ppermute | solution.py:137
  819.0 23.9 %collective-permute-start.150 = (f32[64,1792]{1,0:T(8,128)S(1)}, f32[64,1792]{1,0:T(8,128)S(1)}, u32[]{:S(2)}, u32[]{:S(2)}) collective-permute-start(f32[64,1792]{1,0:T(8,128)S(1)} %get-tuple-element.460), channel_id=1, source_target_pairs={{8,0},{16,8},{24,16},{9,1},{17,9},{25,17},{10,2},{18,10},{26,18},{... | collective-permute-start | bytes 1376264 | tf_op jit(solution)/shard_map/ppermute | solution.py:138
  (171 other events, 4793.4 us)

commit v3 on v0

v3 whole, which is shorter than its diff:
```python
import jax
import jax.numpy as jnp
from jax import lax
from jax.experimental import pallas as pl
from jax.sharding import PartitionSpec as P

OUTER_RATE = 0.7
MOMENTUM_COEF = 0.5
STEPS = 8


def blank(shape):
    return pl.pallas_call(
        lambda out: None,
        out_shape=jax.ShapeDtypeStruct(shape, jnp.float32),
        out_specs=pl.BlockSpec(memory_space=pl.ANY),
    )()


def after(first, *arrays):
    return lax.optimization_barrier((first, *arrays))[1:]


def body(inner_weights, start_weights, momentum):
    groups = lax.axis_size("grp")
    plane = lax.axis_size("shard") * lax.axis_size("tp")
    place = lax.axis_index(("shard", "tp"))
    row_count, col_count = start_weights.shape[1:]
    q_rows = row_count // (groups * plane)
    steps = min(STEPS, plane)
    merge = plane // steps
    block = (q_rows, col_count)

    inner = inner_weights.reshape((2, groups, plane) + block)
    start = start_weights.reshape((2, groups, plane) + block)
    held = momentum.reshape((2, plane) + block)

    def rotate(part, shift):
        if shift % plane == 0:
            return part
        return lax.ppermute(part, ("shard", "tp"), [(i, (i + shift) % plane) for i in range(plane)])

    def shifts_of(step):
        return [step * merge + m for m in range(merge)]

    def join(parts, axis):
        return parts[0] if merge == 1 else jnp.concatenate(parts, axis=axis)

    def rows_of(array, step, place):
        return join([lax.dynamic_slice_in_dim(array, lax.rem(place + s, plane), 1, 2) for s in shifts_of(step)], 2)

    def fetch(step, place):
        parts = [lax.dynamic_slice_in_dim(held, lax.rem(place + plane - s, plane), 1, 1) for s in shifts_of(step)]
        return [rotate(part, -s) for part, s in zip(parts, shifts_of(step))]

    def deliver(step, value):
        return [rotate(value[:, m : m + 1], s) for m, s in enumerate(shifts_of(step))]

    def land(array, step, parts):
        for part, s in zip(parts, shifts_of(step)):
            array = lax.dynamic_update_slice_in_dim(array, part, lax.rem(place + plane - s, plane), 1)
        return array

    def spread(array, step, update):
        for m, s in enumerate(shifts_of(step)):
            at = (0, 0, lax.rem(place + s, plane), 0, 0)
            old = lax.dynamic_slice(start, at, (2, groups, 1) + block)
            array = lax.dynamic_update_slice(array, old - update[:, :, m : m + 1], at)
        return array

    new_weights = blank(start.shape)
    new_held = blank(held.shape)
    order = [(turn + 1) % steps for turn in range(steps)]
    now = place
    moved, sent, gathered = [fetch(order[0], place)], [], []
    for turn in range(steps):
        step = order[turn]
        total = lax.psum_scatter(
            rows_of(start, step, now) - rows_of(inner, step, now), "grp", scatter_dimension=1, tiled=True
        )[:, 0]
        if turn + 1 < steps:
            moved.append(fetch(order[turn + 1], now))
        mean_diff = total / groups
        new_momentum = MOMENTUM_COEF * join(moved[turn], 1) + mean_diff
        update = OUTER_RATE * (mean_diff + MOMENTUM_COEF * new_momentum)
        if turn == 0:
            (now,) = after(update, place)
        else:
            now, gathered[turn - 1], *sent[turn - 1] = after(update, place, gathered[turn - 1], *sent[turn - 1])
            new_held = land(new_held, order[turn - 1], sent[turn - 1])
            new_weights = spread(new_weights, order[turn - 1], gathered[turn - 1])
        sent.append(deliver(step, new_momentum))
        gathered.append(lax.all_gather(update[:, None], "grp", axis=1, tiled=True))
    new_held = land(new_held, order[-1], sent[-1])
    new_weights = spread(new_weights, order[-1], gathered[-1])
    return (new_weights.reshape(start_weights.shape), new_held.reshape(momentum.shape))


def solution(mesh):
    in_specs = (
        P("grp", None, "shard", "tp"),
        P(None, "shard", "tp"),
        P(None, None, None, ("grp", "shard", "tp"), None, None),
    )
    out_specs = (P(None, "shard", "tp"), P(None, None, None, ("grp", "shard", "tp"), None, None))
    return jax.shard_map(body, mesh=mesh, in_specs=in_specs, out_specs=out_specs, check_vma=False)
```

time: 1330 us -> 1210 us (0.910)
  blocking collectives: 727 us -> 0 us
  waiting for transfers between devices: 492 us -> 1020 us
  local copies, waits for them, and re-layouts: 15.9 us -> 50.6 us
  other arithmetic: 83.7 us -> 105 us
  starting transfers between devices: 0.04 us -> 19.6 us
    all_to_all x2 -> x0, blocking collectives: 727 us -> none  [the longest x1 640 us: body(): lax.all_to_all(pieces, ('grp', 'shard', 'tp'), split_axis=1, concat_axis=...]
    reduce_scatter x0 -> x8, waiting for transfers between devices: none -> 451 us  [body(): lax.psum_scatter(rows_of(start, step, now) - rows_of(inner, step, now), '...]
    ppermute x0 -> x14, waiting for transfers between devices: none -> 86.1 us  [rotate(): lax.ppermute(part, ('shard', 'tp'), [(i, (i + shift) % plane) for i in ra...]
    dynamic_update_slice x0 -> x6, other arithmetic: none -> 26.9 us  [the longest x5 24.2 us: spread(): array = lax.dynamic_update_slice(array, old - update[:, :, m:m + 1], at)]
    sub x2 -> x8, other arithmetic: 59.6 us -> 37.9 us  [body(): rows_of(start, step, now) - rows_of(inner, step, now)]
    dynamic_slice x0 -> x3, other arithmetic: none -> 21.4 us  [rows_of(): lax.dynamic_slice_in_dim(array, lax.rem(place + s, plane), 1, 2)]
    all_gather x0 -> x5, local copies, waits for them, and re-layouts: none -> 20.7 us  [body(): gathered.append(lax.all_gather(update[:, None], 'grp', axis=1, tiled=True))]
    ppermute x0 -> x14, starting transfers between devices: none -> 19 us  [rotate(): lax.ppermute(part, ('shard', 'tp'), [(i, (i + shift) % plane) for i in ra...]
  transfers between devices with their start and end apart: 1 -> 30, of which waited for: 1 -> 21; matrix products, arithmetic and copies ran while one was open for 0% -> 9% of each run, Pallas kernels for 0% -> 0%
where the time goes in v3:
time: 1210 us
  waiting for transfers between devices  1020 us (84%)
  other arithmetic  105 us (9%)
  local copies, waits for them, and re-layouts  50.6 us (4%)
  starting transfers between devices  19.6 us (2%)
  between operations  14.2 us (1%)
    all_gather x8, waiting for transfers between devices, body(): gathered.append(lax.all_gather(update[:, None], 'grp', axis=1, tiled=True))  484 us
    reduce_scatter x8, waiting for transfers between devices, body(): lax.psum_scatter(rows_of(start, step, now) - rows_of(inner, step, now), '...  451 us
    ppermute x14, waiting for transfers between devices, rotate(): lax.ppermute(part, ('shard', 'tp'), [(i, (i + shift) % plane) for i in ra...  86.1 us
    sub x8, other arithmetic, body(): rows_of(start, step, now) - rows_of(inner, step, now)  37.9 us
    dynamic_update_slice x5, other arithmetic, spread(): array = lax.dynamic_update_slice(array, old - update[:, :, m:m + 1], at)  24.2 us
  transfers between devices with their start and end apart: 30, of which 21 were waited for; matrix products, arithmetic and copies ran while one was open for 9% of the time, Pallas kernels for 0%

profile of v3, /device:TPU:0, one launch (start us, length us, event | category | flops | bytes accessed | tf_op | source)
XLA Modules:
  0.0 1212.1 jit_solution(16059043716808681467)
XLA Ops:
  19.9 10.9 collective-permute-done
  30.8 55.7 %reduce-scatter.9.cloned.1.call-done = f32[2,1,1,64,1792]{4,3,0,2,1:T(8,128)} async-done(((f32[2,4,1,64,1792]{4,3,0,2,1:T(8,128)}), f32[2,1,1,64,1792]{4,3,0,2,1:T(8,128)}) %reduce-scatter.9.cloned.1.call-update) | async-done | bytes 917520 | tf_op jit(solution)/shard_map/reduce_scatter | solution.py:78
  88.8 5.4 copy_subtract_fusion.6
  100.0 19.5 %collective-permute-done.1 = f32[2,1,64,1792]{3,2,0,1:T(8,128)S(1)} collective-permute-done((f32[2,1,64,1792]{3,2,0,1:T(8,128)S(1)}, f32[2,1,64,1792]{3,2,0,1:T(8,128)S(1)}, u32[]{:S(2)}, u32[]{:S(2)}) %collective-permute-start.1) | collective-permute-done | bytes 917536 | tf_op jit(solution)/shard_map/ppermute | solution.py:41
  119.5 43.6 %reduce-scatter.11.cloned.1.call-done = f32[2,1,1,64,1792]{4,3,0,2,1:T(8,128)} async-done(((f32[2,4,1,64,1792]{4,3,0,2,1:T(8,128)}), f32[2,1,1,64,1792]{4,3,0,2,1:T(8,128)}) %reduce-scatter.11.cloned.1.call-update) | async-done | bytes 917520 | tf_op jit(solution)/shard_map/reduce_scatter | solution.py:78
  165.6 13.8 %collective-permute-done.2 = f32[2,1,64,1792]{3,2,0,1:T(8,128)} collective-permute-done((f32[2,1,64,1792]{3,2,0,1:T(8,128)S(1)}, f32[2,1,64,1792]{3,2,0,1:T(8,128)}, u32[]{:S(2)}, u32[]{:S(2)}) %collective-permute-start.2) | collective-permute-done | bytes 917536 | tf_op jit(solution)/shard_map/ppermute | solution.py:41
  179.4 58.4 %all-gather.17.cloned.1.call-done = f32[2,4,64,1792]{3,2,0,1:T(8,128)} async-done(((f32[2,1,64,1792]{3,2,0,1:T(8,128)}), f32[2,4,64,1792]{3,2,0,1:T(8,128)}) %all-gather.17.cloned.1.call-update) | async-done | bytes 3670032 | tf_op jit(solution)/shard_map/all_gather | solution.py:93
  237.8 5.4 copy_subtract_fusion.5
  246.8 63.8 %all-gather.19.cloned.1.call-done = f32[2,4,64,1792]{3,2,0,1:T(8,128)} async-done(((f32[2,1,64,1792]{3,2,0,1:T(8,128)}), f32[2,4,64,1792]{3,2,0,1:T(8,128)}) %all-gather.19.cloned.1.call-update) | async-done | bytes 3670032 | tf_op jit(solution)/shard_map/all_gather | solution.py:93
  314.7 65.6 %reduce-scatter.13.cloned.1.call-done = f32[2,1,1,64,1792]{4,3,0,2,1:T(8,128)} async-done(((f32[2,4,1,64,1792]{4,3,0,2,1:T(8,128)}), f32[2,1,1,64,1792]{4,3,0,2,1:T(8,128)}) %reduce-scatter.13.cloned.1.call-update) | async-done | bytes 917520 | tf_op jit(solution)/shard_map/reduce_scatter | solution.py:78
  382.6 5.4 copy_subtract_fusion.4
  392.9 20.5 %collective-permute-done.5 = f32[2,1,64,1792]{3,2,0,1:T(8,128)S(1)} collective-permute-done((f32[2,1,64,1792]{3,2,0,1:T(8,128)S(1)}, f32[2,1,64,1792]{3,2,0,1:T(8,128)S(1)}, u32[]{:S(2)}, u32[]{:S(2)}) %collective-permute-start.5) | collective-permute-done | bytes 917536 | tf_op jit(solution)/shard_map/ppermute | solution.py:41
  413.4 43.6 %reduce-scatter.15.cloned.1.call-done = f32[2,1,1,64,1792]{4,3,0,2,1:T(8,128)} async-done(((f32[2,4,1,64,1792]{4,3,0,2,1:T(8,128)}), f32[2,1,1,64,1792]{4,3,0,2,1:T(8,128)}) %reduce-scatter.15.cloned.1.call-update) | async-done | bytes 917520 | tf_op jit(solution)/shard_map/reduce_scatter | solution.py:78
  460.2 70.9 %all-gather.21.cloned.1.call-done = f32[2,4,64,1792]{3,2,0,1:T(8,128)} async-done(((f32[2,1,64,1792]{3,2,0,1:T(8,128)}), f32[2,4,64,1792]{3,2,0,1:T(8,128)}) %all-gather.21.cloned.1.call-update) | async-done | bytes 3670032 | tf_op jit(solution)/shard_map/all_gather | solution.py:93
  535.3 6.0 copy_subtract_fusion.3
  544.8 5.5 copy_dynamic-update-slice_fusion
  550.3 53.2 %all-gather.23.cloned.1.call-done = f32[2,4,64,1792]{3,2,0,1:T(8,128)} async-done(((f32[2,1,64,1792]{3,2,0,1:T(8,128)}), f32[2,4,64,1792]{3,2,0,1:T(8,128)}) %all-gather.23.cloned.1.call-update) | async-done | bytes 3670032 | tf_op jit(solution)/shard_map/all_gather | solution.py:93
  607.5 65.3 %reduce-scatter.17.cloned.1.call-done = f32[2,1,1,64,1792]{4,3,0,2,1:T(8,128)} async-done(((f32[2,4,1,64,1792]{4,3,0,2,1:T(8,128)}), f32[2,1,1,64,1792]{4,3,0,2,1:T(8,128)}) %reduce-scatter.17.cloned.1.call-update) | async-done | bytes 917520 | tf_op jit(solution)/shard_map/reduce_scatter | solution.py:78
  675.1 6.8 constant_dynamic-slice_fusion.6
  691.2 21.3 %collective-permute-done.9 = f32[2,1,64,1792]{3,2,0,1:T(8,128)S(1)} collective-permute-done((f32[2,1,64,1792]{3,2,0,1:T(8,128)S(1)}, f32[2,1,64,1792]{3,2,0,1:T(8,128)S(1)}, u32[]{:S(2)}, u32[]{:S(2)}) %collective-permute-start.9) | collective-permute-done | bytes 917536 | tf_op jit(solution)/shard_map/ppermute | solution.py:41
  712.5 42.8 %reduce-scatter.19.cloned.1.call-done = f32[2,1,1,64,1792]{4,3,0,2,1:T(8,128)} async-done(((f32[2,4,1,64,1792]{4,3,0,2,1:T(8,128)}), f32[2,1,1,64,1792]{4,3,0,2,1:T(8,128)}) %reduce-scatter.19.cloned.1.call-update) | async-done | bytes 917520 | tf_op jit(solution)/shard_map/reduce_scatter | solution.py:78
  758.5 70.9 %all-gather.25.cloned.1.call-done = f32[2,4,64,1792]{3,2,0,1:T(8,128)} async-done(((f32[2,1,64,1792]{3,2,0,1:T(8,128)}), f32[2,4,64,1792]{3,2,0,1:T(8,128)}) %all-gather.25.cloned.1.call-update) | async-done | bytes 3670032 | tf_op jit(solution)/shard_map/all_gather | solution.py:93
  833.6 7.7 constant_dynamic-slice_fusion.4
  849.3 52.3 %all-gather.27.cloned.1.call-done = f32[2,4,64,1792]{3,2,0,1:T(8,128)} async-done(((f32[2,1,64,1792]{3,2,0,1:T(8,128)}), f32[2,4,64,1792]{3,2,0,1:T(8,128)}) %all-gather.27.cloned.1.call-update) | async-done | bytes 3670032 | tf_op jit(solution)/shard_map/all_gather | solution.py:93
  905.8 65.8 %reduce-scatter.21.cloned.1.call-done = f32[2,1,1,64,1792]{4,3,0,2,1:T(8,128)} async-done(((f32[2,4,1,64,1792]{4,3,0,2,1:T(8,128)}), f32[2,1,1,64,1792]{4,3,0,2,1:T(8,128)}) %reduce-scatter.21.cloned.1.call-update) | async-done | bytes 917520 | tf_op jit(solution)/shard_map/reduce_scatter | solution.py:78
  973.8 6.8 constant_dynamic-slice_fusion.1
  985.8 68.3 %reduce-scatter.23.cloned.1.call-done = f32[2,1,1,64,1792]{4,3,0,2,1:T(8,128)} async-done(((f32[2,4,1,64,1792]{4,3,0,2,1:T(8,128)}), f32[2,1,1,64,1792]{4,3,0,2,1:T(8,128)}) %reduce-scatter.23.cloned.1.call-update) | async-done | bytes 917520 | tf_op jit(solution)/shard_map/reduce_scatter | solution.py:78
  1067.1 4.5 subtract_dynamic-update-slice_fusion.1
  1073.8 4.5 subtract_dynamic-update-slice_fusion
  1078.2 49.8 %all-gather.29.cloned.1.call-done = f32[2,4,64,1792]{3,2,1,0:T(8,128)} async-done(((f32[2,1,64,1792]{3,2,1,0:T(8,128)}), f32[2,4,64,1792]{3,2,1,0:T(8,128)}) %all-gather.29.cloned.1.call-update) | async-done | bytes 3670032 | tf_op jit(solution)/shard_map/all_gather | solution.py:93
  1136.0 64.2 %all-gather.31.cloned.1.call-done = f32[2,4,64,1792]{3,2,1,0:T(8,128)} async-done(((f32[2,1,64,1792]{3,2,1,0:T(8,128)}), f32[2,4,64,1792]{3,2,1,0:T(8,128)}) %all-gather.31.cloned.1.call-update) | async-done | bytes 3670032 | tf_op jit(solution)/shard_map/all_gather | solution.py:93
  1200.2 5.4 fusion.1
  (112 shorter events, 114.3 us)
Async XLA Ops:
  7.2 79.3 %reduce-scatter.9.cloned.1.call-start = ((), (), s32[]{:S(2)}) async-start(), calls=%async_computation.8 | async-start | bytes 4587520 | tf_op jit(solution)/shard_map/reduce_scatter | solution.py:78
  15.2 147.9 %reduce-scatter.11.cloned.1.call-start = ((), (), s32[]{:S(2)}) async-start(), calls=%async_computation.9 | async-start | bytes 4587520 | tf_op jit(solution)/shard_map/reduce_scatter | solution.py:78
  16.5 14.3 %collective-permute-start = (f32[2,1,64,1792]{3,2,0,1:T(8,128)S(1)}, f32[2,1,64,1792]{3,2,0,1:T(8,128)S(1)}, u32[]{:S(2)}, u32[]{:S(2)}) collective-permute-start(f32[2,1,64,1792]{3,2,0,1:T(8,128)S(1)} %dynamic-slice_bitcast_fusion.5), channel_id=1, source_target_pairs={{0,7},{1,0},{2,1},{3,2},{4,3},{5,4},{6,5},{7,6},{8,15},{9,8},{10,9... | collective-permute-start | bytes 2752520 | tf_op jit(solution)/shard_map/ppermute | solution.py:41
  94.2 143.6 %all-gather.17.cloned.1.call-start = ((), (), s32[]{:S(2)}) async-start(), calls=%async_computation.16 | async-start | bytes 4587520 | tf_op jit(solution)/shard_map/all_gather | solution.py:93
  94.9 215.6 %all-gather.19.cloned.1.call-start = ((), (), s32[]{:S(2)}) async-start(), calls=%async_computation.17 | async-start | bytes 4587520 | tf_op jit(solution)/shard_map/all_gather | solution.py:93
  97.6 21.9 %collective-permute-start.1 = (f32[2,1,64,1792]{3,2,0,1:T(8,128)S(1)}, f32[2,1,64,1792]{3,2,0,1:T(8,128)S(1)}, u32[]{:S(2)}, u32[]{:S(2)}) collective-permute-start(f32[2,1,64,1792]{3,2,0,1:T(8,128)S(1)} %get-tuple-element.61), channel_id=1, source_target_pairs={{0,6},{1,7},{2,0},{3,1},{4,2},{5,3},{6,4},{7,5},{8,14},{9,15},{10,... | collective-permute-start | bytes 2752520 | tf_op jit(solution)/shard_map/ppermute | solution.py:41
  165.5 214.9 %reduce-scatter.13.cloned.1.call-start = ((), (), s32[]{:S(2)}) async-start(), calls=%async_computation.10 | async-start | bytes 4587520 | tf_op jit(solution)/shard_map/reduce_scatter | solution.py:78
  165.5 13.9 %collective-permute-start.2 = (f32[2,1,64,1792]{3,2,0,1:T(8,128)S(1)}, f32[2,1,64,1792]{3,2,0,1:T(8,128)}, u32[]{:S(2)}, u32[]{:S(2)}) collective-permute-start(f32[2,1,64,1792]{3,2,0,1:T(8,128)S(1)} %get-tuple-element.74), channel_id=1, source_target_pairs={{0,1},{1,2},{2,3},{3,4},{4,5},{5,6},{6,7},{7,0},{8,9},{9,10},{10,1... | collective-permute-start | bytes 2752520 | tf_op jit(solution)/shard_map/ppermute | solution.py:41
  243.3 213.8 %reduce-scatter.15.cloned.1.call-start = ((), (), s32[]{:S(2)}) async-start(), calls=%async_computation.11 | async-start | bytes 4587520 | tf_op jit(solution)/shard_map/reduce_scatter | solution.py:78
  244.4 70.3 %collective-permute-start.3 = (f32[2,1,64,1792]{3,2,0,1:T(8,128)S(1)}, f32[2,1,64,1792]{3,2,0,1:T(8,128)S(1)}, u32[]{:S(2)}, u32[]{:S(2)}) collective-permute-start(f32[2,1,64,1792]{3,2,0,1:T(8,128)S(1)} %copy-done.11), channel_id=1, source_target_pairs={{0,5},{1,6},{2,7},{3,0},{4,1},{5,2},{6,3},{7,4},{8,13},{9,14},{10,... | collective-permute-start | bytes 2752520 | tf_op jit(solution)/shard_map/ppermute | solution.py:41
  245.3 137.3 %collective-permute-start.4 = (f32[2,1,64,1792]{3,2,0,1:T(8,128)S(1)}, f32[2,1,64,1792]{3,2,0,1:T(8,128)}, u32[]{:S(2)}, u32[]{:S(2)}) collective-permute-start(f32[2,1,64,1792]{3,2,0,1:T(8,128)S(1)} %get-tuple-element.72), channel_id=1, source_target_pairs={{0,2},{1,3},{2,4},{3,5},{4,6},{5,7},{6,0},{7,1},{8,10},{9,11},{10,... | collective-permute-start | bytes 2752520 | tf_op jit(solution)/shard_map/ppermute | solution.py:41
  388.1 143.0 %all-gather.21.cloned.1.call-start = ((), (), s32[]{:S(2)}) async-start(), calls=%async_computation.18 | async-start | bytes 4587520 | tf_op jit(solution)/shard_map/all_gather | solution.py:93
  388.8 214.6 %all-gather.23.cloned.1.call-start = ((), (), s32[]{:S(2)}) async-start(), calls=%async_computation.19 | async-start | bytes 4587520 | tf_op jit(solution)/shard_map/all_gather | solution.py:93
  391.5 21.9 %collective-permute-start.5 = (f32[2,1,64,1792]{3,2,0,1:T(8,128)S(1)}, f32[2,1,64,1792]{3,2,0,1:T(8,128)S(1)}, u32[]{:S(2)}, u32[]{:S(2)}) collective-permute-start(f32[2,1,64,1792]{3,2,0,1:T(8,128)S(1)} %get-tuple-element.59), channel_id=1, source_target_pairs={{0,4},{1,5},{2,6},{3,7},{4,0},{5,1},{6,2},{7,3},{8,12},{9,13},{10,... | collective-permute-start | bytes 2752520 | tf_op jit(solution)/shard_map/ppermute | solution.py:41
  459.4 213.5 %reduce-scatter.17.cloned.1.call-start = ((), (), s32[]{:S(2)}) async-start(), calls=%async_computation.12 | async-start | bytes 4587520 | tf_op jit(solution)/shard_map/reduce_scatter | solution.py:78
  459.4 75.9 %collective-permute-start.6 = (f32[2,1,64,1792]{3,2,0,1:T(8,128)S(1)}, f32[2,1,64,1792]{3,2,0,1:T(8,128)S(1)}, u32[]{:S(2)}, u32[]{:S(2)}) collective-permute-start(f32[2,1,64,1792]{3,2,0,1:T(8,128)S(1)} %get-tuple-element.70), channel_id=1, source_target_pairs={{0,3},{1,4},{2,5},{3,6},{4,7},{5,0},{6,1},{7,2},{8,11},{9,12},{10,... | collective-permute-start | bytes 2752520 | tf_op jit(solution)/shard_map/ppermute | solution.py:41
  541.4 214.0 %reduce-scatter.19.cloned.1.call-start = ((), (), s32[]{:S(2)}) async-start(), calls=%async_computation.13 | async-start | bytes 4587520 | tf_op jit(solution)/shard_map/reduce_scatter | solution.py:78
  542.5 65.0 %collective-permute-start.7 = (f32[2,1,64,1792]{3,2,0,1:T(8,128)S(1)}, f32[2,1,64,1792]{3,2,0,1:T(8,128)S(1)}, u32[]{:S(2)}, u32[]{:S(2)}) collective-permute-start(f32[2,1,64,1792]{3,2,0,1:T(8,128)S(1)} %copy-done.10), channel_id=1, source_target_pairs={{0,3},{1,4},{2,5},{3,6},{4,7},{5,0},{6,1},{7,2},{8,11},{9,12},{10,... | collective-permute-start | bytes 2752520 | tf_op jit(solution)/shard_map/ppermute | solution.py:41
  543.3 131.8 %collective-permute-start.8 = (f32[2,1,64,1792]{3,2,0,1:T(8,128)S(1)}, f32[2,1,64,1792]{3,2,0,1:T(8,128)}, u32[]{:S(2)}, u32[]{:S(2)}) collective-permute-start(f32[2,1,64,1792]{3,2,0,1:T(8,128)S(1)} %get-tuple-element.68), channel_id=1, source_target_pairs={{0,4},{1,5},{2,6},{3,7},{4,0},{5,1},{6,2},{7,3},{8,12},{9,13},{10,... | collective-permute-start | bytes 2752520 | tf_op jit(solution)/shard_map/ppermute | solution.py:41
  686.4 143.0 %all-gather.25.cloned.1.call-start = ((), (), s32[]{:S(2)}) async-start(), calls=%async_computation.20 | async-start | bytes 4587520 | tf_op jit(solution)/shard_map/all_gather | solution.py:93
  687.2 214.5 %all-gather.27.cloned.1.call-start = ((), (), s32[]{:S(2)}) async-start(), calls=%async_computation.21 | async-start | bytes 4587520 | tf_op jit(solution)/shard_map/all_gather | solution.py:93
  689.7 22.8 %collective-permute-start.9 = (f32[2,1,64,1792]{3,2,0,1:T(8,128)S(1)}, f32[2,1,64,1792]{3,2,0,1:T(8,128)S(1)}, u32[]{:S(2)}, u32[]{:S(2)}) collective-permute-start(f32[2,1,64,1792]{3,2,0,1:T(8,128)S(1)} %get-tuple-element.57), channel_id=1, source_target_pairs={{0,2},{1,3},{2,4},{3,5},{4,6},{5,7},{6,0},{7,1},{8,10},{9,11},{10,... | collective-permute-start | bytes 2752520 | tf_op jit(solution)/shard_map/ppermute | solution.py:41
  757.7 213.9 %reduce-scatter.21.cloned.1.call-start = ((), (), s32[]{:S(2)}) async-start(), calls=%async_computation.14 | async-start | bytes 4587520 | tf_op jit(solution)/shard_map/reduce_scatter | solution.py:78
  757.7 75.8 %collective-permute-start.10 = (f32[2,1,64,1792]{3,2,0,1:T(8,128)S(1)}, f32[2,1,64,1792]{3,2,0,1:T(8,128)S(1)}, u32[]{:S(2)}, u32[]{:S(2)}) collective-permute-start(f32[2,1,64,1792]{3,2,0,1:T(8,128)S(1)} %get-tuple-element.66), channel_id=1, source_target_pairs={{0,5},{1,6},{2,7},{3,0},{4,1},{5,2},{6,3},{7,4},{8,13},{9,14},{10,... | collective-permute-start | bytes 2752520 | tf_op jit(solution)/shard_map/ppermute | solution.py:41
  845.7 208.3 %reduce-scatter.23.cloned.1.call-start = ((), (), s32[]{:S(2)}) async-start(), calls=%async_computation.15 | async-start | bytes 4587520 | tf_op jit(solution)/shard_map/reduce_scatter | solution.py:78
  846.9 58.9 %collective-permute-start.11 = (f32[2,1,64,1792]{3,2,1,0:T(8,128)S(1)}, f32[2,1,64,1792]{3,2,1,0:T(8,128)S(1)}, u32[]{:S(2)}, u32[]{:S(2)}) collective-permute-start(f32[2,1,64,1792]{3,2,1,0:T(8,128)S(1)} %copy-done.9), channel_id=1, source_target_pairs={{0,1},{1,2},{2,3},{3,4},{4,5},{5,6},{6,7},{7,0},{8,9},{9,10},{10,1... | collective-permute-start | bytes 2752520 | tf_op jit(solution)/shard_map/ppermute | solution.py:41
  846.9 126.9 %collective-permute-start.12 = (f32[2,1,64,1792]{3,2,0,1:T(8,128)S(1)}, f32[2,1,64,1792]{3,2,0,1:T(8,128)}, u32[]{:S(2)}, u32[]{:S(2)}) collective-permute-start(f32[2,1,64,1792]{3,2,0,1:T(8,128)S(1)} %get-tuple-element.64), channel_id=1, source_target_pairs={{0,6},{1,7},{2,0},{3,1},{4,2},{5,3},{6,4},{7,5},{8,14},{9,15},{10,... | collective-permute-start | bytes 2752520 | tf_op jit(solution)/shard_map/ppermute | solution.py:41
  985.1 142.9 %all-gather.29.cloned.1.call-start = ((), (), s32[]{:S(2)}) async-start(), calls=%async_computation.22 | async-start | bytes 4587520 | tf_op jit(solution)/shard_map/all_gather | solution.py:93
  985.7 214.5 %all-gather.31.cloned.1.call-start = ((), (), s32[]{:S(2)}) async-start(), calls=%async_computation.23 | async-start | bytes 4587520 | tf_op jit(solution)/shard_map/all_gather | solution.py:93
  985.8 75.4 %copy-start.6 = (f32[2,1,64,1792]{3,2,0,1:T(8,128)S(1)}, f32[2,1,64,1792]{3,2,0,1:T(8,128)}, u32[]{:S(2)}) copy-start(f32[2,1,64,1792]{3,2,0,1:T(8,128)} %copy-done.5) | copy-start | bytes 2752516
  1065.4 12.8 %collective-permute-start.13 = (f32[2,1,64,1792]{3,2,1,0:T(8,128)S(1)}, f32[2,1,64,1792]{3,2,1,0:T(8,128)S(1)}, u32[]{:S(2)}, u32[]{:S(2)}) collective-permute-start(f32[2,1,64,1792]{3,2,1,0:T(8,128)S(1)} %get-tuple-element.62), channel_id=1, source_target_pairs={{0,7},{1,0},{2,1},{3,2},{4,3},{5,4},{6,5},{7,6},{8,15},{9,8},{10,9... | collective-permute-start | bytes 2752520 | tf_op jit(solution)/shard_map/ppermute | solution.py:41
  1073.8 55.2 %copy-start.4 = (f32[2,1,1,64,1792]{4,3,0,2,1:T(8,128)S(1)}, f32[2,1,1,64,1792]{4,3,0,2,1:T(8,128)}, u32[]{:S(2)}) copy-start(f32[2,1,1,64,1792]{4,3,0,2,1:T(8,128)} %reduce-scatter.23.cloned.1.call-done) | copy-start | bytes 2752516
  (10 other events, 45.4 us)
Sparse Core Ops, SparseCore 0:
  15.3 71.1 reduce-scatter.8
  94.3 68.7 reduce-scatter.10
  165.3 72.4 all-gather.16
  239.8 70.7 all-gather.18
  313.3 67.0 reduce-scatter.12
  388.2 68.7 reduce-scatter.14
  458.6 72.4 all-gather.20
  532.7 70.7 all-gather.22
  605.7 67.0 reduce-scatter.16
  686.5 68.7 reduce-scatter.18
  756.9 72.4 all-gather.24
  830.9 70.7 all-gather.26
  904.5 67.0 reduce-scatter.20
  985.2 68.7 reduce-scatter.22
  1055.5 72.4 all-gather.28
  1129.4 70.7 all-gather.30

commit v4 on v3

--- a/solution.py
+++ b/solution.py
@@ -24,6 +24,7 @@
 def body(inner_weights, start_weights, momentum):
     groups = lax.axis_size("grp")
     plane = lax.axis_size("shard") * lax.axis_size("tp")
+    group = lax.axis_index("grp")
     place = lax.axis_index(("shard", "tp"))
     row_count, col_count = start_weights.shape[1:]
     q_rows = row_count // (groups * plane)
@@ -61,38 +62,69 @@
             array = lax.dynamic_update_slice_in_dim(array, part, lax.rem(place + plane - s, plane), 1)
         return array
 
-    def spread(array, step, update):
+    def spread(array, matrix, step, owner, update):
         for m, s in enumerate(shifts_of(step)):
-            at = (0, 0, lax.rem(place + s, plane), 0, 0)
-            old = lax.dynamic_slice(start, at, (2, groups, 1) + block)
-            array = lax.dynamic_update_slice(array, old - update[:, :, m : m + 1], at)
+            at = (matrix, owner, lax.rem(place + s, plane), 0, 0)
+            old = lax.dynamic_slice(start, at, (1, 1, 1) + block)
+            array = lax.dynamic_update_slice(array, old - update[m][None, None, None], at)
         return array
+
+    def hop(number, to_right, to_left):
+        right = [(i, i + 1) for i in range(number, groups - 1)]
+        left = [(groups - 1 - i, groups - 2 - i) for i in range(number, groups - 1)]
+        if 2 * number >= groups:
+            came = lax.ppermute(jnp.where(group < groups - number, to_left, to_right), "grp", right + left)
+            return came, came
+        return lax.ppermute(to_right, "grp", right), lax.ppermute(to_left, "grp", left)
+
+    def part_sum(step, place):
+        differ = rows_of(start, step, place) - rows_of(inner, step, place)
+        return lax.psum_scatter(differ, "grp", scatter_dimension=1, tiled=True)[:, 0]
 
     new_weights = blank(start.shape)
     new_held = blank(held.shape)
     order = [(turn + 1) % steps for turn in range(steps)]
-    now = place
-    moved, sent, gathered = [fetch(order[0], place)], [], []
+    depth = min(3, steps)
+    totals, now = [], place
+    for step in order[:depth]:
+        totals.append(part_sum(step, now))
+    moved = fetch(order[0], place)
+    sent = []
     for turn in range(steps):
         step = order[turn]
-        total = lax.psum_scatter(
-            rows_of(start, step, now) - rows_of(inner, step, now), "grp", scatter_dimension=1, tiled=True
-        )[:, 0]
+        mean_diff = totals[turn] / groups
+        new_momentum = MOMENTUM_COEF * join(moved, 1) + mean_diff
+        update = OUTER_RATE * (mean_diff + MOMENTUM_COEF * new_momentum)
+        chains = [(update[matrix], update[matrix]) for matrix in range(2)]
+        came = [[], []]
+        for number in range(groups - 1):
+            if number == 1:
+                now, *sent = after(came[0][0][0], place, *sent)
+                if sent:
+                    new_held = land(new_held, order[turn - 1], sent)
+                if turn + depth < steps:
+                    totals.append(part_sum(order[turn + depth], now))
+                if turn + 1 < steps:
+                    moved = fetch(order[turn + 1], now)
+            for matrix in range(2):
+                to_right, to_left = chains[matrix]
+                if number == groups - 2 and matrix == 0 and turn + 1 < steps:
+                    to_right, to_left, *moved = lax.optimization_barrier((to_right, to_left, *moved))
+                chains[matrix] = hop(number, to_right, to_left)
+                came[matrix].append(chains[matrix])
         if turn + 1 < steps:
-            moved.append(fetch(order[turn + 1], now))
-        mean_diff = total / groups
-        new_momentum = MOMENTUM_COEF * join(moved[turn], 1) + mean_diff
-        update = OUTER_RATE * (mean_diff + MOMENTUM_COEF * new_momentum)
-        if turn == 0:
-            (now,) = after(update, place)
-        else:
-            now, gathered[turn - 1], *sent[turn - 1] = after(update, place, gathered[turn - 1], *sent[turn - 1])
-            new_held = land(new_held, order[turn - 1], sent[turn - 1])
-            new_weights = spread(new_weights, order[turn - 1], gathered[turn - 1])
-        sent.append(deliver(step, new_momentum))
-        gathered.append(lax.all_gather(update[:, None], "grp", axis=1, tiled=True))
-    new_held = land(new_held, order[-1], sent[-1])
-    new_weights = spread(new_weights, order[-1], gathered[-1])
+            last = came[1][groups - 3]
+            (totals[turn + 1],) = after(last[0], totals[turn + 1])
+            (new_momentum,) = after(last[1], new_momentum)
+        sent = deliver(step, new_momentum)
+        for matrix in range(2):
+            new_weights = spread(new_weights, matrix, step, group, update[matrix])
+            for number in range(groups - 1):
+                from_left, from_right = came[matrix][number][0], came[matrix][groups - 2 - number][1]
+                part = jnp.where(group > number, from_left, from_right)
+                owner = lax.rem(group + groups - 1 - number, groups)
+                new_weights = spread(new_weights, matrix, step, owner, part)
+    new_held = land(new_held, order[-1], sent)
     return (new_weights.reshape(start_weights.shape), new_held.reshape(momentum.shape))
 
 

time: 1210 us -> 1160 us (0.959)
  waiting for transfers between devices: 1020 us -> 676 us
  starting transfers between devices: 19.6 us -> 178 us
  other arithmetic: 105 us -> 198 us
  local copies, waits for them, and re-layouts: 50.6 us -> 82.3 us
    ppermute x0 -> x80, waiting for transfers between devices: none -> 584 us  [the longest x32 269 us: hop(): lax.ppermute(to_left, 'grp', left)]
    all_gather x8 -> x0, waiting for transfers between devices: 484 us -> none  [body(): gathered.append(lax.all_gather(update[:, None], 'grp', axis=1, tiled=True))]
    reduce_scatter x8, waiting for transfers between devices: 451 us -> 76.6 us  [part_sum(): lax.psum_scatter(differ, 'grp', scatter_dimension=1, tiled=True)[:, 0]]
    ppermute x0 -> x80, starting transfers between devices: none -> 159 us  [the longest x32 97 us: hop(): lax.ppermute(to_right, 'grp', right)]
    dynamic_update_slice x5 -> x64, other arithmetic: 24.2 us -> 123 us  [spread(): lax.dynamic_update_slice(array, old - update[m][None, None, None], at)]
    ppermute x14, waiting for transfers between devices: 86.1 us -> 15.3 us  [rotate(): lax.ppermute(part, ('shard', 'tp'), [(i, (i + shift) % plane) for i in ra...]
    dynamic_slice x1 -> x5, local copies, waits for them, and re-layouts: 3.89 us -> 44 us  [rows_of(): lax.dynamic_slice_in_dim(array, lax.rem(place + s, plane), 1, 2)]
    dynamic_slice x3 -> x0, other arithmetic: 21.4 us -> none  [rows_of(): lax.dynamic_slice_in_dim(array, lax.rem(place + s, plane), 1, 2)]
  transfers between devices with their start and end apart: 30 -> 102, of which waited for: 21 -> 41; matrix products, arithmetic and copies ran while one was open for 9% -> 20% of each run, Pallas kernels for 0% -> 0%
where the time goes in v4:
time: 1160 us; the launch traced here: 1150 us
  waiting for transfers between devices  676 us (58%)
  other arithmetic  198 us (17%)
  starting transfers between devices  178 us (15%)
  local copies, waits for them, and re-layouts  82.3 us (7%)
  between operations  15.2 us (1%)
    ppermute x32, waiting for transfers between devices, hop(): lax.ppermute(to_left, 'grp', left)  269 us
    ppermute x16, waiting for transfers between devices, hop(): lax.ppermute(jnp.where(group < groups - number, to_left, to_right), 'grp'...  244 us
    dynamic_update_slice x64, other arithmetic, spread(): lax.dynamic_update_slice(array, old - update[m][None, None, None], at)  123 us
    ppermute x32, starting transfers between devices, hop(): lax.ppermute(to_right, 'grp', right)  97 us
    reduce_scatter x8, waiting for transfers between devices, part_sum(): lax.psum_scatter(differ, 'grp', scatter_dimension=1, tiled=True)[:, 0]  76.6 us
    ppermute x32, waiting for transfers between devices, hop(): lax.ppermute(to_right, 'grp', right)  71.2 us
    dynamic_slice x5, local copies, waits for them, and re-layouts, rows_of(): lax.dynamic_slice_in_dim(array, lax.rem(place + s, plane), 1, 2)  44 us
    ppermute x32, starting transfers between devices, hop(): lax.ppermute(to_left, 'grp', left)  41.1 us
  transfers between devices with their start and end apart: 102, of which 41 were waited for; matrix products, arithmetic and copies ran while one was open for 20% of the time, Pallas kernels for 0%

profile of v4, /device:TPU:0, one launch (start us, length us, event | category | flops | bytes accessed | tf_op | source)
XLA Modules:
  0.0 1150.4 jit_solution(11007524097044034704)
XLA Ops:
  7.2 10.9 constant_dynamic-slice_fusion.18
  33.8 10.9 collective-permute-done
  44.7 50.2 %reduce-scatter.9.cloned.1.call-done = f32[2,1,1,64,1792]{4,3,0,2,1:T(8,128)} async-done(((f32[2,4,1,64,1792]{4,3,0,2,1:T(8,128)}), f32[2,1,1,64,1792]{4,3,0,2,1:T(8,128)}) %reduce-scatter.9.cloned.1.call-update) | async-done | bytes 917520 | tf_op jit(solution)/shard_map/reduce_scatter | solution.py:82
  108.4 10.2 collective-permute-done.1
  123.1 14.1 %collective-permute-done.7 = f32[1,64,1792]{2,1,0:T(8,128)} collective-permute-done((f32[1,64,1792]{2,1,0:T(8,128)S(1)}, f32[1,64,1792]{2,1,0:T(8,128)}, u32[]{:S(2)}, u32[]{:S(2)}) %collective-permute-start.7) | collective-permute-done | bytes 458784 | tf_op jit(solution)/shard_map/ppermute | solution.py:78
  138.0 25.9 %collective-permute-done.8 = f32[1,64,1792]{2,1,0:T(8,128)} collective-permute-done((f32[1,64,1792]{2,1,0:T(8,128)S(1)}, f32[1,64,1792]{2,1,0:T(8,128)}, u32[]{:S(2)}, u32[]{:S(2)}) %collective-permute-start.8) | collective-permute-done | bytes 458784 | tf_op jit(solution)/shard_map/ppermute | solution.py:78
  167.2 26.4 %reduce-scatter.11.cloned.1.call-done = f32[2,1,1,64,1792]{4,3,0,2,1:T(8,128)} async-done(((f32[2,4,1,64,1792]{4,3,0,2,1:T(8,128)}), f32[2,1,1,64,1792]{4,3,0,2,1:T(8,128)}) %reduce-scatter.11.cloned.1.call-update) | async-done | bytes 917520 | tf_op jit(solution)/shard_map/reduce_scatter | solution.py:82
  194.8 8.3 collective-permute-done.4
  211.2 8.4 collective-permute-done.12
  219.6 8.3 constant_dynamic-slice_fusion.6
  227.9 8.3 constant_dynamic-slice_fusion.7
  259.5 55.9 %collective-permute-done.20 = f32[1,64,1792]{2,1,0:T(8,128)S(1)} collective-permute-done((f32[1,64,1792]{2,1,0:T(8,128)S(1)}, f32[1,64,1792]{2,1,0:T(8,128)S(1)}, u32[]{:S(2)}, u32[]{:S(2)}) %collective-permute-start.20) | collective-permute-done | bytes 458784 | tf_op jit(solution)/shard_map/ppermute | solution.py:78
  319.5 16.5 %collective-permute-done.21 = f32[1,64,1792]{2,1,0:T(8,128)S(1)} collective-permute-done((f32[1,64,1792]{2,1,0:T(8,128)S(1)}, f32[1,64,1792]{2,1,0:T(8,128)S(1)}, u32[]{:S(2)}, u32[]{:S(2)}) %collective-permute-start.21) | collective-permute-done | bytes 458784 | tf_op jit(solution)/shard_map/ppermute | solution.py:78
  337.1 23.7 %collective-permute-done.15 = f32[1,64,1792]{2,1,0:T(8,128)S(1)} collective-permute-done((f32[1,64,1792]{2,1,0:T(8,128)S(1)}, f32[1,64,1792]{2,1,0:T(8,128)S(1)}, u32[]{:S(2)}, u32[]{:S(2)}) %collective-permute-start.15) | collective-permute-done | bytes 458784 | tf_op jit(solution)/shard_map/ppermute | solution.py:78
  381.5 12.5 %collective-permute-done.24 = f32[1,64,1792]{2,1,0:T(8,128)} collective-permute-done((f32[1,64,1792]{2,1,0:T(8,128)}, f32[1,64,1792]{2,1,0:T(8,128)}, u32[]{:S(2)}, u32[]{:S(2)}) %collective-permute-start.24) | collective-permute-done | bytes 458784 | tf_op jit(solution)/shard_map/ppermute | solution.py:78
  407.9 17.6 %collective-permute-done.32 = f32[1,64,1792]{2,1,0:T(8,128)} collective-permute-done((f32[1,64,1792]{2,1,0:T(8,128)}, f32[1,64,1792]{2,1,0:T(8,128)}, u32[]{:S(2)}, u32[]{:S(2)}) %collective-permute-start.32) | collective-permute-done | bytes 458784 | tf_op jit(solution)/shard_map/ppermute | solution.py:78
  431.5 51.8 %collective-permute-done.33 = f32[1,64,1792]{2,1,0:T(8,128)} collective-permute-done((f32[1,64,1792]{2,1,0:T(8,128)}, f32[1,64,1792]{2,1,0:T(8,128)}, u32[]{:S(2)}, u32[]{:S(2)}) %collective-permute-start.33) | collective-permute-done | bytes 458784 | tf_op jit(solution)/shard_map/ppermute | solution.py:78
  498.8 11.6 %collective-permute-done.36 = f32[1,64,1792]{2,1,0:T(8,128)} collective-permute-done((f32[1,64,1792]{2,1,0:T(8,128)}, f32[1,64,1792]{2,1,0:T(8,128)}, u32[]{:S(2)}, u32[]{:S(2)}) %collective-permute-start.36) | collective-permute-done | bytes 458784 | tf_op jit(solution)/shard_map/ppermute | solution.py:78
  538.4 14.5 %collective-permute-done.45 = f32[1,64,1792]{2,1,0:T(8,128)} collective-permute-done((f32[1,64,1792]{2,1,0:T(8,128)}, f32[1,64,1792]{2,1,0:T(8,128)}, u32[]{:S(2)}, u32[]{:S(2)}) %collective-permute-start.45) | collective-permute-done | bytes 458784 | tf_op jit(solution)/shard_map/ppermute | solution.py:78
  576.6 8.3 constant_dynamic-slice_fusion.3
  584.9 8.2 constant_dynamic-slice_fusion.4
  612.4 38.6 %collective-permute-done.18 = f32[1,64,1792]{2,1,0:T(8,128)S(1)} collective-permute-done((f32[1,64,1792]{2,1,0:T(8,128)S(1)}, f32[1,64,1792]{2,1,0:T(8,128)S(1)}, u32[]{:S(2)}, u32[]{:S(2)}) %collective-permute-start.18) | collective-permute-done | bytes 458784 | tf_op jit(solution)/shard_map/ppermute | solution.py:76
  658.7 19.3 %collective-permute-done.23 = f32[1,64,1792]{2,1,0:T(8,128)S(1)} collective-permute-done((f32[1,64,1792]{2,1,0:T(8,128)S(1)}, f32[1,64,1792]{2,1,0:T(8,128)S(1)}, u32[]{:S(2)}, u32[]{:S(2)}) %collective-permute-start.23) | collective-permute-done | bytes 458784 | tf_op jit(solution)/shard_map/ppermute | solution.py:76
  700.4 37.3 %collective-permute-done.30 = f32[1,64,1792]{2,1,0:T(8,128)S(1)} collective-permute-done((f32[1,64,1792]{2,1,0:T(8,128)S(1)}, f32[1,64,1792]{2,1,0:T(8,128)S(1)}, u32[]{:S(2)}, u32[]{:S(2)}) %collective-permute-start.30) | collective-permute-done | bytes 458784 | tf_op jit(solution)/shard_map/ppermute | solution.py:76
  745.4 21.4 %collective-permute-done.35 = f32[1,64,1792]{2,1,0:T(8,128)S(1)} collective-permute-done((f32[1,64,1792]{2,1,0:T(8,128)S(1)}, f32[1,64,1792]{2,1,0:T(8,128)S(1)}, u32[]{:S(2)}, u32[]{:S(2)}) %collective-permute-start.35) | collective-permute-done | bytes 458784 | tf_op jit(solution)/shard_map/ppermute | solution.py:76
  798.3 63.0 %collective-permute-done.42 = f32[1,64,1792]{2,1,0:T(8,128)S(1)} collective-permute-done((f32[1,64,1792]{2,1,0:T(8,128)}, f32[1,64,1792]{2,1,0:T(8,128)S(1)}, u32[]{:S(2)}, u32[]{:S(2)}) %collective-permute-start.42) | collective-permute-done | bytes 458784 | tf_op jit(solution)/shard_map/ppermute | solution.py:76
  903.6 8.4 collective-permute-done.54
  997.1 19.5 %collective-permute-done.66 = f32[1,64,1792]{2,1,0:T(8,128)} collective-permute-done((f32[1,64,1792]{2,1,0:T(8,128)}, f32[1,64,1792]{2,1,0:T(8,128)}, u32[]{:S(2)}, u32[]{:S(2)}) %collective-permute-start.66) | collective-permute-done | bytes 458784 | tf_op jit(solution)/shard_map/ppermute | solution.py:76
  1039.1 9.2 collective-permute-start.83
  1059.0 22.3 %collective-permute-done.77 = f32[1,64,1792]{2,1,0:T(8,128)S(1)} collective-permute-done((f32[1,64,1792]{2,1,0:T(8,128)S(1)}, f32[1,64,1792]{2,1,0:T(8,128)S(1)}, u32[]{:S(2)}, u32[]{:S(2)}) %collective-permute-start.77) | collective-permute-done | bytes 458784 | tf_op jit(solution)/shard_map/ppermute | solution.py:76
  1110.3 8.5 collective-permute-done.90
  1120.1 8.8 collective-permute-done.87
  (351 shorter events, 476.4 us)
Async XLA Ops:
  7.2 87.7 %reduce-scatter.9.cloned.1.call-start = ((), (), s32[]{:S(2)}) async-start(), calls=%async_computation.8 | async-start | bytes 4587520 | tf_op jit(solution)/shard_map/reduce_scatter | solution.py:82
  23.6 169.9 %reduce-scatter.11.cloned.1.call-start = ((), (), s32[]{:S(2)}) async-start(), calls=%async_computation.9 | async-start | bytes 4587520 | tf_op jit(solution)/shard_map/reduce_scatter | solution.py:82
  29.1 333.4 %reduce-scatter.13.cloned.1.call-start = ((), (), s32[]{:S(2)}) async-start(), calls=%async_computation.10 | async-start | bytes 4587520 | tf_op jit(solution)/shard_map/reduce_scatter | solution.py:82
  100.5 65.4 %collective-permute-start.3 = (f32[1,64,1792]{2,1,0:T(8,128)S(1)}, f32[1,64,1792]{2,1,0:T(8,128)}, u32[]{:S(2)}, u32[]{:S(2)}) collective-permute-start(f32[1,64,1792]{2,1,0:T(8,128)S(1)} %get-tuple-element.149), channel_id=1, source_target_pairs={{24,16},{16,8},{8,0},{25,17},{17,9},{9,1},{26,18},{18,10},{10,2},{... | collective-permute-start | bytes 1376264 | tf_op jit(solution)/shard_map/ppermute | solution.py:78
  107.2 56.7 %collective-permute-start.8 = (f32[1,64,1792]{2,1,0:T(8,128)S(1)}, f32[1,64,1792]{2,1,0:T(8,128)}, u32[]{:S(2)}, u32[]{:S(2)}) collective-permute-start(f32[1,64,1792]{2,1,0:T(8,128)S(1)} %get-tuple-element.148), channel_id=1, source_target_pairs={{24,16},{16,8},{8,0},{25,17},{17,9},{9,1},{26,18},{18,10},{10,2},{... | collective-permute-start | bytes 1376264 | tf_op jit(solution)/shard_map/ppermute | solution.py:78
  121.0 82.1 %collective-permute-start.5 = (f32[2,1,64,1792]{3,2,1,0:T(8,128)}, f32[2,1,64,1792]{3,2,1,0:T(8,128)}, u32[]{:S(2)}, u32[]{:S(2)}) collective-permute-start(f32[2,1,64,1792]{3,2,1,0:T(8,128)} %constant_dynamic-slice_fusion.20), channel_id=1, source_target_pairs={{0,6},{1,7},{2,0},{3,1},{4,2},{5,3},{6,4},{7,5},{8,14},{9,15},{10,... | collective-permute-start | bytes 2752520 | tf_op jit(solution)/shard_map/ppermute | solution.py:42
  137.3 56.3 %collective-permute-start.10 = (f32[1,64,1792]{2,1,0:T(8,128)}, f32[1,64,1792]{2,1,0:T(8,128)S(1)}, u32[]{:S(2)}, u32[]{:S(2)}) collective-permute-start(f32[1,64,1792]{2,1,0:T(8,128)} %collective-permute-done.7), channel_id=1, source_target_pairs={{8,16},{16,24},{9,17},{17,25},{10,18},{18,26},{11,19},{19,27},{12,... | collective-permute-start | bytes 1376264 | tf_op jit(solution)/shard_map/ppermute | solution.py:78
  238.5 193.0 %reduce-scatter.15.cloned.1.call-start = ((), (), s32[]{:S(2)}) async-start(), calls=%async_computation.11 | async-start | bytes 4587520 | tf_op jit(solution)/shard_map/reduce_scatter | solution.py:82
  244.0 294.4 %reduce-scatter.17.cloned.1.call-start = ((), (), s32[]{:S(2)}) async-start(), calls=%async_computation.12 | async-start | bytes 4587520 | tf_op jit(solution)/shard_map/reduce_scatter | solution.py:82
  250.1 673.1 %reduce-scatter.19.cloned.1.call-start = ((), (), s32[]{:S(2)}) async-start(), calls=%async_computation.13 | async-start | bytes 4587520 | tf_op jit(solution)/shard_map/reduce_scatter | solution.py:82
  250.2 67.2 %collective-permute-start.14 = (f32[1,64,1792]{2,1,0:T(8,128)}, f32[1,64,1792]{2,1,0:T(8,128)S(1)}, u32[]{:S(2)}, u32[]{:S(2)}) collective-permute-start(f32[1,64,1792]{2,1,0:T(8,128)} %get-tuple-element.147), channel_id=1, source_target_pairs={{24,16},{16,8},{8,0},{25,17},{17,9},{9,1},{26,18},{18,10},{10,2},{... | collective-permute-start | bytes 1376264 | tf_op jit(solution)/shard_map/ppermute | solution.py:78
  251.5 63.9 %collective-permute-start.20 = (f32[1,64,1792]{2,1,0:T(8,128)S(1)}, f32[1,64,1792]{2,1,0:T(8,128)S(1)}, u32[]{:S(2)}, u32[]{:S(2)}) collective-permute-start(f32[1,64,1792]{2,1,0:T(8,128)S(1)} %get-tuple-element.146), channel_id=1, source_target_pairs={{24,16},{16,8},{8,0},{25,17},{17,9},{9,1},{26,18},{18,10},{10,2},{... | collective-permute-start | bytes 1376264 | tf_op jit(solution)/shard_map/ppermute | solution.py:78
  254.1 106.7 %collective-permute-start.17 = (f32[2,1,64,1792]{3,2,1,0:T(8,128)S(1)}, f32[2,1,64,1792]{3,2,1,0:T(8,128)S(1)}, u32[]{:S(2)}, u32[]{:S(2)}) collective-permute-start(f32[2,1,64,1792]{3,2,1,0:T(8,128)S(1)} %constant_dynamic-slice_fusion.17), channel_id=1, source_target_pairs={{0,5},{1,6},{2,7},{3,0},{4,1},{5,2},{6,3},{7,4},{8,13},{9,14},{10,... | collective-permute-start | bytes 2752520 | tf_op jit(solution)/shard_map/ppermute | solution.py:42
  254.1 64.6 %collective-permute-start.19 = (f32[1,64,1792]{2,1,0:T(8,128)S(1)}, f32[1,64,1792]{2,1,0:T(8,128)S(1)}, u32[]{:S(2)}, u32[]{:S(2)}) collective-permute-start(f32[1,64,1792]{2,1,0:T(8,128)S(1)} %get-tuple-element.146), channel_id=1, source_target_pairs={{0,8},{8,16},{16,24},{1,9},{9,17},{17,25},{2,10},{10,18},{18,26},{... | collective-permute-start | bytes 1376264 | tf_op jit(solution)/shard_map/ppermute | solution.py:78
  374.9 51.9 %collective-permute-start.31 = (f32[1,64,1792]{2,1,0:T(8,128)}, f32[1,64,1792]{2,1,0:T(8,128)}, u32[]{:S(2)}, u32[]{:S(2)}) collective-permute-start(f32[1,64,1792]{2,1,0:T(8,128)} %get-tuple-element.144), channel_id=1, source_target_pairs={{0,8},{8,16},{16,24},{1,9},{9,17},{17,25},{2,10},{10,18},{18,26},{... | collective-permute-start | bytes 1376264 | tf_op jit(solution)/shard_map/ppermute | solution.py:78
  396.2 87.1 %collective-permute-start.29 = (f32[2,1,64,1792]{3,2,1,0:T(8,128)}, f32[2,1,64,1792]{3,2,1,0:T(8,128)}, u32[]{:S(2)}, u32[]{:S(2)}) collective-permute-start(f32[2,1,64,1792]{3,2,1,0:T(8,128)} %constant_dynamic-slice_fusion.12), channel_id=1, source_target_pairs={{0,4},{1,5},{2,6},{3,7},{4,0},{5,1},{6,2},{7,3},{8,12},{9,13},{10,... | collective-permute-start | bytes 2752520 | tf_op jit(solution)/shard_map/ppermute | solution.py:42
  399.6 83.8 %collective-permute-start.25 = (f32[1,64,1792]{2,1,0:T(8,128)}, f32[1,64,1792]{2,1,0:T(8,128)}, u32[]{:S(2)}, u32[]{:S(2)}) collective-permute-start(f32[1,64,1792]{2,1,0:T(8,128)} %collective-permute-done.24), channel_id=1, source_target_pairs={{8,16},{16,24},{9,17},{17,25},{10,18},{18,26},{11,19},{19,27},{12,... | collective-permute-start | bytes 1376264 | tf_op jit(solution)/shard_map/ppermute | solution.py:78
  406.6 76.8 %collective-permute-start.27 = (f32[1,64,1792]{2,1,0:T(8,128)}, f32[1,64,1792]{2,1,0:T(8,128)}, u32[]{:S(2)}, u32[]{:S(2)}) collective-permute-start(f32[1,64,1792]{2,1,0:T(8,128)} %collective-permute-done.26), channel_id=1, source_target_pairs={{16,8},{8,0},{17,9},{9,1},{18,10},{10,2},{19,11},{11,3},{20,12},{1... | collective-permute-start | bytes 1376264 | tf_op jit(solution)/shard_map/ppermute | solution.py:78
  425.5 57.8 %collective-permute-start.33 = (f32[1,64,1792]{2,1,0:T(8,128)}, f32[1,64,1792]{2,1,0:T(8,128)}, u32[]{:S(2)}, u32[]{:S(2)}) collective-permute-start(f32[1,64,1792]{2,1,0:T(8,128)} %collective-permute-done.32), channel_id=1, source_target_pairs={{16,8},{8,0},{17,9},{9,1},{18,10},{10,2},{19,11},{11,3},{20,12},{1... | collective-permute-start | bytes 1376264 | tf_op jit(solution)/shard_map/ppermute | solution.py:78
  430.2 85.4 %collective-permute-start.6 = (f32[1,64,1792]{2,1,0:T(8,128)}, f32[1,64,1792]{2,1,0:T(8,128)}, u32[]{:S(2)}, u32[]{:S(2)}) collective-permute-start(f32[1,64,1792]{2,1,0:T(8,128)} %broadcast_select_fusion.15), channel_id=1, source_target_pairs={{16,24},{8,0},{17,25},{9,1},{18,26},{10,2},{19,27},{11,3},{20,28},... | collective-permute-start | bytes 1376264 | tf_op jit(solution)/shard_map/ppermute | solution.py:76
  536.9 60.4 %collective-permute-start.11 = (f32[1,64,1792]{2,1,0:T(8,128)}, f32[1,64,1792]{2,1,0:T(8,128)}, u32[]{:S(2)}, u32[]{:S(2)}) collective-permute-start(f32[1,64,1792]{2,1,0:T(8,128)} %broadcast_select_fusion.14), channel_id=1, source_target_pairs={{16,24},{8,0},{17,25},{9,1},{18,26},{10,2},{19,27},{11,3},{20,28},... | collective-permute-start | bytes 1376264 | tf_op jit(solution)/shard_map/ppermute | solution.py:76
  595.4 366.9 %reduce-scatter.21.cloned.1.call-start = ((), (), s32[]{:S(2)}) async-start(), calls=%async_computation.14 | async-start | bytes 4587520 | tf_op jit(solution)/shard_map/reduce_scatter | solution.py:82
  611.1 66.8 %collective-permute-start.23 = (f32[1,64,1792]{2,1,0:T(8,128)S(1)}, f32[1,64,1792]{2,1,0:T(8,128)S(1)}, u32[]{:S(2)}, u32[]{:S(2)}) collective-permute-start(f32[1,64,1792]{2,1,0:T(8,128)S(1)} %broadcast_select_fusion.12), channel_id=1, source_target_pairs={{16,24},{8,0},{17,25},{9,1},{18,26},{10,2},{19,27},{11,3},{20,28},... | collective-permute-start | bytes 1376264 | tf_op jit(solution)/shard_map/ppermute | solution.py:76
  689.3 348.4 %reduce-scatter.23.cloned.1.call-start = ((), (), s32[]{:S(2)}) async-start(), calls=%async_computation.15 | async-start | bytes 4587520 | tf_op jit(solution)/shard_map/reduce_scatter | solution.py:82
  697.0 69.9 %collective-permute-start.35 = (f32[1,64,1792]{2,1,0:T(8,128)S(1)}, f32[1,64,1792]{2,1,0:T(8,128)S(1)}, u32[]{:S(2)}, u32[]{:S(2)}) collective-permute-start(f32[1,64,1792]{2,1,0:T(8,128)S(1)} %broadcast_select_fusion.10), channel_id=1, source_target_pairs={{16,24},{8,0},{17,25},{9,1},{18,26},{10,2},{19,27},{11,3},{20,28},... | collective-permute-start | bytes 1376264 | tf_op jit(solution)/shard_map/ppermute | solution.py:76
  776.4 96.6 %collective-permute-start.47 = (f32[1,64,1792]{2,1,0:T(8,128)}, f32[1,64,1792]{2,1,0:T(8,128)S(1)}, u32[]{:S(2)}, u32[]{:S(2)}) collective-permute-start(f32[1,64,1792]{2,1,0:T(8,128)} %broadcast_select_fusion.8), channel_id=1, source_target_pairs={{16,24},{8,0},{17,25},{9,1},{18,26},{10,2},{19,27},{11,3},{20,28},... | collective-permute-start | bytes 1376264 | tf_op jit(solution)/shard_map/ppermute | solution.py:76
  777.7 96.0 %collective-permute-start.50 = (f32[1,64,1792]{2,1,0:T(8,128)}, f32[1,64,1792]{2,1,0:T(8,128)}, u32[]{:S(2)}, u32[]{:S(2)}) collective-permute-start(f32[1,64,1792]{2,1,0:T(8,128)} %get-tuple-element.141), channel_id=1, source_target_pairs={{24,16},{16,8},{8,0},{25,17},{17,9},{9,1},{26,18},{18,10},{10,2},{... | collective-permute-start | bytes 1376264 | tf_op jit(solution)/shard_map/ppermute | solution.py:78
  779.0 101.2 %collective-permute-start.55 = (f32[1,64,1792]{2,1,0:T(8,128)S(1)}, f32[1,64,1792]{2,1,0:T(8,128)}, u32[]{:S(2)}, u32[]{:S(2)}) collective-permute-start(f32[1,64,1792]{2,1,0:T(8,128)S(1)} %copy-done.17), channel_id=1, source_target_pairs={{0,8},{8,16},{16,24},{1,9},{9,17},{17,25},{2,10},{10,18},{18,26},{... | collective-permute-start | bytes 1376264 | tf_op jit(solution)/shard_map/ppermute | solution.py:78
  785.0 90.0 %collective-permute-start.56 = (f32[1,64,1792]{2,1,0:T(8,128)S(1)}, f32[1,64,1792]{2,1,0:T(8,128)}, u32[]{:S(2)}, u32[]{:S(2)}) collective-permute-start(f32[1,64,1792]{2,1,0:T(8,128)S(1)} %copy-done.17), channel_id=1, source_target_pairs={{24,16},{16,8},{8,0},{25,17},{17,9},{9,1},{26,18},{18,10},{10,2},{... | collective-permute-start | bytes 1376264 | tf_op jit(solution)/shard_map/ppermute | solution.py:78
  788.1 73.2 %collective-permute-start.42 = (f32[1,64,1792]{2,1,0:T(8,128)}, f32[1,64,1792]{2,1,0:T(8,128)S(1)}, u32[]{:S(2)}, u32[]{:S(2)}) collective-permute-start(f32[1,64,1792]{2,1,0:T(8,128)} %broadcast_select_fusion.9), channel_id=1, source_target_pairs={{16,24},{8,0},{17,25},{9,1},{18,26},{10,2},{19,27},{11,3},{20,28},... | collective-permute-start | bytes 1376264 | tf_op jit(solution)/shard_map/ppermute | solution.py:76
  961.0 69.0 %collective-permute-start.71 = (f32[1,64,1792]{2,1,0:T(8,128)}, f32[1,64,1792]{2,1,0:T(8,128)}, u32[]{:S(2)}, u32[]{:S(2)}) collective-permute-start(f32[1,64,1792]{2,1,0:T(8,128)} %broadcast_select_fusion.4), channel_id=1, source_target_pairs={{16,24},{8,0},{17,25},{9,1},{18,26},{10,2},{19,27},{11,3},{20,28},... | collective-permute-start | bytes 1376264 | tf_op jit(solution)/shard_map/ppermute | solution.py:76
  1039.1 55.9 %collective-permute-start.83 = (f32[1,64,1792]{2,1,0:T(8,128)S(1)}, f32[1,64,1792]{2,1,0:T(8,128)S(1)}, u32[]{:S(2)}, u32[]{:S(2)}) collective-permute-start(f32[1,64,1792]{2,1,0:T(8,128)S(1)} %get-tuple-element.135), channel_id=1, source_target_pairs={{0,8},{8,16},{16,24},{1,9},{9,17},{17,25},{2,10},{10,18},{18,26},{... | collective-permute-start | bytes 1376264 | tf_op jit(solution)/shard_map/ppermute | solution.py:78
  (92 other events, 2664.8 us)
Sparse Core Ops, SparseCore 0:
  23.7 71.1 reduce-scatter.8
  97.7 95.7 reduce-scatter.10
  238.6 91.5 reduce-scatter.12
  332.4 88.6 reduce-scatter.14
  423.2 98.0 reduce-scatter.16
  595.6 88.8 reduce-scatter.18
  689.4 88.1 reduce-scatter.20
  795.0 91.7 reduce-scatter.22

commit v5 on v2

v5 whole, which is shorter than its diff:
```python
import jax
import jax.numpy as jnp
from jax import lax
from jax.experimental import pallas as pl
from jax.sharding import PartitionSpec as P

OUTER_RATE = 0.7
MOMENTUM_COEF = 0.5
STEPS = 8
STREAMS = 2


def blank(shape):
    return pl.pallas_call(
        lambda out: None,
        out_shape=jax.ShapeDtypeStruct(shape, jnp.float32),
        out_specs=pl.BlockSpec(memory_space=pl.ANY),
    )()


def body(inner_weights, start_weights, momentum):
    groups = lax.axis_size("grp")
    shards = lax.axis_size("shard")
    tp_size = lax.axis_size("tp")
    plane = shards * tp_size
    group = lax.axis_index("grp")
    place = lax.axis_index(("shard", "tp"))
    row_count, col_count = start_weights.shape[1:]
    q_rows = row_count // (groups * plane)
    steps = min(STEPS, plane)
    merge = plane // steps
    turns = steps // STREAMS
    block = (q_rows, col_count)

    inner = inner_weights.reshape((2, groups, plane) + block)
    start = start_weights.reshape((2, groups, plane) + block)
    held = momentum.reshape((2, plane) + block)
    rightward = [(i, i + 1) for i in range(groups - 1)]
    leftward = [(i + 1, i) for i in range(groups - 1)]

    def lane(shift):
        return lax.rem(place + shift, plane)

    def shifts_of(step):
        return [step * merge + m for m in range(merge)]

    def join(parts):
        return parts[0] if merge == 1 else jnp.concatenate(parts, axis=1)

    def parts_of(chunk):
        return [chunk[:, m * q_rows : (m + 1) * q_rows] for m in range(merge)]

    def rows_of(array, owner, step):
        def cut(shift):
            return lax.dynamic_slice(array, (0, owner, lane(shift), 0, 0), (2, 1, 1) + block).reshape((2,) + block)

        return join([cut(shift) for shift in shifts_of(step)])

    def own(owner, step):
        return rows_of(start, owner, step) - rows_of(inner, owner, step)

    def rotate(part, shift):
        if shift % plane == 0:
            return part
        return lax.ppermute(part, ("shard", "tp"), [(i, (i + shift) % plane) for i in range(plane)])

    new_weights = blank(start.shape)
    new_held = blank(held.shape)

    def write_weights(array, owner, step, update):
        for shift, part in zip(shifts_of(step), parts_of(update)):
            at = (0, owner, lane(shift), 0, 0)
            old = lax.dynamic_slice(start, at, (2, 1, 1) + block)
            array = lax.dynamic_update_slice(array, old - part[:, None, None], at)
        return array

    def after(first, *arrays):
        return lax.optimization_barrier((first, *arrays))[1:]

    order = [[(stream * turns + turn + 1) % steps for turn in range(turns)] for stream in range(STREAMS)]
    zero = jnp.zeros((2, merge * q_rows, col_count), jnp.float32)
    from_left, from_right = [zero] * STREAMS, [zero] * STREAMS
    arrived_left, arrived_right = [[]] * STREAMS, [[]] * STREAMS
    moved, outgoing, transit = {}, {}, []
    payload = zero

    def fetch(step):
        parts = [lax.dynamic_slice_in_dim(held, lane(plane - shift), 1, 1)[:, 0] for shift in shifts_of(step)]
        parts = after(payload, *parts)
        return ("fetch", step, [rotate(part, -shift) for part, shift in zip(parts, shifts_of(step))])

    def deliver(step):
        parts = after(payload, *parts_of(outgoing[step]))
        return ("deliver", step, [rotate(part, shift) for part, shift in zip(parts, shifts_of(step))])

    def land(array, step, parts):
        for shift, part in zip(shifts_of(step), parts):
            array = lax.dynamic_update_slice_in_dim(array, part[:, None], lane(plane - shift), 1)
        return array

    for turn in range(turns + 1):
        for phase in range(1, groups + 1):
            if turn == turns and phase > groups - 2:
                break
            for stream in range(STREAMS):
                in_turn = (phase - 1) * STREAMS + stream
                tick = turn * groups * STREAMS + in_turn
                landed = [entry for entry in transit if entry[0] <= tick]
                transit = [entry for entry in transit if entry[0] > tick]
                values = after(payload, from_left[stream], from_right[stream], *[p for e in landed for p in e[3]])
                here_left, here_right, values = values[0], values[1], list(values[2:])
                for _, kind, step, parts in landed:
                    parts, values = values[: len(parts)], values[len(parts) :]
                    if kind == "fetch":
                        moved[step] = join(parts)
                    else:
                        new_held = land(new_held, step, parts)
                step = order[stream][turn] if turn < turns else None
                if phase < groups:
                    to_right, to_left = here_left, here_right
                    if turn < turns:
                        right_owner = jnp.minimum(groups - phase + group, groups - 1)
                        left_owner = jnp.maximum(group - (groups - phase), 0)
                        to_right = jnp.where(group < phase, to_right + own(right_owner, step), to_right)
                        to_left = jnp.where(groups - 1 - group < phase, to_left + own(left_owner, step), to_left)
                else:
                    if step not in moved:
                        moved[step] = join(fetch(step)[2])
                    total = own(group, step) + here_left + here_right
                    mean_diff = total / groups
                    new_momentum = MOMENTUM_COEF * moved[step] + mean_diff
                    update = OUTER_RATE * (mean_diff + MOMENTUM_COEF * new_momentum)
                    outgoing[step] = new_momentum
                    if step == 0:
                        new_held = land(new_held, *deliver(step)[1:])
                    new_weights = write_weights(new_weights, group, step, update)
                    to_right = to_left = update
                payload = to_right
                from_left[stream] = lax.ppermute(to_right, "grp", rightward)
                from_right[stream] = lax.ppermute(to_left, "grp", leftward)
                slot = in_turn // 2
                if in_turn % 2 == 0 and slot < STREAMS and turn < turns and order[slot][turn] != 0:
                    transit.append((tick + 2,) + fetch(order[slot][turn]))
                slot = slot - STREAMS if turn < turns else slot
                if in_turn % 2 == 0 and 0 <= slot < STREAMS and turn > 0 and order[slot][turn - 1] != 0:
                    transit.append((tick + 2,) + deliver(order[slot][turn - 1]))
                if phase == groups:
                    arrived_left[stream], arrived_right[stream] = [], []
                arrived_left[stream].append(from_left[stream])
                arrived_right[stream].append(from_right[stream])
                if len(arrived_left[stream]) == groups - 1 and turn > 0:
                    for hop in range(groups - 1):
                        update = jnp.where(
                            group > hop,
                            arrived_left[stream][hop],
                            arrived_right[stream][groups - 2 - hop],
                        )
                        owner = lax.rem(group + groups - 1 - hop, groups)
                        new_weights = write_weights(new_weights, owner, order[stream][turn - 1], update)
    for _, _, step, parts in transit:
        new_held = land(new_held, step, parts)
    return (new_weights.reshape(start_weights.shape), new_held.reshape(momentum.shape))


def solution(mesh):
    in_specs = (
        P("grp", None, "shard", "tp"),
        P(None, "shard", "tp"),
        P(None, None, None, ("grp", "shard", "tp"), None, None),
    )
    out_specs = (P(None, "shard", "tp"), P(None, None, None, ("grp", "shard", "tp"), None, None))
    return jax.shard_map(body, mesh=mesh, in_specs=in_specs, out_specs=out_specs, check_vma=False)
```

time: 915 us -> 837 us (0.915)
  starting transfers between devices: 443 us -> 212 us
  waiting for transfers between devices: 253 us -> 433 us
  other arithmetic: 194 us -> 166 us
  local copies, waits for them, and re-layouts: 7.79 us -> 19.8 us
    ppermute x136 -> x72, starting transfers between devices: 404 us -> 203 us  [the longest x36 156 us: body(): from_left[stream] = lax.ppermute(to_right, 'grp', rightward)]
    ppermute x136 -> x72, waiting for transfers between devices: 245 us -> 433 us  [the longest x36 406 us: body(): from_right[stream] = lax.ppermute(to_left, 'grp', leftward)]
    ppermute x28 -> x14, starting transfers between devices: 39.4 us -> 8.81 us  [rotate(): lax.ppermute(part, ('shard', 'tp'), [(i, (i + shift) % plane) for i in ra...]
    dynamic_update_slice x64 -> x32, other arithmetic: 86.4 us -> 68.8 us  [write_weights(): array = lax.dynamic_update_slice(array, old - part[:, None, None], at)]
    dynamic_update_slice x16 -> x8, local copies, waits for them, and re-layouts: 0.59 us -> 12.7 us  [land(): lax.dynamic_update_slice_in_dim(array, part[:, None], lane(plane - shift)...]
    add x16 -> x8, other arithmetic: 26.2 us -> 20.5 us  [body(): new_momentum = MOMENTUM_COEF * moved[step] + mean_diff]
    select_n x48 -> x24, other arithmetic: 81.5 us -> 77.1 us  [the longest x14 51 us: body(): jnp.where(groups - 1 - group < phase, to_left + own(left_owner, step), to...]
  transfers between devices with their start and end apart: 164 -> 86, of which waited for: 71 -> 44; matrix products, arithmetic and copies ran while one was open for 22% -> 22% of each run, Pallas kernels for 0% -> 0%
where the time goes in v5:
time: 837 us; the launch traced here: 833 us
  waiting for transfers between devices  433 us (52%)
  starting transfers between devices  212 us (25%)
  other arithmetic  166 us (20%)
  local copies, waits for them, and re-layouts  19.8 us (2%)
    ppermute x36, waiting for transfers between devices, body(): from_right[stream] = lax.ppermute(to_left, 'grp', leftward)  406 us
    ppermute x36, starting transfers between devices, body(): from_left[stream] = lax.ppermute(to_right, 'grp', rightward)  156 us
    dynamic_update_slice x32, other arithmetic, write_weights(): array = lax.dynamic_update_slice(array, old - part[:, None, None], at)  68.8 us
    select_n x14, other arithmetic, body(): jnp.where(groups - 1 - group < phase, to_left + own(left_owner, step), to...  51 us
    ppermute x36, starting transfers between devices, body(): from_right[stream] = lax.ppermute(to_left, 'grp', leftward)  47.2 us
    ppermute x36, waiting for transfers between devices, body(): from_left[stream] = lax.ppermute(to_right, 'grp', rightward)  27.2 us
    select_n x10, other arithmetic, body(): jnp.where(group < phase, to_right + own(right_owner, step), to_right)  26.1 us
    add x8, other arithmetic, body(): new_momentum = MOMENTUM_COEF * moved[step] + mean_diff  20.5 us
  transfers between devices with their start and end apart: 86, of which 44 were waited for; matrix products, arithmetic and copies ran while one was open for 22% of the time, Pallas kernels for 0%

profile of v5, /device:TPU:0, one launch (start us, length us, event | category | flops | bytes accessed | tf_op | source)
XLA Modules:
  0.0 833.0 jit_solution(8278556897596639457)
XLA Ops:
  29.2 7.5 collective-permute-done.1
  48.9 14.7 %collective-permute-done.4 = f32[2,64,1792]{2,1,0:T(8,128)} collective-permute-done((f32[2,64,1792]{2,1,0:T(8,128)}, f32[2,64,1792]{2,1,0:T(8,128)}, u32[]{:S(2)}, u32[]{:S(2)}) %collective-permute-start.4) | collective-permute-done | bytes 917536 | tf_op jit(solution)/shard_map/ppermute | solution.py:140
  74.6 15.4 %collective-permute-done.6 = f32[2,64,1792]{2,1,0:T(8,128)} collective-permute-done((f32[2,64,1792]{2,1,0:T(8,128)}, f32[2,64,1792]{2,1,0:T(8,128)}, u32[]{:S(2)}, u32[]{:S(2)}) %collective-permute-start.6) | collective-permute-done | bytes 917536 | tf_op jit(solution)/shard_map/ppermute | solution.py:140
  101.0 14.4 %collective-permute-done.9 = f32[2,64,1792]{2,1,0:T(8,128)} collective-permute-done((f32[2,64,1792]{2,1,0:T(8,128)}, f32[2,64,1792]{2,1,0:T(8,128)}, u32[]{:S(2)}, u32[]{:S(2)}) %collective-permute-start.9) | collective-permute-done | bytes 917536 | tf_op jit(solution)/shard_map/ppermute | solution.py:140
  127.8 18.1 %collective-permute-done.11 = f32[2,64,1792]{2,1,0:T(8,128)} collective-permute-done((f32[2,64,1792]{2,1,0:T(8,128)}, f32[2,64,1792]{2,1,0:T(8,128)}, u32[]{:S(2)}, u32[]{:S(2)}) %collective-permute-start.11) | collective-permute-done | bytes 917536 | tf_op jit(solution)/shard_map/ppermute | solution.py:140
  155.3 10.2 %collective-permute-done.13 = f32[2,64,1792]{2,1,0:T(8,128)S(1)} collective-permute-done((f32[2,64,1792]{2,1,0:T(8,128)}, f32[2,64,1792]{2,1,0:T(8,128)S(1)}, u32[]{:S(2)}, u32[]{:S(2)}) %collective-permute-start.13) | collective-permute-done | bytes 917536 | tf_op jit(solution)/shard_map/ppermute | solution.py:140
  174.4 10.7 %collective-permute-done.15 = f32[2,64,1792]{2,1,0:T(8,128)S(1)} collective-permute-done((f32[2,64,1792]{2,1,0:T(8,128)S(1)}, f32[2,64,1792]{2,1,0:T(8,128)S(1)}, u32[]{:S(2)}, u32[]{:S(2)}) %collective-permute-start.15) | collective-permute-done | bytes 917536 | tf_op jit(solution)/shard_map/ppermute | solution.py:140
  189.7 9.9 %collective-permute-done.17 = f32[2,64,1792]{2,1,0:T(8,128)S(1)} collective-permute-done((f32[2,64,1792]{2,1,0:T(8,128)S(1)}, f32[2,64,1792]{2,1,0:T(8,128)S(1)}, u32[]{:S(2)}, u32[]{:S(2)}) %collective-permute-start.17) | collective-permute-done | bytes 917536 | tf_op jit(solution)/shard_map/ppermute | solution.py:140
  210.8 10.7 %collective-permute-done.19 = f32[2,64,1792]{2,1,0:T(8,128)S(1)} collective-permute-done((f32[2,64,1792]{2,1,0:T(8,128)S(1)}, f32[2,64,1792]{2,1,0:T(8,128)S(1)}, u32[]{:S(2)}, u32[]{:S(2)}) %collective-permute-start.19) | collective-permute-done | bytes 917536 | tf_op jit(solution)/shard_map/ppermute | solution.py:140
  233.7 9.7 %collective-permute-done.24 = f32[2,64,1792]{2,1,0:T(8,128)} collective-permute-done((f32[2,64,1792]{2,1,0:T(8,128)S(1)}, f32[2,64,1792]{2,1,0:T(8,128)}, u32[]{:S(2)}, u32[]{:S(2)}) %collective-permute-start.24) | collective-permute-done | bytes 917536 | tf_op jit(solution)/shard_map/ppermute | solution.py:140
  253.3 11.3 %collective-permute-done.21 = f32[2,64,1792]{2,1,0:T(8,128)S(1)} collective-permute-done((f32[2,64,1792]{2,1,0:T(8,128)}, f32[2,64,1792]{2,1,0:T(8,128)S(1)}, u32[]{:S(2)}, u32[]{:S(2)}) %collective-permute-start.21) | collective-permute-done | bytes 917536 | tf_op jit(solution)/shard_map/ppermute | solution.py:140
  302.3 10.2 %collective-permute-done.29 = f32[2,64,1792]{2,1,0:T(8,128)S(1)} collective-permute-done((f32[2,64,1792]{2,1,0:T(8,128)S(1)}, f32[2,64,1792]{2,1,0:T(8,128)S(1)}, u32[]{:S(2)}, u32[]{:S(2)}) %collective-permute-start.29) | collective-permute-done | bytes 917536 | tf_op jit(solution)/shard_map/ppermute | solution.py:140
  321.6 10.5 %collective-permute-done.32 = f32[2,64,1792]{2,1,0:T(8,128)S(1)} collective-permute-done((f32[2,64,1792]{2,1,0:T(8,128)S(1)}, f32[2,64,1792]{2,1,0:T(8,128)S(1)}, u32[]{:S(2)}, u32[]{:S(2)}) %collective-permute-start.32) | collective-permute-done | bytes 917536 | tf_op jit(solution)/shard_map/ppermute | solution.py:140
  342.0 9.8 %collective-permute-done.34 = f32[2,64,1792]{2,1,0:T(8,128)S(1)} collective-permute-done((f32[2,64,1792]{2,1,0:T(8,128)S(1)}, f32[2,64,1792]{2,1,0:T(8,128)S(1)}, u32[]{:S(2)}, u32[]{:S(2)}) %collective-permute-start.34) | collective-permute-done | bytes 917536 | tf_op jit(solution)/shard_map/ppermute | solution.py:140
  359.3 10.2 %collective-permute-done.37 = f32[2,64,1792]{2,1,0:T(8,128)S(1)} collective-permute-done((f32[2,64,1792]{2,1,0:T(8,128)S(1)}, f32[2,64,1792]{2,1,0:T(8,128)S(1)}, u32[]{:S(2)}, u32[]{:S(2)}) %collective-permute-start.37) | collective-permute-done | bytes 917536 | tf_op jit(solution)/shard_map/ppermute | solution.py:140
  379.0 16.9 %collective-permute-done.39 = f32[2,64,1792]{2,1,0:T(8,128)S(1)} collective-permute-done((f32[2,64,1792]{2,1,0:T(8,128)S(1)}, f32[2,64,1792]{2,1,0:T(8,128)S(1)}, u32[]{:S(2)}, u32[]{:S(2)}) %collective-permute-start.39) | collective-permute-done | bytes 917536 | tf_op jit(solution)/shard_map/ppermute | solution.py:140
  405.9 17.8 %collective-permute-done.44 = f32[2,64,1792]{2,1,0:T(8,128)S(1)} collective-permute-done((f32[2,64,1792]{2,1,0:T(8,128)}, f32[2,64,1792]{2,1,0:T(8,128)S(1)}, u32[]{:S(2)}, u32[]{:S(2)}) %collective-permute-start.44) | collective-permute-done | bytes 917536 | tf_op jit(solution)/shard_map/ppermute | solution.py:140
  433.2 19.0 %collective-permute-done.41 = f32[2,64,1792]{2,1,0:T(8,128)S(1)} collective-permute-done((f32[2,64,1792]{2,1,0:T(8,128)}, f32[2,64,1792]{2,1,0:T(8,128)S(1)}, u32[]{:S(2)}, u32[]{:S(2)}) %collective-permute-start.41) | collective-permute-done | bytes 917536 | tf_op jit(solution)/shard_map/ppermute | solution.py:140
  465.5 14.2 %collective-permute-done.45 = f32[2,64,1792]{2,1,0:T(8,128)S(1)} collective-permute-done((f32[2,64,1792]{2,1,0:T(8,128)}, f32[2,64,1792]{2,1,0:T(8,128)S(1)}, u32[]{:S(2)}, u32[]{:S(2)}) %collective-permute-start.45) | collective-permute-done | bytes 917536 | tf_op jit(solution)/shard_map/ppermute | solution.py:140
  496.3 12.5 %collective-permute-done.49 = f32[2,64,1792]{2,1,0:T(8,128)S(1)} collective-permute-done((f32[2,64,1792]{2,1,0:T(8,128)}, f32[2,64,1792]{2,1,0:T(8,128)S(1)}, u32[]{:S(2)}, u32[]{:S(2)}) %collective-permute-start.49) | collective-permute-done | bytes 917536 | tf_op jit(solution)/shard_map/ppermute | solution.py:140
  517.9 10.5 %collective-permute-done.52 = f32[2,64,1792]{2,1,0:T(8,128)S(1)} collective-permute-done((f32[2,64,1792]{2,1,0:T(8,128)}, f32[2,64,1792]{2,1,0:T(8,128)S(1)}, u32[]{:S(2)}, u32[]{:S(2)}) %collective-permute-start.52) | collective-permute-done | bytes 917536 | tf_op jit(solution)/shard_map/ppermute | solution.py:140
  538.3 9.9 %collective-permute-done.54 = f32[2,64,1792]{2,1,0:T(8,128)} collective-permute-done((f32[2,64,1792]{2,1,0:T(8,128)}, f32[2,64,1792]{2,1,0:T(8,128)}, u32[]{:S(2)}, u32[]{:S(2)}) %collective-permute-start.54) | collective-permute-done | bytes 917536 | tf_op jit(solution)/shard_map/ppermute | solution.py:140
  555.7 10.4 %collective-permute-done.57 = f32[2,64,1792]{2,1,0:T(8,128)S(1)} collective-permute-done((f32[2,64,1792]{2,1,0:T(8,128)}, f32[2,64,1792]{2,1,0:T(8,128)S(1)}, u32[]{:S(2)}, u32[]{:S(2)}) %collective-permute-start.57) | collective-permute-done | bytes 917536 | tf_op jit(solution)/shard_map/ppermute | solution.py:140
  577.0 15.9 %collective-permute-done.59 = f32[2,64,1792]{2,1,0:T(8,128)} collective-permute-done((f32[2,64,1792]{2,1,0:T(8,128)S(1)}, f32[2,64,1792]{2,1,0:T(8,128)}, u32[]{:S(2)}, u32[]{:S(2)}) %collective-permute-start.59) | collective-permute-done | bytes 917536 | tf_op jit(solution)/shard_map/ppermute | solution.py:140
  604.9 13.9 %collective-permute-done.64 = f32[2,64,1792]{2,1,0:T(8,128)} collective-permute-done((f32[2,64,1792]{2,1,0:T(8,128)}, f32[2,64,1792]{2,1,0:T(8,128)}, u32[]{:S(2)}, u32[]{:S(2)}) %collective-permute-start.64) | collective-permute-done | bytes 917536 | tf_op jit(solution)/shard_map/ppermute | solution.py:140
  632.1 10.6 %collective-permute-done.61 = f32[2,64,1792]{2,1,0:T(8,128)S(1)} collective-permute-done((f32[2,64,1792]{2,1,0:T(8,128)S(1)}, f32[2,64,1792]{2,1,0:T(8,128)S(1)}, u32[]{:S(2)}, u32[]{:S(2)}) %collective-permute-start.61) | collective-permute-done | bytes 917536 | tf_op jit(solution)/shard_map/ppermute | solution.py:140
  658.8 7.1 collective-permute-done.65
  683.3 10.9 %collective-permute-done.68 = f32[2,64,1792]{2,1,0:T(8,128)S(1)} collective-permute-done((f32[2,64,1792]{2,1,0:T(8,128)S(1)}, f32[2,64,1792]{2,1,0:T(8,128)S(1)}, u32[]{:S(2)}, u32[]{:S(2)}) %collective-permute-start.68) | collective-permute-done | bytes 917536 | tf_op jit(solution)/shard_map/ppermute | solution.py:140
  703.3 10.6 %collective-permute-done.71 = f32[2,64,1792]{2,1,0:T(8,128)S(1)} collective-permute-done((f32[2,64,1792]{2,1,0:T(8,128)S(1)}, f32[2,64,1792]{2,1,0:T(8,128)S(1)}, u32[]{:S(2)}, u32[]{:S(2)}) %collective-permute-start.71) | collective-permute-done | bytes 917536 | tf_op jit(solution)/shard_map/ppermute | solution.py:140
  754.8 7.1 collective-permute-done.77
  795.3 12.8 %collective-permute-done.80 = f32[2,64,1792]{2,1,0:T(8,128)S(1)} collective-permute-done((f32[2,64,1792]{2,1,0:T(8,128)S(1)}, f32[2,64,1792]{2,1,0:T(8,128)S(1)}, u32[]{:S(2)}, u32[]{:S(2)}) %collective-permute-start.80) | collective-permute-done | bytes 917536 | tf_op jit(solution)/shard_map/ppermute | solution.py:140
  814.8 11.4 %collective-permute-done.84 = f32[2,64,1792]{2,1,0:T(8,128)S(1)} collective-permute-done((f32[2,64,1792]{2,1,0:T(8,128)S(1)}, f32[2,64,1792]{2,1,0:T(8,128)S(1)}, u32[]{:S(2)}, u32[]{:S(2)}) %collective-permute-start.84) | collective-permute-done | bytes 917536 | tf_op jit(solution)/shard_map/ppermute | solution.py:140
  (273 shorter events, 446.3 us)
Async XLA Ops:
  41.8 32.8 %collective-permute-start.5 = (f32[2,64,1792]{2,1,0:T(8,128)}, f32[2,64,1792]{2,1,0:T(8,128)}, u32[]{:S(2)}, u32[]{:S(2)}) collective-permute-start(f32[2,64,1792]{2,1,0:T(8,128)} %get-tuple-element.283), channel_id=1, source_target_pairs={{0,8},{8,16},{16,24},{1,9},{9,17},{17,25},{2,10},{10,18},{18,26},{... | collective-permute-start | bytes 2752520 | tf_op jit(solution)/shard_map/ppermute | solution.py:139
  69.1 31.9 %collective-permute-start.8 = (f32[2,64,1792]{2,1,0:T(8,128)}, f32[2,64,1792]{2,1,0:T(8,128)}, u32[]{:S(2)}, u32[]{:S(2)}) collective-permute-start(f32[2,64,1792]{2,1,0:T(8,128)} %get-tuple-element.281), channel_id=1, source_target_pairs={{0,8},{8,16},{16,24},{1,9},{9,17},{17,25},{2,10},{10,18},{18,26},{... | collective-permute-start | bytes 2752520 | tf_op jit(solution)/shard_map/ppermute | solution.py:139
  95.5 32.3 %collective-permute-start.10 = (f32[2,64,1792]{2,1,0:T(8,128)}, f32[2,64,1792]{2,1,0:T(8,128)}, u32[]{:S(2)}, u32[]{:S(2)}) collective-permute-start(f32[2,64,1792]{2,1,0:T(8,128)} %get-tuple-element.279), channel_id=1, source_target_pairs={{0,8},{8,16},{16,24},{1,9},{9,17},{17,25},{2,10},{10,18},{18,26},{... | collective-permute-start | bytes 2752520 | tf_op jit(solution)/shard_map/ppermute | solution.py:139
  121.7 33.5 %collective-permute-start.12 = (f32[2,64,1792]{2,1,0:T(8,128)}, f32[2,64,1792]{2,1,0:T(8,128)S(1)}, u32[]{:S(2)}, u32[]{:S(2)}) collective-permute-start(f32[2,64,1792]{2,1,0:T(8,128)} %get-tuple-element.277), channel_id=1, source_target_pairs={{0,8},{8,16},{16,24},{1,9},{9,17},{17,25},{2,10},{10,18},{18,26},{... | collective-permute-start | bytes 2752520 | tf_op jit(solution)/shard_map/ppermute | solution.py:139
  126.5 39.0 %collective-permute-start.13 = (f32[2,64,1792]{2,1,0:T(8,128)}, f32[2,64,1792]{2,1,0:T(8,128)S(1)}, u32[]{:S(2)}, u32[]{:S(2)}) collective-permute-start(f32[2,64,1792]{2,1,0:T(8,128)} %get-tuple-element.275), channel_id=1, source_target_pairs={{8,0},{16,8},{24,16},{9,1},{17,9},{25,17},{10,2},{18,10},{26,18},{... | collective-permute-start | bytes 2752520 | tf_op jit(solution)/shard_map/ppermute | solution.py:140
  248.4 32.8 %collective-permute-start.26 = (f32[2,64,1792]{2,1,0:T(8,128)}, f32[2,64,1792]{2,1,0:T(8,128)S(1)}, u32[]{:S(2)}, u32[]{:S(2)}) collective-permute-start(f32[2,64,1792]{2,1,0:T(8,128)} %get-tuple-element.269), channel_id=1, source_target_pairs={{0,8},{8,16},{16,24},{1,9},{9,17},{17,25},{2,10},{10,18},{18,26},{... | collective-permute-start | bytes 2752520 | tf_op jit(solution)/shard_map/ppermute | solution.py:139
  269.1 33.2 %collective-permute-start.28 = (f32[2,64,1792]{2,1,0:T(8,128)S(1)}, f32[2,64,1792]{2,1,0:T(8,128)S(1)}, u32[]{:S(2)}, u32[]{:S(2)}) collective-permute-start(f32[2,64,1792]{2,1,0:T(8,128)S(1)} %get-tuple-element.267), channel_id=1, source_target_pairs={{0,8},{8,16},{16,24},{1,9},{9,17},{17,25},{2,10},{10,18},{18,26},{... | collective-permute-start | bytes 2752520 | tf_op jit(solution)/shard_map/ppermute | solution.py:139
  288.6 33.0 %collective-permute-start.31 = (f32[2,64,1792]{2,1,0:T(8,128)S(1)}, f32[2,64,1792]{2,1,0:T(8,128)S(1)}, u32[]{:S(2)}, u32[]{:S(2)}) collective-permute-start(f32[2,64,1792]{2,1,0:T(8,128)S(1)} %get-tuple-element.266), channel_id=1, source_target_pairs={{0,8},{8,16},{16,24},{1,9},{9,17},{17,25},{2,10},{10,18},{18,26},{... | collective-permute-start | bytes 2752520 | tf_op jit(solution)/shard_map/ppermute | solution.py:139
  293.2 38.9 %collective-permute-start.32 = (f32[2,64,1792]{2,1,0:T(8,128)S(1)}, f32[2,64,1792]{2,1,0:T(8,128)S(1)}, u32[]{:S(2)}, u32[]{:S(2)}) collective-permute-start(f32[2,64,1792]{2,1,0:T(8,128)S(1)} %get-tuple-element.264), channel_id=1, source_target_pairs={{8,0},{16,8},{24,16},{9,1},{17,9},{25,17},{10,2},{18,10},{26,18},{... | collective-permute-start | bytes 2752520 | tf_op jit(solution)/shard_map/ppermute | solution.py:140
  374.0 31.9 %collective-permute-start.43 = (f32[2,64,1792]{2,1,0:T(8,128)}, f32[2,64,1792]{2,1,0:T(8,128)S(1)}, u32[]{:S(2)}, u32[]{:S(2)}) collective-permute-start(f32[2,64,1792]{2,1,0:T(8,128)} %get-tuple-element.263), channel_id=1, source_target_pairs={{0,8},{8,16},{16,24},{1,9},{9,17},{17,25},{2,10},{10,18},{18,26},{... | collective-permute-start | bytes 2752520 | tf_op jit(solution)/shard_map/ppermute | solution.py:139
  400.2 33.0 %collective-permute-start.42 = (f32[2,64,1792]{2,1,0:T(8,128)}, f32[2,64,1792]{2,1,0:T(8,128)S(1)}, u32[]{:S(2)}, u32[]{:S(2)}) collective-permute-start(f32[2,64,1792]{2,1,0:T(8,128)} %get-tuple-element.261), channel_id=1, source_target_pairs={{0,8},{8,16},{16,24},{1,9},{9,17},{17,25},{2,10},{10,18},{18,26},{... | collective-permute-start | bytes 2752520 | tf_op jit(solution)/shard_map/ppermute | solution.py:139
  428.6 37.0 %collective-permute-start.46 = (f32[2,64,1792]{2,1,0:T(8,128)}, f32[2,64,1792]{2,1,0:T(8,128)S(1)}, u32[]{:S(2)}, u32[]{:S(2)}) collective-permute-start(f32[2,64,1792]{2,1,0:T(8,128)} %get-tuple-element.258), channel_id=1, source_target_pairs={{0,8},{8,16},{16,24},{1,9},{9,17},{17,25},{2,10},{10,18},{18,26},{... | collective-permute-start | bytes 2752520 | tf_op jit(solution)/shard_map/ppermute | solution.py:139
  456.7 39.6 %collective-permute-start.48 = (f32[2,64,1792]{2,1,0:T(8,128)}, f32[2,64,1792]{2,1,0:T(8,128)}, u32[]{:S(2)}, u32[]{:S(2)}) collective-permute-start(f32[2,64,1792]{2,1,0:T(8,128)} %get-tuple-element.256), channel_id=1, source_target_pairs={{0,8},{8,16},{16,24},{1,9},{9,17},{17,25},{2,10},{10,18},{18,26},{... | collective-permute-start | bytes 2752520 | tf_op jit(solution)/shard_map/ppermute | solution.py:139
  462.2 34.1 %collective-permute-start.50 = (f32[2,64,1792]{2,1,0:T(8,128)}, f32[2,64,1792]{2,1,0:T(8,128)}, u32[]{:S(2)}, u32[]{:S(2)}) collective-permute-start(f32[2,64,1792]{2,1,0:T(8,128)} %get-tuple-element.159), channel_id=1, source_target_pairs={{0,2},{1,3},{2,4},{3,5},{4,6},{5,7},{6,0},{7,1},{8,10},{9,11},{10,... | collective-permute-start | bytes 2752520 | tf_op jit(solution)/shard_map/ppermute | solution.py:65
  484.7 33.2 %collective-permute-start.51 = (f32[2,64,1792]{2,1,0:T(8,128)}, f32[2,64,1792]{2,1,0:T(8,128)S(1)}, u32[]{:S(2)}, u32[]{:S(2)}) collective-permute-start(f32[2,64,1792]{2,1,0:T(8,128)} %get-tuple-element.255), channel_id=1, source_target_pairs={{0,8},{8,16},{16,24},{1,9},{9,17},{17,25},{2,10},{10,18},{18,26},{... | collective-permute-start | bytes 2752520 | tf_op jit(solution)/shard_map/ppermute | solution.py:139
  489.3 39.1 %collective-permute-start.52 = (f32[2,64,1792]{2,1,0:T(8,128)}, f32[2,64,1792]{2,1,0:T(8,128)S(1)}, u32[]{:S(2)}, u32[]{:S(2)}) collective-permute-start(f32[2,64,1792]{2,1,0:T(8,128)} %get-tuple-element.253), channel_id=1, source_target_pairs={{8,0},{16,8},{24,16},{9,1},{17,9},{25,17},{10,2},{18,10},{26,18},{... | collective-permute-start | bytes 2752520 | tf_op jit(solution)/shard_map/ppermute | solution.py:140
  516.6 31.6 %collective-permute-start.54 = (f32[2,64,1792]{2,1,0:T(8,128)}, f32[2,64,1792]{2,1,0:T(8,128)}, u32[]{:S(2)}, u32[]{:S(2)}) collective-permute-start(f32[2,64,1792]{2,1,0:T(8,128)} %get-tuple-element.227), channel_id=1, source_target_pairs={{8,0},{16,8},{24,16},{9,1},{17,9},{25,17},{10,2},{18,10},{26,18},{... | collective-permute-start | bytes 2752520 | tf_op jit(solution)/shard_map/ppermute | solution.py:140
  571.5 33.4 %collective-permute-start.63 = (f32[2,64,1792]{2,1,0:T(8,128)}, f32[2,64,1792]{2,1,0:T(8,128)}, u32[]{:S(2)}, u32[]{:S(2)}) collective-permute-start(f32[2,64,1792]{2,1,0:T(8,128)} %get-tuple-element.252), channel_id=1, source_target_pairs={{0,8},{8,16},{16,24},{1,9},{9,17},{17,25},{2,10},{10,18},{18,26},{... | collective-permute-start | bytes 2752520 | tf_op jit(solution)/shard_map/ppermute | solution.py:139
  600.3 31.8 %collective-permute-start.62 = (f32[2,64,1792]{2,1,0:T(8,128)}, f32[2,64,1792]{2,1,0:T(8,128)S(1)}, u32[]{:S(2)}, u32[]{:S(2)}) collective-permute-start(f32[2,64,1792]{2,1,0:T(8,128)} %get-tuple-element.250), channel_id=1, source_target_pairs={{0,8},{8,16},{16,24},{1,9},{9,17},{17,25},{2,10},{10,18},{18,26},{... | collective-permute-start | bytes 2752520 | tf_op jit(solution)/shard_map/ppermute | solution.py:139
  646.7 36.6 %collective-permute-start.67 = (f32[2,64,1792]{2,1,0:T(8,128)S(1)}, f32[2,64,1792]{2,1,0:T(8,128)S(1)}, u32[]{:S(2)}, u32[]{:S(2)}) collective-permute-start(f32[2,64,1792]{2,1,0:T(8,128)S(1)} %get-tuple-element.245), channel_id=1, source_target_pairs={{0,8},{8,16},{16,24},{1,9},{9,17},{17,25},{2,10},{10,18},{18,26},{... | collective-permute-start | bytes 2752520 | tf_op jit(solution)/shard_map/ppermute | solution.py:139
  651.3 32.0 %collective-permute-start.69 = (f32[2,64,1792]{2,1,0:T(8,128)}, f32[2,64,1792]{2,1,0:T(8,128)S(1)}, u32[]{:S(2)}, u32[]{:S(2)}) collective-permute-start(f32[2,64,1792]{2,1,0:T(8,128)} %get-tuple-element.180), channel_id=1, source_target_pairs={{0,3},{1,4},{2,5},{3,6},{4,7},{5,0},{6,1},{7,2},{8,11},{9,12},{10,... | collective-permute-start | bytes 2752520 | tf_op jit(solution)/shard_map/ppermute | solution.py:65
  670.3 32.9 %collective-permute-start.70 = (f32[2,64,1792]{2,1,0:T(8,128)S(1)}, f32[2,64,1792]{2,1,0:T(8,128)S(1)}, u32[]{:S(2)}, u32[]{:S(2)}) collective-permute-start(f32[2,64,1792]{2,1,0:T(8,128)S(1)} %get-tuple-element.244), channel_id=1, source_target_pairs={{0,8},{8,16},{16,24},{1,9},{9,17},{17,25},{2,10},{10,18},{18,26},{... | collective-permute-start | bytes 2752520 | tf_op jit(solution)/shard_map/ppermute | solution.py:139
  674.9 38.9 %collective-permute-start.71 = (f32[2,64,1792]{2,1,0:T(8,128)S(1)}, f32[2,64,1792]{2,1,0:T(8,128)S(1)}, u32[]{:S(2)}, u32[]{:S(2)}) collective-permute-start(f32[2,64,1792]{2,1,0:T(8,128)S(1)} %get-tuple-element.242), channel_id=1, source_target_pairs={{8,0},{16,8},{24,16},{9,1},{17,9},{25,17},{10,2},{18,10},{26,18},{... | collective-permute-start | bytes 2752520 | tf_op jit(solution)/shard_map/ppermute | solution.py:140
  729.4 32.5 %collective-permute-start.77 = (f32[2,64,1792]{2,1,0:T(8,128)S(1)}, f32[2,64,1792]{2,1,0:T(8,128)S(1)}, u32[]{:S(2)}, u32[]{:S(2)}) collective-permute-start(f32[2,64,1792]{2,1,0:T(8,128)S(1)} %collective-permute-done.72), channel_id=1, source_target_pairs={{0,8},{8,16},{16,24},{1,9},{9,17},{17,25},{2,10},{10,18},{18,26},{... | collective-permute-start | bytes 2752520 | tf_op jit(solution)/shard_map/ppermute | solution.py:139
  732.9 35.9 %collective-permute-start.78 = (f32[2,64,1792]{2,1,0:T(8,128)S(1)}, f32[2,64,1792]{2,1,0:T(8,128)S(1)}, u32[]{:S(2)}, u32[]{:S(2)}) collective-permute-start(f32[2,64,1792]{2,1,0:T(8,128)S(1)} %collective-permute-done.73), channel_id=1, source_target_pairs={{8,0},{16,8},{24,16},{9,1},{17,9},{25,17},{10,2},{18,10},{26,18},{... | collective-permute-start | bytes 2752520 | tf_op jit(solution)/shard_map/ppermute | solution.py:140
  734.2 34.6 %collective-permute-start.79 = (f32[2,64,1792]{2,1,0:T(8,128)S(1)}, f32[2,64,1792]{2,1,0:T(8,128)S(1)}, u32[]{:S(2)}, u32[]{:S(2)}) collective-permute-start(f32[2,64,1792]{2,1,0:T(8,128)S(1)} %get-tuple-element.192), channel_id=1, source_target_pairs={{0,4},{1,5},{2,6},{3,7},{4,0},{5,1},{6,2},{7,3},{8,12},{9,13},{10,... | collective-permute-start | bytes 2752520 | tf_op jit(solution)/shard_map/ppermute | solution.py:65
  749.0 32.5 %collective-permute-start.82 = (f32[2,64,1792]{2,1,0:T(8,128)S(1)}, f32[2,64,1792]{2,1,0:T(8,128)S(1)}, u32[]{:S(2)}, u32[]{:S(2)}) collective-permute-start(f32[2,64,1792]{2,1,0:T(8,128)S(1)} %collective-permute-done.75), channel_id=1, source_target_pairs={{0,8},{8,16},{16,24},{1,9},{9,17},{17,25},{2,10},{10,18},{18,26},{... | collective-permute-start | bytes 2752520 | tf_op jit(solution)/shard_map/ppermute | solution.py:139
  752.5 35.9 %collective-permute-start.83 = (f32[2,64,1792]{2,1,0:T(8,128)S(1)}, f32[2,64,1792]{2,1,0:T(8,128)S(1)}, u32[]{:S(2)}, u32[]{:S(2)}) collective-permute-start(f32[2,64,1792]{2,1,0:T(8,128)S(1)} %collective-permute-done.76), channel_id=1, source_target_pairs={{8,0},{16,8},{24,16},{9,1},{17,9},{25,17},{10,2},{18,10},{26,18},{... | collective-permute-start | bytes 2752520 | tf_op jit(solution)/shard_map/ppermute | solution.py:140
  768.7 39.3 %collective-permute-start.80 = (f32[2,64,1792]{2,1,0:T(8,128)S(1)}, f32[2,64,1792]{2,1,0:T(8,128)S(1)}, u32[]{:S(2)}, u32[]{:S(2)}) collective-permute-start(f32[2,64,1792]{2,1,0:T(8,128)S(1)} %collective-permute-done.78), channel_id=1, source_target_pairs={{8,0},{16,8},{24,16},{9,1},{17,9},{25,17},{10,2},{18,10},{26,18},{... | collective-permute-start | bytes 2752520 | tf_op jit(solution)/shard_map/ppermute | solution.py:140
  771.0 41.6 %collective-permute-start.81 = (f32[2,64,1792]{2,1,0:T(8,128)S(1)}, f32[2,64,1792]{2,1,0:T(8,128)S(1)}, u32[]{:S(2)}, u32[]{:S(2)}) collective-permute-start(f32[2,64,1792]{2,1,0:T(8,128)S(1)} %collective-permute-done.77), channel_id=1, source_target_pairs={{0,8},{8,16},{16,24},{1,9},{9,17},{17,25},{2,10},{10,18},{18,26},{... | collective-permute-start | bytes 2752520 | tf_op jit(solution)/shard_map/ppermute | solution.py:139
  788.4 37.8 %collective-permute-start.84 = (f32[2,64,1792]{2,1,0:T(8,128)S(1)}, f32[2,64,1792]{2,1,0:T(8,128)S(1)}, u32[]{:S(2)}, u32[]{:S(2)}) collective-permute-start(f32[2,64,1792]{2,1,0:T(8,128)S(1)} %collective-permute-done.83), channel_id=1, source_target_pairs={{8,0},{16,8},{24,16},{9,1},{17,9},{25,17},{10,2},{18,10},{26,18},{... | collective-permute-start | bytes 2752520 | tf_op jit(solution)/shard_map/ppermute | solution.py:140
  789.7 41.1 %collective-permute-start.85 = (f32[2,64,1792]{2,1,0:T(8,128)S(1)}, f32[2,64,1792]{2,1,0:T(8,128)S(1)}, u32[]{:S(2)}, u32[]{:S(2)}) collective-permute-start(f32[2,64,1792]{2,1,0:T(8,128)S(1)} %collective-permute-done.82), channel_id=1, source_target_pairs={{0,8},{8,16},{16,24},{1,9},{9,17},{17,25},{2,10},{10,18},{18,26},{... | collective-permute-start | bytes 2752520 | tf_op jit(solution)/shard_map/ppermute | solution.py:139
  (82 other events, 2631.8 us)

commit v6 on v5

--- a/solution.py
+++ b/solution.py
@@ -75,18 +75,22 @@
         return array
 
     def after(first, *arrays):
-        return lax.optimization_barrier((first, *arrays))[1:]
+        return lax.optimization_barrier((*first, *arrays))[len(first) :]
 
     order = [[(stream * turns + turn + 1) % steps for turn in range(turns)] for stream in range(STREAMS)]
     zero = jnp.zeros((2, merge * q_rows, col_count), jnp.float32)
     from_left, from_right = [zero] * STREAMS, [zero] * STREAMS
     arrived_left, arrived_right = [[]] * STREAMS, [[]] * STREAMS
     moved, outgoing, transit = {}, {}, []
-    payload = zero
+    payload = (zero,)
 
     def fetch(step):
-        parts = [lax.dynamic_slice_in_dim(held, lane(plane - shift), 1, 1)[:, 0] for shift in shifts_of(step)]
-        parts = after(payload, *parts)
+        (here,) = after(payload, place)
+        parts = []
+        for shift in shifts_of(step):
+            at = lax.rem(here + plane - shift, plane)
+            halves = [lax.dynamic_slice(held, (matrix, at, 0, 0), (1, 1) + block)[0] for matrix in range(2)]
+            parts.append(jnp.concatenate(halves, axis=0))
         return ("fetch", step, [rotate(part, -shift) for part, shift in zip(parts, shifts_of(step))])
 
     def deliver(step):
@@ -135,7 +139,7 @@
                         new_held = land(new_held, *deliver(step)[1:])
                     new_weights = write_weights(new_weights, group, step, update)
                     to_right = to_left = update
-                payload = to_right
+                payload = (to_right, to_left)
                 from_left[stream] = lax.ppermute(to_right, "grp", rightward)
                 from_right[stream] = lax.ppermute(to_left, "grp", leftward)
                 slot = in_turn // 2

time: 837 us -> 733 us (0.88)
  waiting for transfers between devices: 433 us -> 319 us
  other arithmetic: 166 us -> 188 us
  starting transfers between devices: 212 us -> 198 us
    ppermute x36, waiting for transfers between devices: 406 us -> 226 us  [body(): from_right[stream] = lax.ppermute(to_left, 'grp', leftward)]
    ppermute x36, waiting for transfers between devices: 27.2 us -> 89.1 us  [body(): from_left[stream] = lax.ppermute(to_right, 'grp', rightward)]
    ppermute x36, starting transfers between devices: 156 us -> 135 us  [body(): from_left[stream] = lax.ppermute(to_right, 'grp', rightward)]
    select_n x14 -> x18, other arithmetic: 51 us -> 61.1 us  [body(): jnp.where(groups - 1 - group < phase, to_left + own(left_owner, step), to...]
    select_n x10 -> x6, other arithmetic: 26.1 us -> 21.7 us  [body(): jnp.where(group < phase, to_right + own(right_owner, step), to_right)]
  transfers between devices with their start and end apart: 86 -> 86, of which waited for: 44 -> 56; matrix products, arithmetic and copies ran while one was open for 22% -> 28% of each run, Pallas kernels for 0% -> 0%
where the time goes in v6:
time: 733 us; the launch traced here: 729 us
  waiting for transfers between devices  319 us (44%)
  starting transfers between devices  198 us (27%)
  other arithmetic  188 us (26%)
  local copies, waits for them, and re-layouts  23.6 us (3%)
    ppermute x36, waiting for transfers between devices, body(): from_right[stream] = lax.ppermute(to_left, 'grp', leftward)  226 us
    ppermute x36, starting transfers between devices, body(): from_left[stream] = lax.ppermute(to_right, 'grp', rightward)  135 us
    ppermute x36, waiting for transfers between devices, body(): from_left[stream] = lax.ppermute(to_right, 'grp', rightward)  89.1 us
    dynamic_update_slice x32, other arithmetic, write_weights(): array = lax.dynamic_update_slice(array, old - part[:, None, None], at)  76.1 us
    select_n x18, other arithmetic, body(): jnp.where(groups - 1 - group < phase, to_left + own(left_owner, step), to...  61.1 us
    ppermute x36, starting transfers between devices, body(): from_right[stream] = lax.ppermute(to_left, 'grp', leftward)  46.7 us
    add x8, other arithmetic, body(): new_momentum = MOMENTUM_COEF * moved[step] + mean_diff  22.6 us
    select_n x6, other arithmetic, body(): jnp.where(group < phase, to_right + own(right_owner, step), to_right)  21.7 us
  transfers between devices with their start and end apart: 86, of which 56 were waited for; matrix products, arithmetic and copies ran while one was open for 28% of the time, Pallas kernels for 0%

profile of v6, /device:TPU:0, one launch (start us, length us, event | category | flops | bytes accessed | tf_op | source)
XLA Modules:
  0.0 728.9 jit_solution(3400943628155832581)
XLA Ops:
  4.2 5.8 collective-permute-start
  49.9 5.3 collective-permute-done.4
  63.2 6.3 collective-permute-done.5
  83.8 5.4 collective-permute-done.8
  101.1 7.8 %collective-permute-done.10 = f32[2,64,1792]{2,1,0:T(8,128)} collective-permute-done((f32[2,64,1792]{2,1,0:T(8,128)}, f32[2,64,1792]{2,1,0:T(8,128)}, u32[]{:S(2)}, u32[]{:S(2)}) %collective-permute-start.10) | collective-permute-done | bytes 917536 | tf_op jit(solution)/shard_map/ppermute | solution.py:143
  108.8 5.3 collective-permute-done.11
  128.4 5.3 collective-permute-done.13
  198.2 5.5 collective-permute-start.22
  217.9 5.5 collective-permute-start.26
  223.4 8.8 %collective-permute-done.21 = f32[2,64,1792]{2,1,0:T(8,128)} collective-permute-done((f32[2,64,1792]{2,1,0:T(8,128)}, f32[2,64,1792]{2,1,0:T(8,128)}, u32[]{:S(2)}, u32[]{:S(2)}) %collective-permute-start.21) | collective-permute-done | bytes 917536 | tf_op jit(solution)/shard_map/ppermute | solution.py:144
  239.0 12.8 %collective-permute-done.25 = f32[2,64,1792]{2,1,0:T(8,128)} collective-permute-done((f32[2,64,1792]{2,1,0:T(8,128)}, f32[2,64,1792]{2,1,0:T(8,128)}, u32[]{:S(2)}, u32[]{:S(2)}) %collective-permute-start.25) | collective-permute-done | bytes 917536 | tf_op jit(solution)/shard_map/ppermute | solution.py:144
  284.7 5.7 collective-permute-done.32
  304.3 5.9 collective-permute-done.34
  324.0 5.8 collective-permute-done.37
  338.1 5.6 collective-permute-done.38
  343.7 5.9 collective-permute-done.39
  355.0 5.5 collective-permute-start.42
  363.4 5.9 collective-permute-done.44
  374.6 5.5 collective-permute-start.46
  380.2 8.7 %collective-permute-done.41 = f32[2,64,1792]{2,1,0:T(8,128)} collective-permute-done((f32[2,64,1792]{2,1,0:T(8,128)}, f32[2,64,1792]{2,1,0:T(8,128)}, u32[]{:S(2)}, u32[]{:S(2)}) %collective-permute-start.41) | collective-permute-done | bytes 917536 | tf_op jit(solution)/shard_map/ppermute | solution.py:144
  395.0 13.5 %collective-permute-done.45 = f32[2,64,1792]{2,1,0:T(8,128)} collective-permute-done((f32[2,64,1792]{2,1,0:T(8,128)}, f32[2,64,1792]{2,1,0:T(8,128)}, u32[]{:S(2)}, u32[]{:S(2)}) %collective-permute-start.45) | collective-permute-done | bytes 917536 | tf_op jit(solution)/shard_map/ppermute | solution.py:144
  442.3 5.5 collective-permute-done.52
  461.7 5.7 collective-permute-done.54
  481.5 5.6 collective-permute-done.57
  501.2 5.7 collective-permute-done.59
  520.7 5.7 collective-permute-done.64
  536.9 9.2 %collective-permute-done.61 = f32[2,64,1792]{2,1,0:T(8,128)S(1)} collective-permute-done((f32[2,64,1792]{2,1,0:T(8,128)S(1)}, f32[2,64,1792]{2,1,0:T(8,128)S(1)}, u32[]{:S(2)}, u32[]{:S(2)}) %collective-permute-start.61) | collective-permute-done | bytes 917536 | tf_op jit(solution)/shard_map/ppermute | solution.py:144
  552.7 13.1 %collective-permute-done.65 = f32[2,64,1792]{2,1,0:T(8,128)S(1)} collective-permute-done((f32[2,64,1792]{2,1,0:T(8,128)S(1)}, f32[2,64,1792]{2,1,0:T(8,128)S(1)}, u32[]{:S(2)}, u32[]{:S(2)}) %collective-permute-start.65) | collective-permute-done | bytes 917536 | tf_op jit(solution)/shard_map/ppermute | solution.py:144
  648.8 9.0 %collective-permute-done.77 = f32[2,64,1792]{2,1,0:T(8,128)S(1)} collective-permute-done((f32[2,64,1792]{2,1,0:T(8,128)S(1)}, f32[2,64,1792]{2,1,0:T(8,128)S(1)}, u32[]{:S(2)}, u32[]{:S(2)}) %collective-permute-start.77) | collective-permute-done | bytes 917536 | tf_op jit(solution)/shard_map/ppermute | solution.py:143
  670.0 7.5 %collective-permute-done.82 = f32[2,64,1792]{2,1,0:T(8,128)S(1)} collective-permute-done((f32[2,64,1792]{2,1,0:T(8,128)S(1)}, f32[2,64,1792]{2,1,0:T(8,128)S(1)}, u32[]{:S(2)}, u32[]{:S(2)}) %collective-permute-start.82) | collective-permute-done | bytes 917536 | tf_op jit(solution)/shard_map/ppermute | solution.py:143
  689.7 12.8 %collective-permute-done.80 = f32[2,64,1792]{2,1,0:T(8,128)S(1)} collective-permute-done((f32[2,64,1792]{2,1,0:T(8,128)S(1)}, f32[2,64,1792]{2,1,0:T(8,128)S(1)}, u32[]{:S(2)}, u32[]{:S(2)}) %collective-permute-start.80) | collective-permute-done | bytes 917536 | tf_op jit(solution)/shard_map/ppermute | solution.py:144
  709.3 12.8 %collective-permute-done.84 = f32[2,64,1792]{2,1,0:T(8,128)S(1)} collective-permute-done((f32[2,64,1792]{2,1,0:T(8,128)S(1)}, f32[2,64,1792]{2,1,0:T(8,128)S(1)}, u32[]{:S(2)}, u32[]{:S(2)}) %collective-permute-start.84) | collective-permute-done | bytes 917536 | tf_op jit(solution)/shard_map/ppermute | solution.py:144
  (262 shorter events, 493.1 us)
Async XLA Ops:
  61.9 32.6 %collective-permute-start.9 = (f32[2,64,1792]{2,1,0:T(8,128)}, f32[2,64,1792]{2,1,0:T(8,128)}, u32[]{:S(2)}, u32[]{:S(2)}) collective-permute-start(f32[2,64,1792]{2,1,0:T(8,128)} %get-tuple-element.282), channel_id=1, source_target_pairs={{8,0},{16,8},{24,16},{9,1},{17,9},{25,17},{10,2},{18,10},{26,18},{... | collective-permute-start | bytes 2752520 | tf_op jit(solution)/shard_map/ppermute | solution.py:144
  99.8 34.0 %collective-permute-start.13 = (f32[2,64,1792]{2,1,0:T(8,128)S(1)}, f32[2,64,1792]{2,1,0:T(8,128)S(1)}, u32[]{:S(2)}, u32[]{:S(2)}) collective-permute-start(f32[2,64,1792]{2,1,0:T(8,128)S(1)} %get-tuple-element.278), channel_id=1, source_target_pairs={{8,0},{16,8},{24,16},{9,1},{17,9},{25,17},{10,2},{18,10},{26,18},{... | collective-permute-start | bytes 2752520 | tf_op jit(solution)/shard_map/ppermute | solution.py:144
  196.9 35.2 %collective-permute-start.21 = (f32[2,64,1792]{2,1,0:T(8,128)}, f32[2,64,1792]{2,1,0:T(8,128)}, u32[]{:S(2)}, u32[]{:S(2)}) collective-permute-start(f32[2,64,1792]{2,1,0:T(8,128)} %get-tuple-element.273), channel_id=1, source_target_pairs={{8,0},{16,8},{24,16},{9,1},{17,9},{25,17},{10,2},{18,10},{26,18},{... | collective-permute-start | bytes 2752520 | tf_op jit(solution)/shard_map/ppermute | solution.py:144
  198.2 33.9 %collective-permute-start.22 = (f32[2,64,1792]{2,1,0:T(8,128)}, f32[2,64,1792]{2,1,0:T(8,128)}, u32[]{:S(2)}, u32[]{:S(2)}) collective-permute-start(f32[2,64,1792]{2,1,0:T(8,128)} %get-tuple-element.272), channel_id=1, source_target_pairs={{0,8},{8,16},{16,24},{1,9},{9,17},{17,25},{2,10},{10,18},{18,26},{... | collective-permute-start | bytes 2752520 | tf_op jit(solution)/shard_map/ppermute | solution.py:143
  216.6 35.2 %collective-permute-start.25 = (f32[2,64,1792]{2,1,0:T(8,128)}, f32[2,64,1792]{2,1,0:T(8,128)}, u32[]{:S(2)}, u32[]{:S(2)}) collective-permute-start(f32[2,64,1792]{2,1,0:T(8,128)} %get-tuple-element.271), channel_id=1, source_target_pairs={{8,0},{16,8},{24,16},{9,1},{17,9},{25,17},{10,2},{18,10},{26,18},{... | collective-permute-start | bytes 2752520 | tf_op jit(solution)/shard_map/ppermute | solution.py:144
  217.9 34.0 %collective-permute-start.26 = (f32[2,64,1792]{2,1,0:T(8,128)}, f32[2,64,1792]{2,1,0:T(8,128)}, u32[]{:S(2)}, u32[]{:S(2)}) collective-permute-start(f32[2,64,1792]{2,1,0:T(8,128)} %get-tuple-element.270), channel_id=1, source_target_pairs={{0,8},{8,16},{16,24},{1,9},{9,17},{17,25},{2,10},{10,18},{18,26},{... | collective-permute-start | bytes 2752520 | tf_op jit(solution)/shard_map/ppermute | solution.py:143
  235.0 38.2 %collective-permute-start.28 = (f32[2,64,1792]{2,1,0:T(8,128)S(1)}, f32[2,64,1792]{2,1,0:T(8,128)S(1)}, u32[]{:S(2)}, u32[]{:S(2)}) collective-permute-start(f32[2,64,1792]{2,1,0:T(8,128)S(1)} %get-tuple-element.269), channel_id=1, source_target_pairs={{0,8},{8,16},{16,24},{1,9},{9,17},{17,25},{2,10},{10,18},{18,26},{... | collective-permute-start | bytes 2752520 | tf_op jit(solution)/shard_map/ppermute | solution.py:143
  237.7 35.6 %collective-permute-start.29 = (f32[2,64,1792]{2,1,0:T(8,128)S(1)}, f32[2,64,1792]{2,1,0:T(8,128)S(1)}, u32[]{:S(2)}, u32[]{:S(2)}) collective-permute-start(f32[2,64,1792]{2,1,0:T(8,128)S(1)} %get-tuple-element.268), channel_id=1, source_target_pairs={{8,0},{16,8},{24,16},{9,1},{17,9},{25,17},{10,2},{18,10},{26,18},{... | collective-permute-start | bytes 2752520 | tf_op jit(solution)/shard_map/ppermute | solution.py:144
  257.3 33.1 %collective-permute-start.32 = (f32[2,64,1792]{2,1,0:T(8,128)S(1)}, f32[2,64,1792]{2,1,0:T(8,128)S(1)}, u32[]{:S(2)}, u32[]{:S(2)}) collective-permute-start(f32[2,64,1792]{2,1,0:T(8,128)S(1)} %get-tuple-element.266), channel_id=1, source_target_pairs={{8,0},{16,8},{24,16},{9,1},{17,9},{25,17},{10,2},{18,10},{26,18},{... | collective-permute-start | bytes 2752520 | tf_op jit(solution)/shard_map/ppermute | solution.py:144
  336.8 32.5 %collective-permute-start.44 = (f32[2,64,1792]{2,1,0:T(8,128)}, f32[2,64,1792]{2,1,0:T(8,128)}, u32[]{:S(2)}, u32[]{:S(2)}) collective-permute-start(f32[2,64,1792]{2,1,0:T(8,128)} %get-tuple-element.262), channel_id=1, source_target_pairs={{8,0},{16,8},{24,16},{9,1},{17,9},{25,17},{10,2},{18,10},{26,18},{... | collective-permute-start | bytes 2752520 | tf_op jit(solution)/shard_map/ppermute | solution.py:144
  353.7 35.2 %collective-permute-start.41 = (f32[2,64,1792]{2,1,0:T(8,128)}, f32[2,64,1792]{2,1,0:T(8,128)}, u32[]{:S(2)}, u32[]{:S(2)}) collective-permute-start(f32[2,64,1792]{2,1,0:T(8,128)} %get-tuple-element.261), channel_id=1, source_target_pairs={{8,0},{16,8},{24,16},{9,1},{17,9},{25,17},{10,2},{18,10},{26,18},{... | collective-permute-start | bytes 2752520 | tf_op jit(solution)/shard_map/ppermute | solution.py:144
  355.0 33.9 %collective-permute-start.42 = (f32[2,64,1792]{2,1,0:T(8,128)}, f32[2,64,1792]{2,1,0:T(8,128)}, u32[]{:S(2)}, u32[]{:S(2)}) collective-permute-start(f32[2,64,1792]{2,1,0:T(8,128)} %get-tuple-element.260), channel_id=1, source_target_pairs={{0,8},{8,16},{16,24},{1,9},{9,17},{17,25},{2,10},{10,18},{18,26},{... | collective-permute-start | bytes 2752520 | tf_op jit(solution)/shard_map/ppermute | solution.py:143
  373.4 35.2 %collective-permute-start.45 = (f32[2,64,1792]{2,1,0:T(8,128)}, f32[2,64,1792]{2,1,0:T(8,128)}, u32[]{:S(2)}, u32[]{:S(2)}) collective-permute-start(f32[2,64,1792]{2,1,0:T(8,128)} %get-tuple-element.259), channel_id=1, source_target_pairs={{8,0},{16,8},{24,16},{9,1},{17,9},{25,17},{10,2},{18,10},{26,18},{... | collective-permute-start | bytes 2752520 | tf_op jit(solution)/shard_map/ppermute | solution.py:144
  374.6 33.9 %collective-permute-start.46 = (f32[2,64,1792]{2,1,0:T(8,128)}, f32[2,64,1792]{2,1,0:T(8,128)}, u32[]{:S(2)}, u32[]{:S(2)}) collective-permute-start(f32[2,64,1792]{2,1,0:T(8,128)} %get-tuple-element.258), channel_id=1, source_target_pairs={{0,8},{8,16},{16,24},{1,9},{9,17},{17,25},{2,10},{10,18},{18,26},{... | collective-permute-start | bytes 2752520 | tf_op jit(solution)/shard_map/ppermute | solution.py:143
  391.8 39.1 %collective-permute-start.48 = (f32[2,64,1792]{2,1,0:T(8,128)S(1)}, f32[2,64,1792]{2,1,0:T(8,128)S(1)}, u32[]{:S(2)}, u32[]{:S(2)}) collective-permute-start(f32[2,64,1792]{2,1,0:T(8,128)S(1)} %get-tuple-element.257), channel_id=1, source_target_pairs={{0,8},{8,16},{16,24},{1,9},{9,17},{17,25},{2,10},{10,18},{18,26},{... | collective-permute-start | bytes 2752520 | tf_op jit(solution)/shard_map/ppermute | solution.py:143
  393.7 37.2 %collective-permute-start.49 = (f32[2,64,1792]{2,1,0:T(8,128)S(1)}, f32[2,64,1792]{2,1,0:T(8,128)S(1)}, u32[]{:S(2)}, u32[]{:S(2)}) collective-permute-start(f32[2,64,1792]{2,1,0:T(8,128)S(1)} %get-tuple-element.256), channel_id=1, source_target_pairs={{8,0},{16,8},{24,16},{9,1},{17,9},{25,17},{10,2},{18,10},{26,18},{... | collective-permute-start | bytes 2752520 | tf_op jit(solution)/shard_map/ppermute | solution.py:144
  415.0 32.8 %collective-permute-start.52 = (f32[2,64,1792]{2,1,0:T(8,128)S(1)}, f32[2,64,1792]{2,1,0:T(8,128)S(1)}, u32[]{:S(2)}, u32[]{:S(2)}) collective-permute-start(f32[2,64,1792]{2,1,0:T(8,128)S(1)} %get-tuple-element.254), channel_id=1, source_target_pairs={{8,0},{16,8},{24,16},{9,1},{17,9},{25,17},{10,2},{18,10},{26,18},{... | collective-permute-start | bytes 2752520 | tf_op jit(solution)/shard_map/ppermute | solution.py:144
  512.0 34.1 %collective-permute-start.61 = (f32[2,64,1792]{2,1,0:T(8,128)S(1)}, f32[2,64,1792]{2,1,0:T(8,128)S(1)}, u32[]{:S(2)}, u32[]{:S(2)}) collective-permute-start(f32[2,64,1792]{2,1,0:T(8,128)S(1)} %get-tuple-element.249), channel_id=1, source_target_pairs={{8,0},{16,8},{24,16},{9,1},{17,9},{25,17},{10,2},{18,10},{26,18},{... | collective-permute-start | bytes 2752520 | tf_op jit(solution)/shard_map/ppermute | solution.py:144
  513.3 32.8 %collective-permute-start.62 = (f32[2,64,1792]{2,1,0:T(8,128)S(1)}, f32[2,64,1792]{2,1,0:T(8,128)S(1)}, u32[]{:S(2)}, u32[]{:S(2)}) collective-permute-start(f32[2,64,1792]{2,1,0:T(8,128)S(1)} %get-tuple-element.248), channel_id=1, source_target_pairs={{0,8},{8,16},{16,24},{1,9},{9,17},{17,25},{2,10},{10,18},{18,26},{... | collective-permute-start | bytes 2752520 | tf_op jit(solution)/shard_map/ppermute | solution.py:143
  528.8 36.9 %collective-permute-start.65 = (f32[2,64,1792]{2,1,0:T(8,128)S(1)}, f32[2,64,1792]{2,1,0:T(8,128)S(1)}, u32[]{:S(2)}, u32[]{:S(2)}) collective-permute-start(f32[2,64,1792]{2,1,0:T(8,128)S(1)} %get-tuple-element.247), channel_id=1, source_target_pairs={{8,0},{16,8},{24,16},{9,1},{17,9},{25,17},{10,2},{18,10},{26,18},{... | collective-permute-start | bytes 2752520 | tf_op jit(solution)/shard_map/ppermute | solution.py:144
  530.1 35.7 %collective-permute-start.66 = (f32[2,64,1792]{2,1,0:T(8,128)S(1)}, f32[2,64,1792]{2,1,0:T(8,128)S(1)}, u32[]{:S(2)}, u32[]{:S(2)}) collective-permute-start(f32[2,64,1792]{2,1,0:T(8,128)S(1)} %get-tuple-element.246), channel_id=1, source_target_pairs={{0,8},{8,16},{16,24},{1,9},{9,17},{17,25},{2,10},{10,18},{18,26},{... | collective-permute-start | bytes 2752520 | tf_op jit(solution)/shard_map/ppermute | solution.py:143
  548.5 39.7 %collective-permute-start.67 = (f32[2,64,1792]{2,1,0:T(8,128)S(1)}, f32[2,64,1792]{2,1,0:T(8,128)S(1)}, u32[]{:S(2)}, u32[]{:S(2)}) collective-permute-start(f32[2,64,1792]{2,1,0:T(8,128)S(1)} %get-tuple-element.245), channel_id=1, source_target_pairs={{0,8},{8,16},{16,24},{1,9},{9,17},{17,25},{2,10},{10,18},{18,26},{... | collective-permute-start | bytes 2752520 | tf_op jit(solution)/shard_map/ppermute | solution.py:143
  551.1 37.0 %collective-permute-start.68 = (f32[2,64,1792]{2,1,0:T(8,128)S(1)}, f32[2,64,1792]{2,1,0:T(8,128)S(1)}, u32[]{:S(2)}, u32[]{:S(2)}) collective-permute-start(f32[2,64,1792]{2,1,0:T(8,128)S(1)} %get-tuple-element.244), channel_id=1, source_target_pairs={{8,0},{16,8},{24,16},{9,1},{17,9},{25,17},{10,2},{18,10},{26,18},{... | collective-permute-start | bytes 2752520 | tf_op jit(solution)/shard_map/ppermute | solution.py:144
  623.8 34.0 %collective-permute-start.77 = (f32[2,64,1792]{2,1,0:T(8,128)S(1)}, f32[2,64,1792]{2,1,0:T(8,128)S(1)}, u32[]{:S(2)}, u32[]{:S(2)}) collective-permute-start(f32[2,64,1792]{2,1,0:T(8,128)S(1)} %collective-permute-done.72), channel_id=1, source_target_pairs={{0,8},{8,16},{16,24},{1,9},{9,17},{17,25},{2,10},{10,18},{18,26},{... | collective-permute-start | bytes 2752520 | tf_op jit(solution)/shard_map/ppermute | solution.py:143
  626.9 36.2 %collective-permute-start.78 = (f32[2,64,1792]{2,1,0:T(8,128)S(1)}, f32[2,64,1792]{2,1,0:T(8,128)S(1)}, u32[]{:S(2)}, u32[]{:S(2)}) collective-permute-start(f32[2,64,1792]{2,1,0:T(8,128)S(1)} %collective-permute-done.73), channel_id=1, source_target_pairs={{8,0},{16,8},{24,16},{9,1},{17,9},{25,17},{10,2},{18,10},{26,18},{... | collective-permute-start | bytes 2752520 | tf_op jit(solution)/shard_map/ppermute | solution.py:144
  628.2 34.9 %collective-permute-start.79 = (f32[2,64,1792]{2,1,0:T(8,128)}, f32[2,64,1792]{2,1,0:T(8,128)S(1)}, u32[]{:S(2)}, u32[]{:S(2)}) collective-permute-start(f32[2,64,1792]{2,1,0:T(8,128)} %get-tuple-element.193), channel_id=1, source_target_pairs={{0,4},{1,5},{2,6},{3,7},{4,0},{5,1},{6,2},{7,3},{8,12},{9,13},{10,... | collective-permute-start | bytes 2752520 | tf_op jit(solution)/shard_map/ppermute | solution.py:65
  643.5 34.0 %collective-permute-start.82 = (f32[2,64,1792]{2,1,0:T(8,128)S(1)}, f32[2,64,1792]{2,1,0:T(8,128)S(1)}, u32[]{:S(2)}, u32[]{:S(2)}) collective-permute-start(f32[2,64,1792]{2,1,0:T(8,128)S(1)} %collective-permute-done.75), channel_id=1, source_target_pairs={{0,8},{8,16},{16,24},{1,9},{9,17},{17,25},{2,10},{10,18},{18,26},{... | collective-permute-start | bytes 2752520 | tf_op jit(solution)/shard_map/ppermute | solution.py:143
  646.6 36.2 %collective-permute-start.83 = (f32[2,64,1792]{2,1,0:T(8,128)S(1)}, f32[2,64,1792]{2,1,0:T(8,128)S(1)}, u32[]{:S(2)}, u32[]{:S(2)}) collective-permute-start(f32[2,64,1792]{2,1,0:T(8,128)S(1)} %collective-permute-done.76), channel_id=1, source_target_pairs={{8,0},{16,8},{24,16},{9,1},{17,9},{25,17},{10,2},{18,10},{26,18},{... | collective-permute-start | bytes 2752520 | tf_op jit(solution)/shard_map/ppermute | solution.py:144
  663.1 39.3 %collective-permute-start.80 = (f32[2,64,1792]{2,1,0:T(8,128)S(1)}, f32[2,64,1792]{2,1,0:T(8,128)S(1)}, u32[]{:S(2)}, u32[]{:S(2)}) collective-permute-start(f32[2,64,1792]{2,1,0:T(8,128)S(1)} %collective-permute-done.78), channel_id=1, source_target_pairs={{8,0},{16,8},{24,16},{9,1},{17,9},{25,17},{10,2},{18,10},{26,18},{... | collective-permute-start | bytes 2752520 | tf_op jit(solution)/shard_map/ppermute | solution.py:144
  665.4 41.6 %collective-permute-start.81 = (f32[2,64,1792]{2,1,0:T(8,128)S(1)}, f32[2,64,1792]{2,1,0:T(8,128)S(1)}, u32[]{:S(2)}, u32[]{:S(2)}) collective-permute-start(f32[2,64,1792]{2,1,0:T(8,128)S(1)} %collective-permute-done.77), channel_id=1, source_target_pairs={{0,8},{8,16},{16,24},{1,9},{9,17},{17,25},{2,10},{10,18},{18,26},{... | collective-permute-start | bytes 2752520 | tf_op jit(solution)/shard_map/ppermute | solution.py:143
  682.8 39.3 %collective-permute-start.84 = (f32[2,64,1792]{2,1,0:T(8,128)S(1)}, f32[2,64,1792]{2,1,0:T(8,128)S(1)}, u32[]{:S(2)}, u32[]{:S(2)}) collective-permute-start(f32[2,64,1792]{2,1,0:T(8,128)S(1)} %collective-permute-done.83), channel_id=1, source_target_pairs={{8,0},{16,8},{24,16},{9,1},{17,9},{25,17},{10,2},{18,10},{26,18},{... | collective-permute-start | bytes 2752520 | tf_op jit(solution)/shard_map/ppermute | solution.py:144
  684.1 42.6 %collective-permute-start.85 = (f32[2,64,1792]{2,1,0:T(8,128)S(1)}, f32[2,64,1792]{2,1,0:T(8,128)S(1)}, u32[]{:S(2)}, u32[]{:S(2)}) collective-permute-start(f32[2,64,1792]{2,1,0:T(8,128)S(1)} %collective-permute-done.82), channel_id=1, source_target_pairs={{0,8},{8,16},{16,24},{1,9},{9,17},{17,25},{2,10},{10,18},{18,26},{... | collective-permute-start | bytes 2752520 | tf_op jit(solution)/shard_map/ppermute | solution.py:143
  (70 other events, 2130.4 us)

commit v7 on v0

v7 whole, which is shorter than its diff:
```python
import jax
import jax.numpy as jnp
from jax import lax
from jax.experimental import pallas as pl
from jax.sharding import PartitionSpec as P

OUTER_RATE = 0.7
MOMENTUM_COEF = 0.5
BLOCKS = 4
CUTS = 3
ORDER = ((1, 3), (2, 0))


def blank(shape):
    return pl.pallas_call(
        lambda out: None,
        out_shape=jax.ShapeDtypeStruct(shape, jnp.float32),
        out_specs=pl.BlockSpec(memory_space=pl.ANY),
    )()


def mix(adds, term, passed):
    width = max(term.shape[2], passed.shape[2])
    term, passed = [jnp.pad(array, ((0, 0), (0, 0), (0, width - array.shape[2]))) for array in (term, passed)]
    return jnp.where(adds, passed + term, passed)


def body(inner_weights, start_weights, momentum):
    groups = lax.axis_size("grp")
    plane = lax.axis_size("shard") * lax.axis_size("tp")
    group = lax.axis_index("grp")
    place = lax.axis_index(("shard", "tp"))
    row_count, col_count = start_weights.shape[1:]
    lanes = plane // BLOCKS
    q_rows = row_count // (groups * plane)
    rows = lanes * q_rows
    streams = len(ORDER)

    inner = inner_weights.reshape(2, groups, BLOCKS, rows, col_count)
    start = start_weights.reshape(2, groups, BLOCKS, rows, col_count)
    held = momentum.reshape(2, plane, q_rows, col_count)
    rightward = [(i, i + 1) for i in range(groups - 1)]
    leftward = [(i + 1, i) for i in range(groups - 1)]

    wide = -(-col_count // (128 * CUTS)) * 128
    narrow = col_count - (CUTS - 1) * wide
    parts = []
    for blocks in ORDER:
        widths = [narrow] + [wide] * (2 * CUTS - 2) + [narrow]
        firsts = [sum(widths[at - at % CUTS : at]) for at in range(2 * CUTS)]
        parts.append([(blocks[at // CUTS], firsts[at], widths[at]) for at in range(2 * CUTS)])
    turns = 2 * CUTS

    def spot(block):
        return lax.bitwise_xor(place // lanes, block)

    def rows_of(array, owner, part):
        block, first, width = part
        return lax.dynamic_slice(array, (0, owner, spot(block), 0, first), (2, 1, 1, rows, width))[:, 0, 0]

    def own(owner, part):
        return rows_of(start, owner, part) - rows_of(inner, owner, part)

    def write_weights(array, owner, part, update):
        block, first, _ = part
        value = rows_of(start, owner, part) - update
        return lax.dynamic_update_slice(array, value[:, None, None], (0, owner, spot(block), 0, first))

    def after(first, *arrays):
        return lax.optimization_barrier((*first, *arrays))[len(first) :]

    def swap(array, key):
        (here,) = after(payload, place)
        at = lax.bitwise_xor(here, key)
        lane = jnp.stack([lax.dynamic_slice(array, (m, at, 0, 0), (1, 1, q_rows, col_count))[0, 0] for m in range(2)])
        if key == 0:
            return lane
        return lax.ppermute(lane, ("shard", "tp"), [(i, i ^ key) for i in range(plane)])

    def land(array, key, lane):
        return lax.dynamic_update_slice(array, lane[:, None], (0, lax.bitwise_xor(place, key), 0, 0))

    plan = {}
    ticks = (turns * groups + groups - 2) * streams
    for half in range(2):
        keys = [ORDER[stream][half] * lanes + r for stream in range(streams) for r in reversed(range(lanes))]
        for at, key in enumerate(keys):
            need = (half * CUTS + 1) * groups * streams - streams + at // lanes
            ready = ((half + 1) * CUTS * groups - 1) * streams
            if half == 0:
                fetch = min(4 * at // lanes, need - 1)
                deliver = ready + 2 + 8 * at // lanes
            else:
                fetch = groups * streams + 8 * at // lanes
                deliver = min(ready + 4 * at // lanes, ticks - 1)
            plan.setdefault(fetch, []).append(("fetch", key, min(fetch + 2 + half, need)))
            plan.setdefault(deliver, []).append(("deliver", key, deliver + 3 - half))

    new_weights = blank(start.shape)
    new_held = blank(held.shape)
    old, new = blank(held.shape), blank(held.shape)
    payload = (place,)
    zero = jnp.zeros((2, rows, narrow), jnp.float32)
    from_left, from_right = [zero] * streams, [zero] * streams
    arrived_left, arrived_right = [[] for _ in ORDER], [[] for _ in ORDER]
    transit = []

    for tick in range(ticks):
        turn, phase, stream = tick // (groups * streams), tick // streams % groups + 1, tick % streams
        landed = [entry for entry in transit if entry[2] <= tick]
        transit = [entry for entry in transit if entry[2] > tick]
        values = after(payload, from_left[stream], from_right[stream], *[entry[3] for entry in landed])
        here_left, here_right = values[:2]
        for (kind, key, _, _), lane in zip(landed, values[2:]):
            if kind == "fetch":
                old = land(old, key, lane)
            else:
                new_held = land(new_held, key, lane)
        part = parts[stream][turn] if turn < turns else None
        if phase < groups:
            to_right, to_left = here_left, here_right
            if turn < turns:
                right_owner = jnp.minimum(groups - phase + group, groups - 1)
                left_owner = jnp.maximum(group - (groups - phase), 0)
                to_right = mix(group < phase, own(right_owner, part), to_right)
                to_left = mix(groups - 1 - group < phase, own(left_owner, part), to_left)
        else:
            block, first, width = part
            total = own(group, part) + here_left[:, :, :width] + here_right[:, :, :width]
            mean_diff = total / groups
            mine = old.reshape(2, BLOCKS, rows, col_count)
            old_momentum = lax.dynamic_slice(mine, (0, spot(block), 0, first), (2, 1, rows, width))[:, 0]
            new_momentum = MOMENTUM_COEF * old_momentum + mean_diff
            update = OUTER_RATE * (mean_diff + MOMENTUM_COEF * new_momentum)
            mine = new.reshape(2, BLOCKS, rows, col_count)
            mine = lax.dynamic_update_slice(mine, new_momentum[:, None], (0, spot(block), 0, first))
            new = mine.reshape(held.shape)
            new_weights = write_weights(new_weights, group, part, update)
            to_right = to_left = update
        payload = (to_right, to_left)
        from_left[stream] = lax.ppermute(to_right, "grp", rightward)
        from_right[stream] = lax.ppermute(to_left, "grp", leftward)
        for kind, key, use in plan.get(tick, []):
            transit.append((kind, key, use, swap(held if kind == "fetch" else new, key)))
        if phase == groups:
            arrived_left[stream], arrived_right[stream] = [], []
        arrived_left[stream].append(from_left[stream])
        arrived_right[stream].append(from_right[stream])
        if len(arrived_left[stream]) == groups - 1 and turn > 0:
            part = parts[stream][turn - 1]
            width = part[2]
            for hop in range(groups - 1):
                update = jnp.where(
                    group > hop,
                    arrived_left[stream][hop][:, :, :width],
                    arrived_right[stream][groups - 2 - hop][:, :, :width],
                )
                owner = lax.rem(group + groups - 1 - hop, groups)
                new_weights = write_weights(new_weights, owner, part, update)
    for _, key, _, lane in transit:
        new_held = land(new_held, key, lane)
    return (new_weights.reshape(start_weights.shape), new_held.reshape(momentum.shape))


def solution(mesh):
    in_specs = (
        P("grp", None, "shard", "tp"),
        P(None, "shard", "tp"),
        P(None, None, None, ("grp", "shard", "tp"), None, None),
    )
    out_specs = (P(None, "shard", "tp"), P(None, None, None, ("grp", "shard", "tp"), None, None))
    return jax.shard_map(body, mesh=mesh, in_specs=in_specs, out_specs=out_specs, check_vma=False)
```

time: 1330 us -> 811 us (0.61); the launches traced: 1330 us -> 799 us
  blocking collectives: 727 us -> 0 us
  starting transfers between devices: 0.04 us -> 297 us
  waiting for transfers between devices: 492 us -> 213 us
  other arithmetic: 83.7 us -> 240 us
  local copies, waits for them, and re-layouts: 15.9 us -> 45.3 us
    all_to_all x2 -> x0, blocking collectives: 727 us -> none  [the longest x1 640 us: body(): lax.all_to_all(pieces, ('grp', 'shard', 'tp'), split_axis=1, concat_axis=...]
    all_gather x1 -> x0, waiting for transfers between devices: 492 us -> none  [body(): gathered = lax.all_gather(own_part, 'grp', axis=1, tiled=True)]
    ppermute x0 -> x118, starting transfers between devices: none -> 297 us  [the longest x52 208 us: body(): from_left[stream] = lax.ppermute(to_right, 'grp', rightward)]
    ppermute x0 -> x118, waiting for transfers between devices: none -> 213 us  [the longest x52 135 us: body(): from_right[stream] = lax.ppermute(to_left, 'grp', leftward)]
    dynamic_update_slice x0 -> x61, other arithmetic: none -> 138 us  [the longest x48 104 us: write_weights(): lax.dynamic_update_slice(array, value[:, None, None], (0, owner, spot(blo...]
    select_n x0 -> x42, other arithmetic: none -> 91.7 us  [mix(): return jnp.where(adds, passed + term, passed)]
    sub x2 -> x1, other arithmetic: 59.6 us -> 8.13 us  [own(): return rows_of(start, owner, part) - rows_of(inner, owner, part)]
    dynamic_update_slice x0 -> x15, local copies, waits for them, and re-layouts: none -> 22 us  [land(): lax.dynamic_update_slice(array, lane[:, None], (0, lax.bitwise_xor(place,...]
  transfers between devices with their start and end apart: 1 -> 118, of which waited for: 1 -> 57; matrix products, arithmetic and copies ran while one was open for 0% -> 33% of each run, Pallas kernels for 0% -> 0%
where the time goes in v7:
time: 811 us; the launch traced here: 799 us
  starting transfers between devices  297 us (37%)
  other arithmetic  240 us (30%)
  waiting for transfers between devices  213 us (26%)
  local copies, waits for them, and re-layouts  45.3 us (6%)
    ppermute x52, starting transfers between devices, body(): from_left[stream] = lax.ppermute(to_right, 'grp', rightward)  208 us
    ppermute x52, waiting for transfers between devices, body(): from_right[stream] = lax.ppermute(to_left, 'grp', leftward)  135 us
    dynamic_update_slice x48, other arithmetic, write_weights(): lax.dynamic_update_slice(array, value[:, None, None], (0, owner, spot(blo...  104 us
    select_n x42, other arithmetic, mix(): return jnp.where(adds, passed + term, passed)  91.7 us
    ppermute x52, starting transfers between devices, body(): from_right[stream] = lax.ppermute(to_left, 'grp', leftward)  77.4 us
    ppermute x52, waiting for transfers between devices, body(): from_left[stream] = lax.ppermute(to_right, 'grp', rightward)  55 us
    dynamic_update_slice x12, other arithmetic, body(): lax.dynamic_update_slice(mine, new_momentum[:, None], (0, spot(block), 0,...  32.9 us
    ppermute x14, waiting for transfers between devices, swap(): lax.ppermute(lane, ('shard', 'tp'), [(i, i ^ key) for i in range(plane)])  23.6 us
  transfers between devices with their start and end apart: 118, of which 57 were waited for; matrix products, arithmetic and copies ran while one was open for 33% of the time, Pallas kernels for 0%

profile of v7, /device:TPU:0, one launch (start us, length us, event | category | flops | bytes accessed | tf_op | source)
XLA Modules:
  0.0 798.7 jit_solution(10475308233611807591)
XLA Ops:
  14.8 7.1 collective-permute-done
  21.8 5.0 collective-permute-done.1
  39.5 5.3 collective-permute-start.5
  50.0 5.2 collective-permute-done.4
  80.4 4.9 collective-permute-done.10
  85.3 4.7 collective-permute-done.11
  110.1 5.5 collective-permute-done.13
  171.0 4.6 collective-permute-start.23
  186.1 4.6 collective-permute-start.28
  215.6 4.7 collective-permute-start.31
  233.1 4.7 collective-permute-start.34
  284.4 4.6 collective-permute-start.41
  300.2 5.4 collective-permute-start.46
  398.1 4.6 collective-permute-start.58
  413.3 5.4 collective-permute-start.63
  489.2 11.5 %collective-permute-start.74 = (f32[2,128,640]{2,1,0:T(8,128)}, f32[2,128,640]{2,1,0:T(8,128)}, u32[]{:S(2)}, u32[]{:S(2)}) collective-permute-start(f32[2,128,640]{2,1,0:T(8,128)} %get-tuple-element.344), channel_id=1, source_target_pairs={{8,0},{16,8},{24,16},{9,1},{17,9},{25,17},{10,2},{18,10},{26,18},{... | collective-permute-start | bytes 1966088 | tf_op jit(solution)/shard_map/ppermute | solution.py:142
  504.0 4.6 collective-permute-start.77
  513.4 5.2 collective-permute-start.76
  532.7 5.4 collective-permute-start.81
  562.8 5.2 collective-permute-start.84
  586.8 8.1 %fusion.111 = (f32[2,128,512]{2,1,0:T(8,128)S(1)}, f32[2,128,512]{2,1,0:T(8,128)S(1)}, f32[2,128,512]{2,1,0:T(8,128)S(1)}, f32[2,128,512]{2,1,0:T(8,128)S(1)}, f...) fusion(f32[2,4,4,128,1792]{4,3,2,1,0:T(8,128)} %bitcast.1864, ...), kind=kLoop, calls=%fused_computation.367 | loop fusion | flops 1572864 | bytes 18874400 | tf_op jit(solution)/shard_map/sub | solution.py:62
  600.2 4.7 collective-permute-start.89
  609.7 5.2 collective-permute-start.91
  628.0 4.6 collective-permute-start.95
  632.6 5.9 collective-permute-done.92
  646.1 6.4 collective-permute-done.96
  668.0 4.6 collective-permute-start.99
  719.8 7.5 collective-permute-done.105
  727.3 5.3 collective-permute-start.108
  749.4 7.9 collective-permute-done.110
  761.2 6.0 collective-permute-start.112
  773.1 10.8 %collective-permute-done.111 = f32[2,128,512]{2,1,0:T(8,128)} collective-permute-done((f32[2,128,512]{2,1,0:T(8,128)}, f32[2,128,512]{2,1,0:T(8,128)}, u32[]{:S(2)}, u32[]{:S(2)}) %collective-permute-start.111) | collective-permute-done | bytes 524320 | tf_op jit(solution)/shard_map/ppermute | solution.py:142
  (396 shorter events, 610.8 us)
Async XLA Ops:
  31.4 34.9 %collective-permute-start.7 = (f32[2,64,1792]{2,1,0:T(8,128)S(1)}, f32[2,64,1792]{2,1,0:T(8,128)S(1)}, u32[]{:S(2)}, u32[]{:S(2)}) collective-permute-start(f32[2,64,1792]{2,1,0:T(8,128)S(1)} %pad_maximum_fusion.1), channel_id=1, source_target_pairs={{0,2},{1,3},{2,0},{3,1},{4,6},{5,7},{6,4},{7,5},{8,10},{9,11},{10,... | collective-permute-start | bytes 2752520 | tf_op jit(solution)/shard_map/ppermute | solution.py:78
  145.3 30.3 %collective-permute-start.26 = (f32[2,64,1792]{2,1,0:T(8,128)S(1)}, f32[2,64,1792]{2,1,0:T(8,128)}, u32[]{:S(2)}, u32[]{:S(2)}) collective-permute-start(f32[2,64,1792]{2,1,0:T(8,128)S(1)} %pad_maximum_fusion.4), channel_id=1, source_target_pairs={{0,7},{1,6},{2,5},{3,4},{4,3},{5,2},{6,1},{7,0},{8,15},{9,14},{10,... | collective-permute-start | bytes 2752520 | tf_op jit(solution)/shard_map/ppermute | solution.py:78
  184.8 28.8 %collective-permute-start.27 = (f32[2,128,640]{2,1,0:T(8,128)}, f32[2,128,640]{2,1,0:T(8,128)}, u32[]{:S(2)}, u32[]{:S(2)}) collective-permute-start(f32[2,128,640]{2,1,0:T(8,128)} %get-tuple-element.375), channel_id=1, source_target_pairs={{8,0},{16,8},{24,16},{9,1},{17,9},{25,17},{10,2},{18,10},{26,18},{... | collective-permute-start | bytes 1966088 | tf_op jit(solution)/shard_map/ppermute | solution.py:142
  186.1 27.5 %collective-permute-start.28 = (f32[2,128,640]{2,1,0:T(8,128)}, f32[2,128,640]{2,1,0:T(8,128)S(1)}, u32[]{:S(2)}, u32[]{:S(2)}) collective-permute-start(f32[2,128,640]{2,1,0:T(8,128)} %get-tuple-element.374), channel_id=1, source_target_pairs={{0,8},{8,16},{16,24},{1,9},{9,17},{17,25},{2,10},{10,18},{18,26},{... | collective-permute-start | bytes 1966088 | tf_op jit(solution)/shard_map/ppermute | solution.py:141
  199.8 28.0 %collective-permute-start.29 = (f32[2,128,640]{2,1,0:T(8,128)}, f32[2,128,640]{2,1,0:T(8,128)}, u32[]{:S(2)}, u32[]{:S(2)}) collective-permute-start(f32[2,128,640]{2,1,0:T(8,128)} %get-tuple-element.373), channel_id=1, source_target_pairs={{0,8},{8,16},{16,24},{1,9},{9,17},{17,25},{2,10},{10,18},{18,26},{... | collective-permute-start | bytes 1966088 | tf_op jit(solution)/shard_map/ppermute | solution.py:141
  205.4 33.9 %collective-permute-start.33 = (f32[2,64,1792]{2,1,0:T(8,128)S(1)}, f32[2,64,1792]{2,1,0:T(8,128)S(1)}, u32[]{:S(2)}, u32[]{:S(2)}) collective-permute-start(f32[2,64,1792]{2,1,0:T(8,128)S(1)} %pad_maximum_fusion.5), channel_id=1, source_target_pairs={{0,6},{1,7},{2,4},{3,5},{4,2},{5,3},{6,0},{7,1},{8,14},{9,15},{10,... | collective-permute-start | bytes 2752520 | tf_op jit(solution)/shard_map/ppermute | solution.py:78
  262.5 26.5 %collective-permute-start.44 = (f32[2,64,1792]{2,1,0:T(8,128)}, f32[2,64,1792]{2,1,0:T(8,128)}, u32[]{:S(2)}, u32[]{:S(2)}) collective-permute-start(f32[2,64,1792]{2,1,0:T(8,128)} %pad_maximum_fusion.6), channel_id=1, source_target_pairs={{0,1},{1,0},{2,3},{3,2},{4,5},{5,4},{6,7},{7,6},{8,9},{9,8},{10,11... | collective-permute-start | bytes 2752520 | tf_op jit(solution)/shard_map/ppermute | solution.py:78
  298.9 26.6 %collective-permute-start.45 = (f32[2,128,640]{2,1,0:T(8,128)}, f32[2,128,640]{2,1,0:T(8,128)}, u32[]{:S(2)}, u32[]{:S(2)}) collective-permute-start(f32[2,128,640]{2,1,0:T(8,128)} %get-tuple-element.363), channel_id=1, source_target_pairs={{8,0},{16,8},{24,16},{9,1},{17,9},{25,17},{10,2},{18,10},{26,18},{... | collective-permute-start | bytes 1966088 | tf_op jit(solution)/shard_map/ppermute | solution.py:142
  313.5 26.5 %collective-permute-start.47 = (f32[2,128,640]{2,1,0:T(8,128)}, f32[2,128,640]{2,1,0:T(8,128)}, u32[]{:S(2)}, u32[]{:S(2)}) collective-permute-start(f32[2,128,640]{2,1,0:T(8,128)} %get-tuple-element.361), channel_id=1, source_target_pairs={{0,8},{8,16},{16,24},{1,9},{9,17},{17,25},{2,10},{10,18},{18,26},{... | collective-permute-start | bytes 1966088 | tf_op jit(solution)/shard_map/ppermute | solution.py:141
  374.3 28.3 %collective-permute-start.61 = (f32[2,64,1792]{2,1,0:T(8,128)S(1)}, f32[2,64,1792]{2,1,0:T(8,128)S(1)}, u32[]{:S(2)}, u32[]{:S(2)}) collective-permute-start(f32[2,64,1792]{2,1,0:T(8,128)S(1)} %pad_maximum_fusion.8), channel_id=1, source_target_pairs={{0,3},{1,2},{2,1},{3,0},{4,7},{5,6},{6,5},{7,4},{8,11},{9,10},{10,... | collective-permute-start | bytes 2752520 | tf_op jit(solution)/shard_map/ppermute | solution.py:78
  412.0 28.8 %collective-permute-start.62 = (f32[2,128,640]{2,1,0:T(8,128)}, f32[2,128,640]{2,1,0:T(8,128)}, u32[]{:S(2)}, u32[]{:S(2)}) collective-permute-start(f32[2,128,640]{2,1,0:T(8,128)} %get-tuple-element.351), channel_id=1, source_target_pairs={{8,0},{16,8},{24,16},{9,1},{17,9},{25,17},{10,2},{18,10},{26,18},{... | collective-permute-start | bytes 1966088 | tf_op jit(solution)/shard_map/ppermute | solution.py:142
  413.3 27.5 %collective-permute-start.63 = (f32[2,128,640]{2,1,0:T(8,128)}, f32[2,128,640]{2,1,0:T(8,128)}, u32[]{:S(2)}, u32[]{:S(2)}) collective-permute-start(f32[2,128,640]{2,1,0:T(8,128)} %get-tuple-element.350), channel_id=1, source_target_pairs={{0,8},{8,16},{16,24},{1,9},{9,17},{17,25},{2,10},{10,18},{18,26},{... | collective-permute-start | bytes 1966088 | tf_op jit(solution)/shard_map/ppermute | solution.py:141
  426.6 28.6 %collective-permute-start.64 = (f32[2,128,640]{2,1,0:T(8,128)}, f32[2,128,640]{2,1,0:T(8,128)}, u32[]{:S(2)}, u32[]{:S(2)}) collective-permute-start(f32[2,128,640]{2,1,0:T(8,128)} %get-tuple-element.349), channel_id=1, source_target_pairs={{0,8},{8,16},{16,24},{1,9},{9,17},{17,25},{2,10},{10,18},{18,26},{... | collective-permute-start | bytes 1966088 | tf_op jit(solution)/shard_map/ppermute | solution.py:141
  431.9 34.2 %collective-permute-start.68 = (f32[2,64,1792]{2,1,0:T(8,128)S(1)}, f32[2,64,1792]{2,1,0:T(8,128)S(1)}, u32[]{:S(2)}, u32[]{:S(2)}) collective-permute-start(f32[2,64,1792]{2,1,0:T(8,128)S(1)} %pad_maximum_fusion.9), channel_id=1, source_target_pairs={{0,2},{1,3},{2,0},{3,1},{4,6},{5,7},{6,4},{7,5},{8,10},{9,11},{10,... | collective-permute-start | bytes 2752520 | tf_op jit(solution)/shard_map/ppermute | solution.py:78
  471.5 30.6 %collective-permute-start.71 = (f32[2,128,640]{2,1,0:T(8,128)}, f32[2,128,640]{2,1,0:T(8,128)S(1)}, u32[]{:S(2)}, u32[]{:S(2)}) collective-permute-start(f32[2,128,640]{2,1,0:T(8,128)} %get-tuple-element.295), channel_id=1, source_target_pairs={{0,8},{8,16},{16,24},{1,9},{9,17},{17,25},{2,10},{10,18},{18,26},{... | collective-permute-start | bytes 1966088 | tf_op jit(solution)/shard_map/ppermute | solution.py:141
  512.1 30.1 %collective-permute-start.75 = (f32[2,128,640]{2,1,0:T(8,128)S(1)}, f32[2,128,640]{2,1,0:T(8,128)S(1)}, u32[]{:S(2)}, u32[]{:S(2)}) collective-permute-start(f32[2,128,640]{2,1,0:T(8,128)S(1)} %get-tuple-element.341), channel_id=1, source_target_pairs={{8,0},{16,8},{24,16},{9,1},{17,9},{25,17},{10,2},{18,10},{26,18},{... | collective-permute-start | bytes 1966088 | tf_op jit(solution)/shard_map/ppermute | solution.py:142
  513.4 28.8 %collective-permute-start.76 = (f32[2,128,640]{2,1,0:T(8,128)S(1)}, f32[2,128,640]{2,1,0:T(8,128)S(1)}, u32[]{:S(2)}, u32[]{:S(2)}) collective-permute-start(f32[2,128,640]{2,1,0:T(8,128)S(1)} %get-tuple-element.340), channel_id=1, source_target_pairs={{0,8},{8,16},{16,24},{1,9},{9,17},{17,25},{2,10},{10,18},{18,26},{... | collective-permute-start | bytes 1966088 | tf_op jit(solution)/shard_map/ppermute | solution.py:141
  531.4 28.0 %collective-permute-start.80 = (f32[2,128,640]{2,1,0:T(8,128)}, f32[2,128,640]{2,1,0:T(8,128)}, u32[]{:S(2)}, u32[]{:S(2)}) collective-permute-start(f32[2,128,640]{2,1,0:T(8,128)} %get-tuple-element.339), channel_id=1, source_target_pairs={{8,0},{16,8},{24,16},{9,1},{17,9},{25,17},{10,2},{18,10},{26,18},{... | collective-permute-start | bytes 1966088 | tf_op jit(solution)/shard_map/ppermute | solution.py:142
  532.7 26.7 %collective-permute-start.81 = (f32[2,128,640]{2,1,0:T(8,128)}, f32[2,128,640]{2,1,0:T(8,128)}, u32[]{:S(2)}, u32[]{:S(2)}) collective-permute-start(f32[2,128,640]{2,1,0:T(8,128)} %get-tuple-element.338), channel_id=1, source_target_pairs={{0,8},{8,16},{16,24},{1,9},{9,17},{17,25},{2,10},{10,18},{18,26},{... | collective-permute-start | bytes 1966088 | tf_op jit(solution)/shard_map/ppermute | solution.py:141
  546.3 29.4 %collective-permute-start.82 = (f32[2,128,640]{2,1,0:T(8,128)}, f32[2,128,640]{2,1,0:T(8,128)}, u32[]{:S(2)}, u32[]{:S(2)}) collective-permute-start(f32[2,128,640]{2,1,0:T(8,128)} %get-tuple-element.337), channel_id=1, source_target_pairs={{0,8},{8,16},{16,24},{1,9},{9,17},{17,25},{2,10},{10,18},{18,26},{... | collective-permute-start | bytes 1966088 | tf_op jit(solution)/shard_map/ppermute | solution.py:141
  552.9 42.0 %collective-permute-start.86 = (f32[2,64,1792]{2,1,0:T(8,128)}, f32[2,64,1792]{2,1,0:T(8,128)}, u32[]{:S(2)}, u32[]{:S(2)}) collective-permute-start(f32[2,64,1792]{2,1,0:T(8,128)} %pad_maximum_fusion.11), channel_id=1, source_target_pairs={{0,4},{1,5},{2,6},{3,7},{4,0},{5,1},{6,2},{7,3},{8,12},{9,13},{10,... | collective-permute-start | bytes 2752520 | tf_op jit(solution)/shard_map/ppermute | solution.py:78
  562.8 32.2 %collective-permute-start.84 = (f32[2,128,640]{2,1,0:T(8,128)}, f32[2,128,640]{2,1,0:T(8,128)}, u32[]{:S(2)}, u32[]{:S(2)}) collective-permute-start(f32[2,128,640]{2,1,0:T(8,128)} %get-tuple-element.335), channel_id=1, source_target_pairs={{0,8},{8,16},{16,24},{1,9},{9,17},{17,25},{2,10},{10,18},{18,26},{... | collective-permute-start | bytes 1966088 | tf_op jit(solution)/shard_map/ppermute | solution.py:141
  568.0 27.0 %collective-permute-start.85 = (f32[2,128,640]{2,1,0:T(8,128)}, f32[2,128,640]{2,1,0:T(8,128)}, u32[]{:S(2)}, u32[]{:S(2)}) collective-permute-start(f32[2,128,640]{2,1,0:T(8,128)} %get-tuple-element.334), channel_id=1, source_target_pairs={{8,0},{16,8},{24,16},{9,1},{17,9},{25,17},{10,2},{18,10},{26,18},{... | collective-permute-start | bytes 1966088 | tf_op jit(solution)/shard_map/ppermute | solution.py:142
  607.3 31.2 %collective-permute-start.92 = (f32[2,128,640]{2,1,0:T(8,128)S(1)}, f32[2,128,640]{2,1,0:T(8,128)S(1)}, u32[]{:S(2)}, u32[]{:S(2)}) collective-permute-start(f32[2,128,640]{2,1,0:T(8,128)S(1)} %add_select_fusion.10), channel_id=1, source_target_pairs={{8,0},{16,8},{24,16},{9,1},{17,9},{25,17},{10,2},{18,10},{26,18},{... | collective-permute-start | bytes 1966088 | tf_op jit(solution)/shard_map/ppermute | solution.py:142
  609.7 28.8 %collective-permute-start.91 = (f32[2,128,640]{2,1,0:T(8,128)S(1)}, f32[2,128,640]{2,1,0:T(8,128)S(1)}, u32[]{:S(2)}, u32[]{:S(2)}) collective-permute-start(f32[2,128,640]{2,1,0:T(8,128)S(1)} %add_select_fusion.11), channel_id=1, source_target_pairs={{0,8},{8,16},{16,24},{1,9},{9,17},{17,25},{2,10},{10,18},{18,26},{... | collective-permute-start | bytes 1966088 | tf_op jit(solution)/shard_map/ppermute | solution.py:141
  625.6 27.0 %collective-permute-start.96 = (f32[2,128,640]{2,1,0:T(8,128)S(1)}, f32[2,128,640]{2,1,0:T(8,128)S(1)}, u32[]{:S(2)}, u32[]{:S(2)}) collective-permute-start(f32[2,128,640]{2,1,0:T(8,128)S(1)} %add_select_fusion.8), channel_id=1, source_target_pairs={{8,0},{16,8},{24,16},{9,1},{17,9},{25,17},{10,2},{18,10},{26,18},{... | collective-permute-start | bytes 1966088 | tf_op jit(solution)/shard_map/ppermute | solution.py:142
  666.7 28.0 %collective-permute-start.100 = (f32[2,128,640]{2,1,0:T(8,128)S(1)}, f32[2,128,640]{2,1,0:T(8,128)S(1)}, u32[]{:S(2)}, u32[]{:S(2)}) collective-permute-start(f32[2,128,640]{2,1,0:T(8,128)S(1)} %add_select_fusion.2), channel_id=1, source_target_pairs={{8,0},{16,8},{24,16},{9,1},{17,9},{25,17},{10,2},{18,10},{26,18},{... | collective-permute-start | bytes 1966088 | tf_op jit(solution)/shard_map/ppermute | solution.py:142
  668.0 26.6 %collective-permute-start.99 = (f32[2,128,640]{2,1,0:T(8,128)S(1)}, f32[2,128,640]{2,1,0:T(8,128)S(1)}, u32[]{:S(2)}, u32[]{:S(2)}) collective-permute-start(f32[2,128,640]{2,1,0:T(8,128)S(1)} %add_select_fusion.3), channel_id=1, source_target_pairs={{0,8},{8,16},{16,24},{1,9},{9,17},{17,25},{2,10},{10,18},{18,26},{... | collective-permute-start | bytes 1966088 | tf_op jit(solution)/shard_map/ppermute | solution.py:141
  680.7 28.1 %collective-permute-start.102 = (f32[2,128,640]{2,1,0:T(8,128)S(1)}, f32[2,128,640]{2,1,0:T(8,128)}, u32[]{:S(2)}, u32[]{:S(2)}) collective-permute-start(f32[2,128,640]{2,1,0:T(8,128)S(1)} %add_select_fusion), channel_id=1, source_target_pairs={{8,0},{16,8},{24,16},{9,1},{17,9},{25,17},{10,2},{18,10},{26,18},{... | collective-permute-start | bytes 1966088 | tf_op jit(solution)/shard_map/ppermute | solution.py:142
  758.6 31.6 %collective-permute-start.115 = (f32[2,128,512]{2,1,0:T(8,128)}, f32[2,128,512]{2,1,0:T(8,128)}, u32[]{:S(2)}, u32[]{:S(2)}) collective-permute-start(f32[2,128,512]{2,1,0:T(8,128)} %collective-permute-done.114), channel_id=1, source_target_pairs={{8,0},{16,8},{24,16},{9,1},{17,9},{25,17},{10,2},{18,10},{26,18},{... | collective-permute-start | bytes 1572872 | tf_op jit(solution)/shard_map/ppermute | solution.py:142
  761.2 27.0 %collective-permute-start.112 = (f32[2,128,512]{2,1,0:T(8,128)}, f32[2,128,512]{2,1,0:T(8,128)}, u32[]{:S(2)}, u32[]{:S(2)}) collective-permute-start(f32[2,128,512]{2,1,0:T(8,128)} %collective-permute-done.108), channel_id=1, source_target_pairs={{0,8},{8,16},{16,24},{1,9},{9,17},{17,25},{2,10},{10,18},{18,26},{... | collective-permute-start | bytes 1572872 | tf_op jit(solution)/shard_map/ppermute | solution.py:141
  767.2 27.3 %collective-permute-start.116 = (f32[2,128,512]{2,1,0:T(8,128)S(1)}, f32[2,128,512]{2,1,0:T(8,128)S(1)}, u32[]{:S(2)}, u32[]{:S(2)}) collective-permute-start(f32[2,128,512]{2,1,0:T(8,128)S(1)} %collective-permute-done.113), channel_id=1, source_target_pairs={{0,8},{8,16},{16,24},{1,9},{9,17},{17,25},{2,10},{10,18},{18,26},{... | collective-permute-start | bytes 1572872 | tf_op jit(solution)/shard_map/ppermute | solution.py:141
  (105 other events, 1934.3 us)

commit v8 on v6

--- a/solution.py
+++ b/solution.py
@@ -67,11 +67,9 @@
     new_weights = blank(start.shape)
     new_held = blank(held.shape)
 
-    def write_weights(array, owner, step, update):
-        for shift, part in zip(shifts_of(step), parts_of(update)):
-            at = (0, owner, lane(shift), 0, 0)
-            old = lax.dynamic_slice(start, at, (2, 1, 1) + block)
-            array = lax.dynamic_update_slice(array, old - part[:, None, None], at)
+    def write_weights(array, owner, step, value):
+        for shift, part in zip(shifts_of(step), parts_of(value)):
+            array = lax.dynamic_update_slice(array, part[:, None, None], (0, owner, lane(shift), 0, 0))
         return array
 
     def after(first, *arrays):
@@ -120,7 +118,15 @@
                     else:
                         new_held = land(new_held, step, parts)
                 step = order[stream][turn] if turn < turns else None
-                if phase < groups:
+                alone = None
+                if turn == 0 and phase == 1:
+                    (owner,) = after(payload, jnp.where(group == 0, groups - 1, 0))
+                    alone = own(owner, step)
+                    to_right = to_left = alone
+                elif turn == turns and phase == groups - 2:
+                    alone = jnp.where(group >= groups // 2, here_left, here_right)
+                    to_right = to_left = alone
+                elif phase < groups:
                     to_right, to_left = here_left, here_right
                     if turn < turns:
                         right_owner = jnp.minimum(groups - phase + group, groups - 1)
@@ -137,11 +143,18 @@
                     outgoing[step] = new_momentum
                     if step == 0:
                         new_held = land(new_held, *deliver(step)[1:])
-                    new_weights = write_weights(new_weights, group, step, update)
-                    to_right = to_left = update
+                    fresh = rows_of(start, group, step) - update
+                    new_weights = write_weights(new_weights, group, step, fresh)
+                    to_right = to_left = fresh
                 payload = (to_right, to_left)
-                from_left[stream] = lax.ppermute(to_right, "grp", rightward)
-                from_right[stream] = lax.ppermute(to_left, "grp", leftward)
+                if alone is None:
+                    from_left[stream] = lax.ppermute(to_right, "grp", rightward)
+                    from_right[stream] = lax.ppermute(to_left, "grp", leftward)
+                else:
+                    outer = [(0, 1), (groups - 1, groups - 2)]
+                    ends = [(groups - 2, groups - 1), (1, 0)]
+                    came = lax.ppermute(alone, "grp", outer if turn == 0 else ends)
+                    from_left[stream] = from_right[stream] = came
                 slot = in_turn // 2
                 if in_turn % 2 == 0 and slot < STREAMS and turn < turns and order[slot][turn] != 0:
                     transit.append((tick + 2,) + fetch(order[slot][turn]))
@@ -154,13 +167,13 @@
                 arrived_right[stream].append(from_right[stream])
                 if len(arrived_left[stream]) == groups - 1 and turn > 0:
                     for hop in range(groups - 1):
-                        update = jnp.where(
+                        fresh = jnp.where(
                             group > hop,
                             arrived_left[stream][hop],
                             arrived_right[stream][groups - 2 - hop],
                         )
                         owner = lax.rem(group + groups - 1 - hop, groups)
-                        new_weights = write_weights(new_weights, owner, order[stream][turn - 1], update)
+                        new_weights = write_weights(new_weights, owner, order[stream][turn - 1], fresh)
     for _, _, step, parts in transit:
         new_held = land(new_held, step, parts)
     return (new_weights.reshape(start_weights.shape), new_held.reshape(momentum.shape))

time: 733 us -> 720 us (0.982)
  other arithmetic: 188 us -> 162 us
  starting transfers between devices: 198 us -> 223 us
  waiting for transfers between devices: 319 us -> 304 us
    ppermute x36 -> x32, waiting for transfers between devices: 226 us -> 40 us  [body(): from_right[stream] = lax.ppermute(to_left, 'grp', leftward)]
    ppermute x36 -> x32, waiting for transfers between devices: 89.1 us -> 210 us  [body(): from_left[stream] = lax.ppermute(to_right, 'grp', rightward)]
    ppermute x0 -> x4, waiting for transfers between devices: none -> 50.8 us  [body(): came = lax.ppermute(alone, 'grp', outer if turn == 0 else ends)]
    ppermute x36 -> x32, starting transfers between devices: 135 us -> 158 us  [body(): from_left[stream] = lax.ppermute(to_right, 'grp', rightward)]
    dynamic_update_slice x32, other arithmetic: 76.1 us -> 55.8 us  [write_weights(): lax.dynamic_update_slice(array, part[:, None, None], (0, owner, lane(shif...]
    ppermute x0 -> x4, starting transfers between devices: none -> 9.12 us  [body(): came = lax.ppermute(alone, 'grp', outer if turn == 0 else ends)]
    select_n x18 -> x16, other arithmetic: 61.1 us -> 52.7 us  [body(): jnp.where(groups - 1 - group < phase, to_left + own(left_owner, step), to...]
    ppermute x36 -> x32, starting transfers between devices: 46.7 us -> 41.7 us  [body(): from_right[stream] = lax.ppermute(to_left, 'grp', leftward)]
  transfers between devices with their start and end apart: 86 -> 82, of which waited for: 56 -> 43; matrix products, arithmetic and copies ran while one was open for 28% -> 25% of each run, Pallas kernels for 0% -> 0%
where the time goes in v8:
time: 720 us; the launch traced here: 715 us
  waiting for transfers between devices  304 us (42%)
  starting transfers between devices  223 us (31%)
  other arithmetic  162 us (22%)
  local copies, waits for them, and re-layouts  25.5 us (4%)
    ppermute x32, waiting for transfers between devices, body(): from_left[stream] = lax.ppermute(to_right, 'grp', rightward)  210 us
    ppermute x32, starting transfers between devices, body(): from_left[stream] = lax.ppermute(to_right, 'grp', rightward)  158 us
    dynamic_update_slice x32, other arithmetic, write_weights(): lax.dynamic_update_slice(array, part[:, None, None], (0, owner, lane(shif...  55.8 us
    select_n x16, other arithmetic, body(): jnp.where(groups - 1 - group < phase, to_left + own(left_owner, step), to...  52.7 us
    ppermute x4, waiting for transfers between devices, body(): came = lax.ppermute(alone, 'grp', outer if turn == 0 else ends)  50.8 us
    ppermute x32, starting transfers between devices, body(): from_right[stream] = lax.ppermute(to_left, 'grp', leftward)  41.7 us
    ppermute x32, waiting for transfers between devices, body(): from_right[stream] = lax.ppermute(to_left, 'grp', leftward)  40 us
    add x8, other arithmetic, body(): new_momentum = MOMENTUM_COEF * moved[step] + mean_diff  22.7 us
  transfers between devices with their start and end apart: 82, of which 43 were waited for; matrix products, arithmetic and copies ran while one was open for 25% of the time, Pallas kernels for 0%

profile of v8, /device:TPU:0, one launch (start us, length us, event | category | flops | bytes accessed | tf_op | source)
XLA Modules:
  0.0 715.4 jit_solution(13208414236139341857)
XLA Ops:
  16.0 13.1 %collective-permute-done = f32[2,64,1792]{2,1,0:T(8,128)S(1)} collective-permute-done((f32[2,64,1792]{2,1,0:T(8,128)}, f32[2,64,1792]{2,1,0:T(8,128)S(1)}, u32[]{:S(2)}, u32[]{:S(2)}) %collective-permute-start) | collective-permute-done | bytes 917536 | tf_op jit(solution)/shard_map/ppermute | solution.py:156
  41.3 7.4 %collective-permute-done.2 = f32[2,64,1792]{2,1,0:T(8,128)S(1)} collective-permute-done((f32[2,64,1792]{2,1,0:T(8,128)}, f32[2,64,1792]{2,1,0:T(8,128)S(1)}, u32[]{:S(2)}, u32[]{:S(2)}) %collective-permute-start.2) | collective-permute-done | bytes 917536 | tf_op jit(solution)/shard_map/ppermute | solution.py:156
  57.9 10.5 %collective-permute-done.3 = f32[2,64,1792]{2,1,0:T(8,128)} collective-permute-done((f32[2,64,1792]{2,1,0:T(8,128)}, f32[2,64,1792]{2,1,0:T(8,128)}, u32[]{:S(2)}, u32[]{:S(2)}) %collective-permute-start.3) | collective-permute-done | bytes 917536 | tf_op jit(solution)/shard_map/ppermute | solution.py:151
  79.2 8.9 %collective-permute-done.6 = f32[2,64,1792]{2,1,0:T(8,128)S(1)} collective-permute-done((f32[2,64,1792]{2,1,0:T(8,128)}, f32[2,64,1792]{2,1,0:T(8,128)S(1)}, u32[]{:S(2)}, u32[]{:S(2)}) %collective-permute-start.6) | collective-permute-done | bytes 917536 | tf_op jit(solution)/shard_map/ppermute | solution.py:151
  96.3 11.4 %collective-permute-done.8 = f32[2,64,1792]{2,1,0:T(8,128)} collective-permute-done((f32[2,64,1792]{2,1,0:T(8,128)}, f32[2,64,1792]{2,1,0:T(8,128)}, u32[]{:S(2)}, u32[]{:S(2)}) %collective-permute-start.8) | collective-permute-done | bytes 917536 | tf_op jit(solution)/shard_map/ppermute | solution.py:151
  119.0 8.3 %collective-permute-done.10 = f32[2,64,1792]{2,1,0:T(8,128)S(1)} collective-permute-done((f32[2,64,1792]{2,1,0:T(8,128)S(1)}, f32[2,64,1792]{2,1,0:T(8,128)S(1)}, u32[]{:S(2)}, u32[]{:S(2)}) %collective-permute-start.10) | collective-permute-done | bytes 917536 | tf_op jit(solution)/shard_map/ppermute | solution.py:151
  139.2 7.7 %collective-permute-done.12 = f32[2,64,1792]{2,1,0:T(8,128)S(1)} collective-permute-done((f32[2,64,1792]{2,1,0:T(8,128)S(1)}, f32[2,64,1792]{2,1,0:T(8,128)S(1)}, u32[]{:S(2)}, u32[]{:S(2)}) %collective-permute-start.12) | collective-permute-done | bytes 917536 | tf_op jit(solution)/shard_map/ppermute | solution.py:151
  177.6 8.8 %collective-permute-done.16 = f32[2,64,1792]{2,1,0:T(8,128)} collective-permute-done((f32[2,64,1792]{2,1,0:T(8,128)}, f32[2,64,1792]{2,1,0:T(8,128)}, u32[]{:S(2)}, u32[]{:S(2)}) %collective-permute-start.16) | collective-permute-done | bytes 917536 | tf_op jit(solution)/shard_map/ppermute | solution.py:151
  191.8 5.9 collective-permute-start.20
  211.4 6.0 collective-permute-start.24
  234.4 6.8 collective-permute-done.23
  277.3 7.3 %collective-permute-done.29 = f32[2,64,1792]{2,1,0:T(8,128)S(1)} collective-permute-done((f32[2,64,1792]{2,1,0:T(8,128)S(1)}, f32[2,64,1792]{2,1,0:T(8,128)S(1)}, u32[]{:S(2)}, u32[]{:S(2)}) %collective-permute-start.29) | collective-permute-done | bytes 917536 | tf_op jit(solution)/shard_map/ppermute | solution.py:151
  296.8 7.5 %collective-permute-done.31 = f32[2,64,1792]{2,1,0:T(8,128)S(1)} collective-permute-done((f32[2,64,1792]{2,1,0:T(8,128)S(1)}, f32[2,64,1792]{2,1,0:T(8,128)S(1)}, u32[]{:S(2)}, u32[]{:S(2)}) %collective-permute-start.31) | collective-permute-done | bytes 917536 | tf_op jit(solution)/shard_map/ppermute | solution.py:151
  309.2 5.5 collective-permute-start.36
  334.9 8.8 %collective-permute-done.36 = f32[2,64,1792]{2,1,0:T(8,128)} collective-permute-done((f32[2,64,1792]{2,1,0:T(8,128)}, f32[2,64,1792]{2,1,0:T(8,128)}, u32[]{:S(2)}, u32[]{:S(2)}) %collective-permute-start.36) | collective-permute-done | bytes 917536 | tf_op jit(solution)/shard_map/ppermute | solution.py:151
  349.1 6.0 collective-permute-start.40
  355.0 8.3 %collective-permute-done.41 = f32[2,64,1792]{2,1,0:T(8,128)} collective-permute-done((f32[2,64,1792]{2,1,0:T(8,128)}, f32[2,64,1792]{2,1,0:T(8,128)}, u32[]{:S(2)}, u32[]{:S(2)}) %collective-permute-start.41) | collective-permute-done | bytes 917536 | tf_op jit(solution)/shard_map/ppermute | solution.py:151
  391.7 7.4 %collective-permute-done.43 = f32[2,64,1792]{2,1,0:T(8,128)S(1)} collective-permute-done((f32[2,64,1792]{2,1,0:T(8,128)S(1)}, f32[2,64,1792]{2,1,0:T(8,128)S(1)}, u32[]{:S(2)}, u32[]{:S(2)}) %collective-permute-start.43) | collective-permute-done | bytes 917536 | tf_op jit(solution)/shard_map/ppermute | solution.py:152
  434.8 7.1 collective-permute-done.49
  473.1 8.2 %collective-permute-done.54 = f32[2,64,1792]{2,1,0:T(8,128)} collective-permute-done((f32[2,64,1792]{2,1,0:T(8,128)}, f32[2,64,1792]{2,1,0:T(8,128)}, u32[]{:S(2)}, u32[]{:S(2)}) %collective-permute-start.54) | collective-permute-done | bytes 917536 | tf_op jit(solution)/shard_map/ppermute | solution.py:151
  494.8 6.2 collective-permute-done.56
  512.1 8.5 %collective-permute-done.61 = f32[2,64,1792]{2,1,0:T(8,128)S(1)} collective-permute-done((f32[2,64,1792]{2,1,0:T(8,128)S(1)}, f32[2,64,1792]{2,1,0:T(8,128)S(1)}, u32[]{:S(2)}, u32[]{:S(2)}) %collective-permute-start.61) | collective-permute-done | bytes 917536 | tf_op jit(solution)/shard_map/ppermute | solution.py:151
  531.5 7.9 %collective-permute-done.59 = f32[2,64,1792]{2,1,0:T(8,128)S(1)} collective-permute-done((f32[2,64,1792]{2,1,0:T(8,128)S(1)}, f32[2,64,1792]{2,1,0:T(8,128)S(1)}, u32[]{:S(2)}, u32[]{:S(2)}) %collective-permute-start.59) | collective-permute-done | bytes 917536 | tf_op jit(solution)/shard_map/ppermute | solution.py:152
  548.3 10.7 %collective-permute-done.63 = f32[2,64,1792]{2,1,0:T(8,128)S(1)} collective-permute-done((f32[2,64,1792]{2,1,0:T(8,128)S(1)}, f32[2,64,1792]{2,1,0:T(8,128)S(1)}, u32[]{:S(2)}, u32[]{:S(2)}) %collective-permute-start.63) | collective-permute-done | bytes 917536 | tf_op jit(solution)/shard_map/ppermute | solution.py:152
  563.6 5.4 collective-permute-start.68
  591.9 7.4 %collective-permute-done.68 = f32[2,64,1792]{2,1,0:T(8,128)} collective-permute-done((f32[2,64,1792]{2,1,0:T(8,128)}, f32[2,64,1792]{2,1,0:T(8,128)}, u32[]{:S(2)}, u32[]{:S(2)}) %collective-permute-start.68) | collective-permute-done | bytes 917536 | tf_op jit(solution)/shard_map/ppermute | solution.py:151
  611.8 7.0 collective-permute-done.70
  627.1 11.4 %collective-permute-done.73 = f32[2,64,1792]{2,1,0:T(8,128)S(1)} collective-permute-done((f32[2,64,1792]{2,1,0:T(8,128)S(1)}, f32[2,64,1792]{2,1,0:T(8,128)S(1)}, u32[]{:S(2)}, u32[]{:S(2)}) %collective-permute-start.73) | collective-permute-done | bytes 917536 | tf_op jit(solution)/shard_map/ppermute | solution.py:151
  645.3 12.9 %collective-permute-done.75 = f32[2,64,1792]{2,1,0:T(8,128)S(1)} collective-permute-done((f32[2,64,1792]{2,1,0:T(8,128)S(1)}, f32[2,64,1792]{2,1,0:T(8,128)S(1)}, u32[]{:S(2)}, u32[]{:S(2)}) %collective-permute-start.75) | collective-permute-done | bytes 917536 | tf_op jit(solution)/shard_map/ppermute | solution.py:151
  659.6 17.1 %collective-permute-done.79 = f32[2,64,1792]{2,1,0:T(8,128)S(1)} collective-permute-done((f32[2,64,1792]{2,1,0:T(8,128)S(1)}, f32[2,64,1792]{2,1,0:T(8,128)S(1)}, u32[]{:S(2)}, u32[]{:S(2)}) %collective-permute-start.79) | collective-permute-done | bytes 917536 | tf_op jit(solution)/shard_map/ppermute | solution.py:151
  679.1 13.6 %collective-permute-done.78 = f32[2,64,1792]{2,1,0:T(8,128)S(1)} collective-permute-done((f32[2,64,1792]{2,1,0:T(8,128)S(1)}, f32[2,64,1792]{2,1,0:T(8,128)S(1)}, u32[]{:S(2)}, u32[]{:S(2)}) %collective-permute-start.78) | collective-permute-done | bytes 917536 | tf_op jit(solution)/shard_map/ppermute | solution.py:156
  695.8 16.6 %collective-permute-done.81 = f32[2,64,1792]{2,1,0:T(8,128)S(1)} collective-permute-done((f32[2,64,1792]{2,1,0:T(8,128)S(1)}, f32[2,64,1792]{2,1,0:T(8,128)S(1)}, u32[]{:S(2)}, u32[]{:S(2)}) %collective-permute-start.81) | collective-permute-done | bytes 917536 | tf_op jit(solution)/shard_map/ppermute | solution.py:156
  (249 shorter events, 428.1 us)
Async XLA Ops:
  14.4 34.4 %collective-permute-start.2 = (f32[2,64,1792]{2,1,0:T(8,128)}, f32[2,64,1792]{2,1,0:T(8,128)S(1)}, u32[]{:S(2)}, u32[]{:S(2)}) collective-permute-start(f32[2,64,1792]{2,1,0:T(8,128)} %fusion.45), channel_id=1, source_target_pairs={{0,8},{24,16},{1,9},{25,17},{2,10},{26,18},{3,11},{27,19},{4,12},{... | collective-permute-start | bytes 2752520 | tf_op jit(solution)/shard_map/ppermute | solution.py:156
  32.6 35.8 %collective-permute-start.3 = (f32[2,64,1792]{2,1,0:T(8,128)}, f32[2,64,1792]{2,1,0:T(8,128)}, u32[]{:S(2)}, u32[]{:S(2)}) collective-permute-start(f32[2,64,1792]{2,1,0:T(8,128)} %get-tuple-element.279), channel_id=1, source_target_pairs={{0,8},{8,16},{16,24},{1,9},{9,17},{17,25},{2,10},{10,18},{18,26},{... | collective-permute-start | bytes 2752520 | tf_op jit(solution)/shard_map/ppermute | solution.py:151
  52.3 35.8 %collective-permute-start.6 = (f32[2,64,1792]{2,1,0:T(8,128)}, f32[2,64,1792]{2,1,0:T(8,128)S(1)}, u32[]{:S(2)}, u32[]{:S(2)}) collective-permute-start(f32[2,64,1792]{2,1,0:T(8,128)} %get-tuple-element.277), channel_id=1, source_target_pairs={{0,8},{8,16},{16,24},{1,9},{9,17},{17,25},{2,10},{10,18},{18,26},{... | collective-permute-start | bytes 2752520 | tf_op jit(solution)/shard_map/ppermute | solution.py:151
  72.5 35.2 %collective-permute-start.8 = (f32[2,64,1792]{2,1,0:T(8,128)}, f32[2,64,1792]{2,1,0:T(8,128)}, u32[]{:S(2)}, u32[]{:S(2)}) collective-permute-start(f32[2,64,1792]{2,1,0:T(8,128)} %get-tuple-element.275), channel_id=1, source_target_pairs={{0,8},{8,16},{16,24},{1,9},{9,17},{17,25},{2,10},{10,18},{18,26},{... | collective-permute-start | bytes 2752520 | tf_op jit(solution)/shard_map/ppermute | solution.py:151
  90.7 36.6 %collective-permute-start.10 = (f32[2,64,1792]{2,1,0:T(8,128)S(1)}, f32[2,64,1792]{2,1,0:T(8,128)S(1)}, u32[]{:S(2)}, u32[]{:S(2)}) collective-permute-start(f32[2,64,1792]{2,1,0:T(8,128)S(1)} %get-tuple-element.273), channel_id=1, source_target_pairs={{0,8},{8,16},{16,24},{1,9},{9,17},{17,25},{2,10},{10,18},{18,26},{... | collective-permute-start | bytes 2752520 | tf_op jit(solution)/shard_map/ppermute | solution.py:151
  113.2 33.7 %collective-permute-start.12 = (f32[2,64,1792]{2,1,0:T(8,128)S(1)}, f32[2,64,1792]{2,1,0:T(8,128)S(1)}, u32[]{:S(2)}, u32[]{:S(2)}) collective-permute-start(f32[2,64,1792]{2,1,0:T(8,128)S(1)} %get-tuple-element.235), channel_id=1, source_target_pairs={{0,8},{8,16},{16,24},{1,9},{9,17},{17,25},{2,10},{10,18},{18,26},{... | collective-permute-start | bytes 2752520 | tf_op jit(solution)/shard_map/ppermute | solution.py:151
  132.6 34.1 %collective-permute-start.14 = (f32[2,64,1792]{2,1,0:T(8,128)}, f32[2,64,1792]{2,1,0:T(8,128)}, u32[]{:S(2)}, u32[]{:S(2)}) collective-permute-start(f32[2,64,1792]{2,1,0:T(8,128)} %get-tuple-element.233), channel_id=1, source_target_pairs={{0,8},{8,16},{16,24},{1,9},{9,17},{17,25},{2,10},{10,18},{18,26},{... | collective-permute-start | bytes 2752520 | tf_op jit(solution)/shard_map/ppermute | solution.py:151
  151.5 34.9 %collective-permute-start.16 = (f32[2,64,1792]{2,1,0:T(8,128)}, f32[2,64,1792]{2,1,0:T(8,128)}, u32[]{:S(2)}, u32[]{:S(2)}) collective-permute-start(f32[2,64,1792]{2,1,0:T(8,128)} %get-tuple-element.271), channel_id=1, source_target_pairs={{0,8},{8,16},{16,24},{1,9},{9,17},{17,25},{2,10},{10,18},{18,26},{... | collective-permute-start | bytes 2752520 | tf_op jit(solution)/shard_map/ppermute | solution.py:151
  170.9 35.1 %collective-permute-start.21 = (f32[2,64,1792]{2,1,0:T(8,128)}, f32[2,64,1792]{2,1,0:T(8,128)}, u32[]{:S(2)}, u32[]{:S(2)}) collective-permute-start(f32[2,64,1792]{2,1,0:T(8,128)} %get-tuple-element.269), channel_id=1, source_target_pairs={{0,8},{8,16},{16,24},{1,9},{9,17},{17,25},{2,10},{10,18},{18,26},{... | collective-permute-start | bytes 2752520 | tf_op jit(solution)/shard_map/ppermute | solution.py:151
  191.8 33.9 %collective-permute-start.20 = (f32[2,64,1792]{2,1,0:T(8,128)}, f32[2,64,1792]{2,1,0:T(8,128)}, u32[]{:S(2)}, u32[]{:S(2)}) collective-permute-start(f32[2,64,1792]{2,1,0:T(8,128)} %get-tuple-element.266), channel_id=1, source_target_pairs={{0,8},{8,16},{16,24},{1,9},{9,17},{17,25},{2,10},{10,18},{18,26},{... | collective-permute-start | bytes 2752520 | tf_op jit(solution)/shard_map/ppermute | solution.py:151
  211.4 34.0 %collective-permute-start.24 = (f32[2,64,1792]{2,1,0:T(8,128)}, f32[2,64,1792]{2,1,0:T(8,128)}, u32[]{:S(2)}, u32[]{:S(2)}) collective-permute-start(f32[2,64,1792]{2,1,0:T(8,128)} %get-tuple-element.264), channel_id=1, source_target_pairs={{0,8},{8,16},{16,24},{1,9},{9,17},{17,25},{2,10},{10,18},{18,26},{... | collective-permute-start | bytes 2752520 | tf_op jit(solution)/shard_map/ppermute | solution.py:151
  228.6 37.4 %collective-permute-start.26 = (f32[2,64,1792]{2,1,0:T(8,128)S(1)}, f32[2,64,1792]{2,1,0:T(8,128)S(1)}, u32[]{:S(2)}, u32[]{:S(2)}) collective-permute-start(f32[2,64,1792]{2,1,0:T(8,128)S(1)} %get-tuple-element.263), channel_id=1, source_target_pairs={{0,8},{8,16},{16,24},{1,9},{9,17},{17,25},{2,10},{10,18},{18,26},{... | collective-permute-start | bytes 2752520 | tf_op jit(solution)/shard_map/ppermute | solution.py:151
  248.3 36.3 %collective-permute-start.29 = (f32[2,64,1792]{2,1,0:T(8,128)S(1)}, f32[2,64,1792]{2,1,0:T(8,128)S(1)}, u32[]{:S(2)}, u32[]{:S(2)}) collective-permute-start(f32[2,64,1792]{2,1,0:T(8,128)S(1)} %get-tuple-element.261), channel_id=1, source_target_pairs={{0,8},{8,16},{16,24},{1,9},{9,17},{17,25},{2,10},{10,18},{18,26},{... | collective-permute-start | bytes 2752520 | tf_op jit(solution)/shard_map/ppermute | solution.py:151
  289.9 34.1 %collective-permute-start.34 = (f32[2,64,1792]{2,1,0:T(8,128)}, f32[2,64,1792]{2,1,0:T(8,128)}, u32[]{:S(2)}, u32[]{:S(2)}) collective-permute-start(f32[2,64,1792]{2,1,0:T(8,128)} %get-tuple-element.227), channel_id=1, source_target_pairs={{0,8},{8,16},{16,24},{1,9},{9,17},{17,25},{2,10},{10,18},{18,26},{... | collective-permute-start | bytes 2752520 | tf_op jit(solution)/shard_map/ppermute | solution.py:151
  309.2 34.5 %collective-permute-start.36 = (f32[2,64,1792]{2,1,0:T(8,128)}, f32[2,64,1792]{2,1,0:T(8,128)}, u32[]{:S(2)}, u32[]{:S(2)}) collective-permute-start(f32[2,64,1792]{2,1,0:T(8,128)} %get-tuple-element.259), channel_id=1, source_target_pairs={{0,8},{8,16},{16,24},{1,9},{9,17},{17,25},{2,10},{10,18},{18,26},{... | collective-permute-start | bytes 2752520 | tf_op jit(solution)/shard_map/ppermute | solution.py:151
  328.2 35.1 %collective-permute-start.41 = (f32[2,64,1792]{2,1,0:T(8,128)}, f32[2,64,1792]{2,1,0:T(8,128)}, u32[]{:S(2)}, u32[]{:S(2)}) collective-permute-start(f32[2,64,1792]{2,1,0:T(8,128)} %get-tuple-element.257), channel_id=1, source_target_pairs={{0,8},{8,16},{16,24},{1,9},{9,17},{17,25},{2,10},{10,18},{18,26},{... | collective-permute-start | bytes 2752520 | tf_op jit(solution)/shard_map/ppermute | solution.py:151
  349.1 33.9 %collective-permute-start.40 = (f32[2,64,1792]{2,1,0:T(8,128)}, f32[2,64,1792]{2,1,0:T(8,128)}, u32[]{:S(2)}, u32[]{:S(2)}) collective-permute-start(f32[2,64,1792]{2,1,0:T(8,128)} %get-tuple-element.254), channel_id=1, source_target_pairs={{0,8},{8,16},{16,24},{1,9},{9,17},{17,25},{2,10},{10,18},{18,26},{... | collective-permute-start | bytes 2752520 | tf_op jit(solution)/shard_map/ppermute | solution.py:151
  385.9 37.2 %collective-permute-start.46 = (f32[2,64,1792]{2,1,0:T(8,128)S(1)}, f32[2,64,1792]{2,1,0:T(8,128)S(1)}, u32[]{:S(2)}, u32[]{:S(2)}) collective-permute-start(f32[2,64,1792]{2,1,0:T(8,128)S(1)} %get-tuple-element.251), channel_id=1, source_target_pairs={{0,8},{8,16},{16,24},{1,9},{9,17},{17,25},{2,10},{10,18},{18,26},{... | collective-permute-start | bytes 2752520 | tf_op jit(solution)/shard_map/ppermute | solution.py:151
  406.5 35.4 %collective-permute-start.49 = (f32[2,64,1792]{2,1,0:T(8,128)S(1)}, f32[2,64,1792]{2,1,0:T(8,128)S(1)}, u32[]{:S(2)}, u32[]{:S(2)}) collective-permute-start(f32[2,64,1792]{2,1,0:T(8,128)S(1)} %get-tuple-element.249), channel_id=1, source_target_pairs={{0,8},{8,16},{16,24},{1,9},{9,17},{17,25},{2,10},{10,18},{18,26},{... | collective-permute-start | bytes 2752520 | tf_op jit(solution)/shard_map/ppermute | solution.py:151
  466.5 34.5 %collective-permute-start.56 = (f32[2,64,1792]{2,1,0:T(8,128)}, f32[2,64,1792]{2,1,0:T(8,128)}, u32[]{:S(2)}, u32[]{:S(2)}) collective-permute-start(f32[2,64,1792]{2,1,0:T(8,128)} %get-tuple-element.247), channel_id=1, source_target_pairs={{0,8},{8,16},{16,24},{1,9},{9,17},{17,25},{2,10},{10,18},{18,26},{... | collective-permute-start | bytes 2752520 | tf_op jit(solution)/shard_map/ppermute | solution.py:151
  522.9 36.1 %collective-permute-start.63 = (f32[2,64,1792]{2,1,0:T(8,128)S(1)}, f32[2,64,1792]{2,1,0:T(8,128)S(1)}, u32[]{:S(2)}, u32[]{:S(2)}) collective-permute-start(f32[2,64,1792]{2,1,0:T(8,128)S(1)} %get-tuple-element.241), channel_id=1, source_target_pairs={{8,0},{16,8},{24,16},{9,1},{17,9},{25,17},{10,2},{18,10},{26,18},{... | collective-permute-start | bytes 2752520 | tf_op jit(solution)/shard_map/ppermute | solution.py:152
  524.2 35.6 %collective-permute-start.64 = (f32[2,64,1792]{2,1,0:T(8,128)S(1)}, f32[2,64,1792]{2,1,0:T(8,128)S(1)}, u32[]{:S(2)}, u32[]{:S(2)}) collective-permute-start(f32[2,64,1792]{2,1,0:T(8,128)S(1)} %get-tuple-element.240), channel_id=1, source_target_pairs={{0,8},{8,16},{16,24},{1,9},{9,17},{17,25},{2,10},{10,18},{18,26},{... | collective-permute-start | bytes 2752520 | tf_op jit(solution)/shard_map/ppermute | solution.py:151
  542.6 36.9 %collective-permute-start.65 = (f32[2,64,1792]{2,1,0:T(8,128)S(1)}, f32[2,64,1792]{2,1,0:T(8,128)S(1)}, u32[]{:S(2)}, u32[]{:S(2)}) collective-permute-start(f32[2,64,1792]{2,1,0:T(8,128)S(1)} %get-tuple-element.239), channel_id=1, source_target_pairs={{0,8},{8,16},{16,24},{1,9},{9,17},{17,25},{2,10},{10,18},{18,26},{... | collective-permute-start | bytes 2752520 | tf_op jit(solution)/shard_map/ppermute | solution.py:151
  563.6 35.7 %collective-permute-start.68 = (f32[2,64,1792]{2,1,0:T(8,128)}, f32[2,64,1792]{2,1,0:T(8,128)}, u32[]{:S(2)}, u32[]{:S(2)}) collective-permute-start(f32[2,64,1792]{2,1,0:T(8,128)} %get-tuple-element.237), channel_id=1, source_target_pairs={{0,8},{8,16},{16,24},{1,9},{9,17},{17,25},{2,10},{10,18},{18,26},{... | collective-permute-start | bytes 2752520 | tf_op jit(solution)/shard_map/ppermute | solution.py:151
  584.9 34.0 %collective-permute-start.70 = (f32[2,64,1792]{2,1,0:T(8,128)S(1)}, f32[2,64,1792]{2,1,0:T(8,128)S(1)}, u32[]{:S(2)}, u32[]{:S(2)}) collective-permute-start(f32[2,64,1792]{2,1,0:T(8,128)S(1)} %get-tuple-element.213), channel_id=1, source_target_pairs={{0,8},{8,16},{16,24},{1,9},{9,17},{17,25},{2,10},{10,18},{18,26},{... | collective-permute-start | bytes 2752520 | tf_op jit(solution)/shard_map/ppermute | solution.py:151
  603.9 34.6 %collective-permute-start.73 = (f32[2,64,1792]{2,1,0:T(8,128)S(1)}, f32[2,64,1792]{2,1,0:T(8,128)S(1)}, u32[]{:S(2)}, u32[]{:S(2)}) collective-permute-start(f32[2,64,1792]{2,1,0:T(8,128)S(1)} %get-tuple-element.211), channel_id=1, source_target_pairs={{0,8},{8,16},{16,24},{1,9},{9,17},{17,25},{2,10},{10,18},{18,26},{... | collective-permute-start | bytes 2752520 | tf_op jit(solution)/shard_map/ppermute | solution.py:151
  618.9 39.3 %collective-permute-start.75 = (f32[2,64,1792]{2,1,0:T(8,128)S(1)}, f32[2,64,1792]{2,1,0:T(8,128)S(1)}, u32[]{:S(2)}, u32[]{:S(2)}) collective-permute-start(f32[2,64,1792]{2,1,0:T(8,128)S(1)} %collective-permute-done.70), channel_id=1, source_target_pairs={{0,8},{8,16},{16,24},{1,9},{9,17},{17,25},{2,10},{10,18},{18,26},{... | collective-permute-start | bytes 2752520 | tf_op jit(solution)/shard_map/ppermute | solution.py:151
  623.3 34.9 %collective-permute-start.76 = (f32[2,64,1792]{2,1,0:T(8,128)S(1)}, f32[2,64,1792]{2,1,0:T(8,128)S(1)}, u32[]{:S(2)}, u32[]{:S(2)}) collective-permute-start(f32[2,64,1792]{2,1,0:T(8,128)S(1)} %collective-permute-done.71), channel_id=1, source_target_pairs={{8,0},{16,8},{24,16},{9,1},{17,9},{25,17},{10,2},{18,10},{26,18},{... | collective-permute-start | bytes 2752520 | tf_op jit(solution)/shard_map/ppermute | solution.py:152
  638.5 38.2 %collective-permute-start.79 = (f32[2,64,1792]{2,1,0:T(8,128)S(1)}, f32[2,64,1792]{2,1,0:T(8,128)S(1)}, u32[]{:S(2)}, u32[]{:S(2)}) collective-permute-start(f32[2,64,1792]{2,1,0:T(8,128)S(1)} %collective-permute-done.73), channel_id=1, source_target_pairs={{0,8},{8,16},{16,24},{1,9},{9,17},{17,25},{2,10},{10,18},{18,26},{... | collective-permute-start | bytes 2752520 | tf_op jit(solution)/shard_map/ppermute | solution.py:151
  643.0 33.7 %collective-permute-start.80 = (f32[2,64,1792]{2,1,0:T(8,128)S(1)}, f32[2,64,1792]{2,1,0:T(8,128)S(1)}, u32[]{:S(2)}, u32[]{:S(2)}) collective-permute-start(f32[2,64,1792]{2,1,0:T(8,128)S(1)} %collective-permute-done.74), channel_id=1, source_target_pairs={{8,0},{16,8},{24,16},{9,1},{17,9},{25,17},{10,2},{18,10},{26,18},{... | collective-permute-start | bytes 2752520 | tf_op jit(solution)/shard_map/ppermute | solution.py:152
  658.3 34.4 %collective-permute-start.78 = (f32[2,64,1792]{2,1,0:T(8,128)S(1)}, f32[2,64,1792]{2,1,0:T(8,128)S(1)}, u32[]{:S(2)}, u32[]{:S(2)}) collective-permute-start(f32[2,64,1792]{2,1,0:T(8,128)S(1)} %broadcast_select_fusion.1), channel_id=1, source_target_pairs={{16,24},{8,0},{17,25},{9,1},{18,26},{10,2},{19,27},{11,3},{20,28},... | collective-permute-start | bytes 2752520 | tf_op jit(solution)/shard_map/ppermute | solution.py:156
  676.8 35.6 %collective-permute-start.81 = (f32[2,64,1792]{2,1,0:T(8,128)S(1)}, f32[2,64,1792]{2,1,0:T(8,128)S(1)}, u32[]{:S(2)}, u32[]{:S(2)}) collective-permute-start(f32[2,64,1792]{2,1,0:T(8,128)S(1)} %broadcast_select_fusion), channel_id=1, source_target_pairs={{16,24},{8,0},{17,25},{9,1},{18,26},{10,2},{19,27},{11,3},{20,28},... | collective-permute-start | bytes 2752520 | tf_op jit(solution)/shard_map/ppermute | solution.py:156
  (63 other events, 1923.0 us)
